TPU v7x, 128 devices: a whole 4x4x4 slice. The times are simulated.
128 devices in a mesh: dp: 8 (over x, y_lo), section: 4 (over z), tensor: 4 (over y_hi, core).
Axes of the slice: x: 4, y: 4 (y_hi: 2, y_lo: 2; y = y_hi * 2 + y_lo), z: 4, core: 2. Of those that a mesh axis runs over, the one named last changes fastest.
Arguments:
- hidden_in: bfloat16 [16, 1024, 768], P('dp', 'tensor'), may hold values from -6 to 6
- segments: int32 [16, 1024], P('dp'), may hold values from 0 to 1023, as said below
- timestep: int32 [16], P('dp'), may hold values from 0 to 999
- w_qkv: bfloat16 [2, 768, 2304], P(None, None, 'tensor'), may hold values from -0.21875 to 0.21875
- w_out: bfloat16 [2, 768, 768], P(None, 'tensor'), may hold values from -1.75 to 1.75
- w_up: bfloat16 [2, 768, 3072], P(None, None, 'tensor'), may hold values from -0.21875 to 0.21875
- w_down: bfloat16 [2, 3072, 768], P(None, 'tensor'), may hold values from -0.109375 to 0.109375
- w_mod: bfloat16 [2, 128, 4608], replicated, may hold values from -0.375 to 0.375
- b_mod: bfloat16 [2, 4608], replicated, may hold values from -3 to 3
- cotangent: bfloat16 [4, 16, 1024, 768], P('section', 'dp', 'tensor'), may hold values from -6 to 6
Outputs:
- layer_outputs: bfloat16 [4, 16, 1024, 768], P('section', 'dp', 'tensor')
- section_grads: float32 [4, 16, 1024, 768], P('section', 'dp', 'tensor')
- grad_qkv: float32 [2, 768, 2304], P(None, None, 'tensor')
- grad_out: float32 [2, 768, 768], P(None, 'tensor')
- grad_up: float32 [2, 768, 3072], P(None, None, 'tensor')
- grad_down: float32 [2, 3072, 768], P(None, 'tensor')
- grad_mod: float32 [2, 128, 4608], replicated
- grad_bias: float32 [2, 4608], replicated
Inputs may be any that keep to these rules, and one draw needn't show every extreme that they name: `segments`: segment numbers of a row start at 0 and never fall; equal numbers mark one document; the last document of every row has the number 1024 - 1.
All inputs are finite; a program needn't handle non-finite values.
Results may differ from a plain program's by a relative error of at most 0.025.
Values may be sent and summed in bfloat16 or wider, within the bound.
A program may use at most 192 MiB of HBM per device.

v0:
```python
import math

import jax
import jax.numpy as jnp
from jax import lax
from jax.sharding import PartitionSpec as P

HEAD_SIZE = 64


highest = lax.Precision.HIGHEST
norm_epsilon = 1e-06


def from_behind(x, axis, by):
    size = lax.axis_size(axis)
    pairs = [(i, i + by) for i in range(size) if 0 <= i + by < size]
    return lax.ppermute(x, axis, pairs)


def time_features(step_values, feature_count):
    half_count = feature_count // 2
    frequency = jnp.exp(-math.log(10000.0) * jnp.arange(half_count, dtype=jnp.float32) / half_count)
    angles = step_values.astype(jnp.float32)[:, None] * frequency[None, :]
    return jnp.concatenate([jnp.cos(angles), jnp.sin(angles)], axis=1)


def rotary_tables(length, table_size):
    half_size = table_size // 2
    frequency = jnp.exp(-math.log(10000.0) * jnp.arange(half_size, dtype=jnp.float32) / half_size)
    angles = jnp.arange(length, dtype=jnp.float32)[:, None] * frequency[None, :]
    return (jnp.cos(angles), jnp.sin(angles))


def rotate(tensor, cosine, sine_table):
    half_size = tensor.shape[-1] // 2
    first_half = tensor[..., :half_size]
    second_half = tensor[..., half_size:]
    cos_part = cosine[:, None, :]
    sin_part = sine_table[:, None, :]
    return jnp.concatenate(
        [
            first_half * cos_part - second_half * sin_part,
            second_half * cos_part + first_half * sin_part,
        ],
        axis=-1,
    )


def normalize(values):
    centred = values - jnp.mean(values, axis=-1, keepdims=True)
    inverse = lax.rsqrt(jnp.mean(centred * centred, axis=-1, keepdims=True) + norm_epsilon)
    return (centred * inverse, inverse)


def norm_back(gradient, normed, inverse):
    return inverse * (
        gradient
        - jnp.mean(gradient, axis=-1, keepdims=True)
        - normed * jnp.mean(gradient * normed, axis=-1, keepdims=True)
    )


def gelu_tanh(values):
    return jax.nn.gelu(values, approximate=True)


def take_row(array, position):
    return lax.dynamic_index_in_dim(array, position, 0, keepdims=False)


def put_row(buffer, piece_new, position, usable):
    merged = jnp.where(usable, piece_new, take_row(buffer, position))
    return lax.dynamic_update_index_in_dim(buffer, merged, position, 0)


def attend(query_rows, key_rows, values, segment_ids):
    seq_len, head_count, head_dim = query_rows.shape
    block_rows = min(512, seq_len)
    block_count = seq_len // block_rows
    scale_value = HEAD_SIZE ** (-0.5)

    def one_block(operands):
        query_block, segment_block = operands
        scores = (
            jnp.einsum("qhd,khd->hqk", query_block, key_rows, preferred_element_type=jnp.float32)
            * scale_value
        )
        same_doc = segment_block[:, None] == segment_ids[None, :]
        scores = jnp.where(same_doc[None, :, :], scores, -1e30)
        largest = jnp.max(scores, axis=-1, keepdims=True)
        shifted = jnp.exp(scores - largest)
        totals = jnp.sum(shifted, axis=-1, keepdims=True)
        weights = (shifted / totals).astype(jnp.bfloat16)
        mixed_heads = jnp.einsum(
            "hqk,khd->qhd", weights, values, preferred_element_type=jnp.float32
        )
        return (mixed_heads.astype(jnp.bfloat16), (largest + jnp.log(totals))[:, :, 0])

    mixed_heads, log_totals = lax.map(
        one_block,
        (
            query_rows.reshape(block_count, block_rows, head_count, head_dim),
            segment_ids.reshape(block_count, block_rows),
        ),
    )
    return (mixed_heads.reshape(seq_len, head_count * head_dim), log_totals)


def attend_back(d_mixed, query_rows, key_rows, values, log_totals, segment_ids):
    seq_len, head_count, head_dim = query_rows.shape
    block_rows = min(512, seq_len)
    block_count = seq_len // block_rows
    scale_value = HEAD_SIZE ** (-0.5)

    def one_block(carried, operands):
        key_grad, value_grad = carried
        query_block, grad_block, log_block, segment_block = operands
        scores = (
            jnp.einsum("qhd,khd->hqk", query_block, key_rows, preferred_element_type=jnp.float32)
            * scale_value
        )
        same_doc = segment_block[:, None] == segment_ids[None, :]
        scores = jnp.where(same_doc[None, :, :], scores, -1e30)
        probabilities = jnp.exp(scores - log_block[:, :, None])
        d_probs = jnp.einsum("qhd,khd->hqk", grad_block, values, preferred_element_type=jnp.float32)
        centre = jnp.sum(d_probs * probabilities, axis=-1, keepdims=True)
        d_scores = (probabilities * (d_probs - centre)).astype(jnp.bfloat16)
        value_grad = value_grad + jnp.einsum(
            "hqk,qhd->khd",
            probabilities.astype(jnp.bfloat16),
            grad_block,
            preferred_element_type=jnp.float32,
        )
        key_grad = (
            key_grad
            + jnp.einsum("hqk,qhd->khd", d_scores, query_block, preferred_element_type=jnp.float32)
            * scale_value
        )
        query_grad = (
            jnp.einsum("hqk,khd->qhd", d_scores, key_rows, preferred_element_type=jnp.float32)
            * scale_value
        )
        return ((key_grad, value_grad), query_grad)

    zero_grads = jnp.zeros((seq_len, head_count, head_dim), jnp.float32)
    (key_grad, value_grad), query_grad = lax.scan(
        one_block,
        (zero_grads, zero_grads),
        (
            query_rows.reshape(block_count, block_rows, head_count, head_dim),
            d_mixed.reshape(block_count, block_rows, head_count, head_dim),
            log_totals,
            segment_ids.reshape(block_count, block_rows),
        ),
    )
    return (query_grad.reshape(seq_len, head_count, head_dim), key_grad, value_grad)


def contract(left_side, right_side):
    return lax.dot_general(
        left_side, right_side, (((0, 1), (0, 1)), ((), ())), preferred_element_type=jnp.float32
    )


def on_device(hidden_in, segments, timestep, w_qkv, w_out, w_up, w_down, w_mod, b_mod, cotangent):
    row_count, local_len, model_width = hidden_in.shape
    seq_len = segments.shape[1]
    section_count = lax.axis_size("section")
    section_index = lax.axis_index("section")
    layer_index = section_index % 2
    even_section = layer_index == 0
    wqkv_own = take_row(w_qkv, layer_index)
    wout_own = take_row(w_out, layer_index)
    wup_own = take_row(w_up, layer_index)
    wdown_own = take_row(w_down, layer_index)
    local_width = wout_own.shape[0]
    head_count = local_width // HEAD_SIZE
    hidden_width = wup_own.shape[1]
    block_rows = min(512, seq_len)
    features = time_features(timestep, w_mod.shape[1])
    modulation = jnp.dot(
        features, take_row(w_mod, layer_index).astype(jnp.float32), precision=highest
    ) + take_row(b_mod, layer_index).astype(jnp.float32)
    cosine, sine_table = rotary_tables(seq_len, HEAD_SIZE)

    def forward_one(layer_in, mod_row, segment_row):
        shift_a, scale_a, gate_a, shift_b, scale_b, gate_b = jnp.split(mod_row, 6)
        normed_a, inverse_a = normalize(layer_in)
        scaled_a = (normed_a * (1.0 + scale_a) + shift_a).astype(jnp.bfloat16)
        gathered_a = lax.all_gather(scaled_a, "tensor", axis=0, tiled=True)
        projected = jnp.dot(gathered_a, wqkv_own, preferred_element_type=jnp.float32).reshape(
            seq_len, head_count, 3, HEAD_SIZE
        )
        query_rows = rotate(projected[:, :, 0], cosine, sine_table).astype(jnp.bfloat16)
        key_rows = rotate(projected[:, :, 1], cosine, sine_table).astype(jnp.bfloat16)
        values = projected[:, :, 2].astype(jnp.bfloat16)
        mixed_heads, log_totals = attend(query_rows, key_rows, values, segment_row)
        branch_a = lax.psum_scatter(
            jnp.dot(mixed_heads, wout_own, preferred_element_type=jnp.float32).astype(jnp.bfloat16),
            "tensor",
            scatter_dimension=0,
            tiled=True,
        ).astype(jnp.float32)
        middle = layer_in + gate_a * branch_a
        normed_b, inverse_b = normalize(middle)
        scaled_b = (normed_b * (1.0 + scale_b) + shift_b).astype(jnp.bfloat16)
        gathered_b = lax.all_gather(scaled_b, "tensor", axis=0, tiled=True)
        pre_act = jnp.dot(gathered_b, wup_own, preferred_element_type=jnp.float32)
        activated = gelu_tanh(pre_act).astype(jnp.bfloat16)
        branch_b = lax.psum_scatter(
            jnp.dot(activated, wdown_own, preferred_element_type=jnp.float32).astype(jnp.bfloat16),
            "tensor",
            scatter_dimension=0,
            tiled=True,
        ).astype(jnp.float32)
        result = middle + gate_b * branch_b
        return (
            result,
            (
                layer_in,
                gathered_a,
                query_rows,
                key_rows,
                values,
                mixed_heads,
                log_totals,
                branch_a,
                middle,
                gathered_b,
                pre_act,
                branch_b,
            ),
        )

    def backward_one(grad_out, kept_rows, mod_row, segment_row):
        (
            layer_in,
            gathered_a,
            query_rows,
            key_rows,
            values,
            mixed_heads,
            log_totals,
            branch_a,
            middle,
            gathered_b,
            pre_act,
            branch_b,
        ) = kept_rows
        shift_a, scale_a, gate_a, shift_b, scale_b, gate_b = jnp.split(mod_row, 6)
        d_gate_b = jnp.sum(grad_out * branch_b, axis=0)
        d_branch_b = (gate_b * grad_out).astype(jnp.bfloat16)
        full_grad_b = lax.all_gather(d_branch_b, "tensor", axis=0, tiled=True)
        d_activated = jnp.dot(full_grad_b, wdown_own.T, preferred_element_type=jnp.float32)
        gelu_pullback = jax.vjp(gelu_tanh, pre_act)[1]
        d_pre = gelu_pullback(d_activated)[0].astype(jnp.bfloat16)
        d_scaled_b = lax.psum_scatter(
            jnp.dot(d_pre, wup_own.T, preferred_element_type=jnp.float32).astype(jnp.bfloat16),
            "tensor",
            scatter_dimension=0,
            tiled=True,
        ).astype(jnp.float32)
        normed_b, inverse_b = normalize(middle)
        d_scale_b = jnp.sum(d_scaled_b * normed_b, axis=0)
        d_shift_b = jnp.sum(d_scaled_b, axis=0)
        d_middle = grad_out + norm_back(d_scaled_b * (1.0 + scale_b), normed_b, inverse_b)
        d_gate_a = jnp.sum(d_middle * branch_a, axis=0)
        d_branch_a = (gate_a * d_middle).astype(jnp.bfloat16)
        full_grad_a = lax.all_gather(d_branch_a, "tensor", axis=0, tiled=True)
        d_mixed = (
            jnp.dot(full_grad_a, wout_own.T, preferred_element_type=jnp.float32)
            .astype(jnp.bfloat16)
            .reshape(seq_len, head_count, HEAD_SIZE)
        )
        d_query, d_keys, d_values = attend_back(
            d_mixed, query_rows, key_rows, values, log_totals, segment_row
        )
        d_projected = (
            jnp.stack(
                [
                    rotate(d_query, cosine, -sine_table),
                    rotate(d_keys, cosine, -sine_table),
                    d_values,
                ],
                axis=2,
            )
            .astype(jnp.bfloat16)
            .reshape(seq_len, 3 * local_width)
        )
        d_scaled_a = lax.psum_scatter(
            jnp.dot(d_projected, wqkv_own.T, preferred_element_type=jnp.float32).astype(
                jnp.bfloat16
            ),
            "tensor",
            scatter_dimension=0,
            tiled=True,
        ).astype(jnp.float32)
        normed_a, inverse_a = normalize(layer_in)
        d_scale_a = jnp.sum(d_scaled_a * normed_a, axis=0)
        d_shift_a = jnp.sum(d_scaled_a, axis=0)
        d_layer_in = d_middle + norm_back(d_scaled_a * (1.0 + scale_a), normed_a, inverse_a)
        d_modulation = jnp.concatenate(
            [d_shift_a, d_scale_a, d_gate_a, d_shift_b, d_scale_b, d_gate_b]
        )
        return (d_layer_in, (full_grad_a, d_projected, full_grad_b, d_pre, d_modulation))

    def zero_rows(shape_tail, dtype_name):
        return jnp.zeros((row_count,) + shape_tail, dtype_name)

    kept_start = (
        zero_rows((local_len, model_width), jnp.float32),
        zero_rows((seq_len, model_width), jnp.bfloat16),
        zero_rows((seq_len, head_count, HEAD_SIZE), jnp.bfloat16),
        zero_rows((seq_len, head_count, HEAD_SIZE), jnp.bfloat16),
        zero_rows((seq_len, head_count, HEAD_SIZE), jnp.bfloat16),
        zero_rows((seq_len, local_width), jnp.bfloat16),
        zero_rows((seq_len // block_rows, head_count, block_rows), jnp.float32),
        zero_rows((local_len, model_width), jnp.float32),
        zero_rows((local_len, model_width), jnp.float32),
        zero_rows((seq_len, model_width), jnp.bfloat16),
        zero_rows((seq_len, hidden_width), jnp.float32),
        zero_rows((local_len, model_width), jnp.float32),
    )

    def forward_tick(tick_index, carried):
        incoming, results, kept_all = carried
        micro_index = tick_index - section_index
        usable = (micro_index >= 0) & (micro_index < row_count)
        clamped = jnp.clip(micro_index, 0, row_count - 1)
        layer_in = incoming.astype(jnp.float32) + jnp.where(
            even_section, take_row(hidden_in, clamped).astype(jnp.float32), 0.0
        )
        result, kept_rows = forward_one(
            layer_in, take_row(modulation, clamped), take_row(segments, clamped)
        )
        outgoing = result.astype(jnp.bfloat16)
        results = put_row(results, outgoing, clamped, usable)
        kept_all = tuple(
            (
                put_row(buffer, piece_new, clamped, usable)
                for buffer, piece_new in zip(kept_all, kept_rows)
            )
        )
        incoming = from_behind(outgoing, "section", 1)
        return (incoming, results, kept_all)

    forward_state = (
        jnp.zeros((local_len, model_width), jnp.bfloat16),
        zero_rows((local_len, model_width), jnp.bfloat16),
        kept_start,
    )
    _, results, kept_all = lax.fori_loop(
        0, row_count + section_count - 1, forward_tick, forward_state
    )
    saved_start = (
        zero_rows((seq_len, model_width), jnp.bfloat16),
        zero_rows((seq_len, 3 * local_width), jnp.bfloat16),
        zero_rows((seq_len, model_width), jnp.bfloat16),
        zero_rows((seq_len, hidden_width), jnp.bfloat16),
        zero_rows((6 * model_width,), jnp.float32),
    )
    own_cot = cotangent[0]

    def backward_tick(tick_index, carried):
        incoming, grads_in, saved_all = carried
        micro_index = tick_index - 1 + layer_index
        usable = (micro_index >= 0) & (micro_index < row_count)
        clamped = jnp.clip(micro_index, 0, row_count - 1)
        grad_out = take_row(own_cot, clamped).astype(jnp.float32) + jnp.where(
            even_section, incoming, 0.0
        )
        kept_rows = tuple((take_row(buffer, clamped) for buffer in kept_all))
        d_layer_in, saved = backward_one(
            grad_out, kept_rows, take_row(modulation, clamped), take_row(segments, clamped)
        )
        grads_in = put_row(grads_in, d_layer_in, clamped, usable)
        saved_all = tuple(
            (
                put_row(buffer, piece_new, clamped, usable)
                for buffer, piece_new in zip(saved_all, saved)
            )
        )
        incoming = from_behind(d_layer_in.astype(jnp.bfloat16), "section", -1).astype(
            d_layer_in.dtype
        )
        return (incoming, grads_in, saved_all)

    backward_state = (
        jnp.zeros((local_len, model_width), jnp.float32),
        zero_rows((local_len, model_width), jnp.float32),
        saved_start,
    )
    _, grads_in, saved_all = lax.fori_loop(0, row_count + 1, backward_tick, backward_state)
    full_grad_a_all, d_projected_all, full_grad_b_all, d_pre_all, d_mod_all = saved_all
    grad_qkv = contract(kept_all[1], d_projected_all)
    grad_out = contract(kept_all[5], full_grad_a_all)
    grad_up = contract(kept_all[9], d_pre_all)
    grad_down = contract(gelu_tanh(kept_all[10]).astype(jnp.bfloat16), full_grad_b_all)
    mod_total = lax.psum(d_mod_all.astype(jnp.bfloat16), "tensor").astype(jnp.float32)
    grad_mod = jnp.dot(features.T, mod_total, precision=highest)
    grad_bias = jnp.sum(mod_total, axis=0)

    def slotted(gradient):
        return jnp.stack(
            [jnp.where(even_section, gradient, 0.0), jnp.where(even_section, 0.0, gradient)]
        )

    summed = (
        lax.psum(slotted(grad_qkv).astype(jnp.bfloat16), ("dp", "section")).astype(jnp.float32),
        lax.psum(slotted(grad_out).astype(jnp.bfloat16), ("dp", "section")).astype(jnp.float32),
        lax.psum(slotted(grad_up).astype(jnp.bfloat16), ("dp", "section")).astype(jnp.float32),
        lax.psum(slotted(grad_down).astype(jnp.bfloat16), ("dp", "section")).astype(jnp.float32),
        lax.psum(slotted(grad_mod).astype(jnp.bfloat16), ("dp", "section")).astype(jnp.float32),
        lax.psum(slotted(grad_bias).astype(jnp.bfloat16), ("dp", "section")).astype(jnp.float32),
    )
    return (
        results[None],
        grads_in[None],
        summed[0],
        summed[1],
        summed[2],
        summed[3],
        summed[4],
        summed[5],
    )


def solution(mesh):
    placed = (
        P("dp", "tensor", None),
        P("dp", None),
        P("dp"),
        P(None, None, "tensor"),
        P(None, "tensor", None),
        P(None, None, "tensor"),
        P(None, "tensor", None),
        P(),
        P(),
        P("section", "dp", "tensor", None),
    )
    return jax.shard_map(
        on_device,
        mesh=mesh,
        in_specs=placed,
        out_specs=(
            P("section", "dp", "tensor", None),
            P("section", "dp", "tensor", None),
            P(None, None, "tensor"),
            P(None, "tensor", None),
            P(None, None, "tensor"),
            P(None, "tensor", None),
            P(),
            P(),
        ),
        check_vma=False,
    )
```

profile of v0, /device:TPU:16, one launch (start us, length us, event | category | flops | bytes accessed | tf_op | source)
XLA Modules:
  0.0 1944.5 jit_solution(7238217486987095349)
XLA Ops:
  33.9 844.4 %while.159 = (s32[]{:T(128)}, bf16[256,768]{1,0:T(8,128)(2,1)S(1)}, bf16[2,256,768]{2,1,0:T(8,128)(2,1)}, f32[2,256,768]{2,1,0:T(8,128)S(1)}, bf16[2,1024,768]{2...) while((s32[]{:T(128)}, bf16[256,768]{1,0:T(8,128)(2,1)S(1)}, ...), condition=%wide.region_11.12_spmd.clone.clone.clone, body=%wide.region_0.11_spmd.clone.clone.clone.sunk | while | flops 4071820800 | bytes 208675632 | solution.py:353
  86.6 30.9 %reduce-scatter.5.cloned.1.call-done = bf16[256,768]{1,0:T(8,128)(2,1)} async-done(((bf16[1024,768]{1,0:T(8,128)(2,1)}), bf16[256,768]{1,0:T(8,128)(2,1)}) %reduce-scatter.5.cloned.1.call-update) | async-done | bytes 393232 | tf_op jit(solution)/shard_map/while/body/eval_jaxpr/reduce_scatter | solution.py:199
  208.7 20.8 %all-gather.5.cloned.1.call-done = bf16[1024,768]{1,0:T(8,128)(2,1)} async-done(((bf16[256,768]{1,0:T(8,128)(2,1)}), bf16[1024,768]{1,0:T(8,128)(2,1)}) %all-gather.5.cloned.1.call-update) | async-done | bytes 1572880 | tf_op jit(solution)/shard_map/while/body/eval_jaxpr/all_gather | solution.py:191
  255.5 30.9 %reduce-scatter.5.cloned.1.call-done = bf16[256,768]{1,0:T(8,128)(2,1)} async-done(((bf16[1024,768]{1,0:T(8,128)(2,1)}), bf16[256,768]{1,0:T(8,128)(2,1)}) %reduce-scatter.5.cloned.1.call-update) | async-done | bytes 393232 | tf_op jit(solution)/shard_map/while/body/eval_jaxpr/reduce_scatter | solution.py:199
  377.6 20.8 %all-gather.5.cloned.1.call-done = bf16[1024,768]{1,0:T(8,128)(2,1)} async-done(((bf16[256,768]{1,0:T(8,128)(2,1)}), bf16[1024,768]{1,0:T(8,128)(2,1)}) %all-gather.5.cloned.1.call-update) | async-done | bytes 1572880 | tf_op jit(solution)/shard_map/while/body/eval_jaxpr/all_gather | solution.py:191
  424.4 30.9 %reduce-scatter.5.cloned.1.call-done = bf16[256,768]{1,0:T(8,128)(2,1)} async-done(((bf16[1024,768]{1,0:T(8,128)(2,1)}), bf16[256,768]{1,0:T(8,128)(2,1)}) %reduce-scatter.5.cloned.1.call-update) | async-done | bytes 393232 | tf_op jit(solution)/shard_map/while/body/eval_jaxpr/reduce_scatter | solution.py:199
  546.6 20.8 %all-gather.5.cloned.1.call-done = bf16[1024,768]{1,0:T(8,128)(2,1)} async-done(((bf16[256,768]{1,0:T(8,128)(2,1)}), bf16[1024,768]{1,0:T(8,128)(2,1)}) %all-gather.5.cloned.1.call-update) | async-done | bytes 1572880 | tf_op jit(solution)/shard_map/while/body/eval_jaxpr/all_gather | solution.py:191
  593.4 30.9 %reduce-scatter.5.cloned.1.call-done = bf16[256,768]{1,0:T(8,128)(2,1)} async-done(((bf16[1024,768]{1,0:T(8,128)(2,1)}), bf16[256,768]{1,0:T(8,128)(2,1)}) %reduce-scatter.5.cloned.1.call-update) | async-done | bytes 393232 | tf_op jit(solution)/shard_map/while/body/eval_jaxpr/reduce_scatter | solution.py:199
  715.5 20.8 %all-gather.5.cloned.1.call-done = bf16[1024,768]{1,0:T(8,128)(2,1)} async-done(((bf16[256,768]{1,0:T(8,128)(2,1)}), bf16[1024,768]{1,0:T(8,128)(2,1)}) %all-gather.5.cloned.1.call-update) | async-done | bytes 1572880 | tf_op jit(solution)/shard_map/while/body/eval_jaxpr/all_gather | solution.py:191
  762.4 30.9 %reduce-scatter.5.cloned.1.call-done = bf16[256,768]{1,0:T(8,128)(2,1)} async-done(((bf16[1024,768]{1,0:T(8,128)(2,1)}), bf16[256,768]{1,0:T(8,128)(2,1)}) %reduce-scatter.5.cloned.1.call-update) | async-done | bytes 393232 | tf_op jit(solution)/shard_map/while/body/eval_jaxpr/reduce_scatter | solution.py:199
  887.5 644.8 %while.161 = (s32[]{:T(128)}, f32[256,768]{1,0:T(8,128)S(1)}, f32[2,256,768]{2,1,0:T(8,128)}, bf16[2,1024,768]{2,1,0:T(8,128)(2,1)}, bf16[2,1024,576]{1,2,0:T(8,...) while((s32[]{:T(128)}, f32[256,768]{1,0:T(8,128)S(1)}, ...), condition=%wide.region_32.33_spmd.clone.clone.clone.clone, body=%wide.region_12.32_spmd.clone.clone.clone.clone.sunk | while | flops 4693361152 | bytes 329208544 | solution.py:394
  908.6 21.2 %all-gather.9.cloned.1.call-done = bf16[1024,768]{1,0:T(8,128)(2,1)} async-done(((bf16[256,768]{1,0:T(8,128)(2,1)}), bf16[1024,768]{1,0:T(8,128)(2,1)}) %all-gather.9.cloned.1.call-update) | async-done | bytes 1572880 | tf_op jit(solution)/shard_map/while/body/eval_jaxpr/all_gather | solution.py:254
  940.4 34.2 %reduce-scatter.9.cloned.1.call-done = bf16[256,768]{1,0:T(8,128)(2,1)} async-done(((bf16[1024,768]{1,0:T(8,128)(2,1)}), bf16[256,768]{1,0:T(8,128)(2,1)}) %reduce-scatter.9.cloned.1.call-update) | async-done | bytes 393232 | tf_op jit(solution)/shard_map/while/body/eval_jaxpr/reduce_scatter | solution.py:258
  1006.7 47.4 %while.163 = (s32[]{:T(128)}, f32[1024,3,64]{0,2,1:T(8,128)}, f32[1024,3,64]{0,2,1:T(8,128)}, f32[2,512,3,64]{1,0,3,2:T(2,128)}, bf16[2,512,3,64]{1,3,2,0:T(8,12...) while((s32[]{:T(128)}, f32[1024,3,64]{0,2,1:T(8,128)}, ...), condition=%wide.region_22.22_spmd.clone, body=%wide.region_20.21_spmd.clone.sunk | while | flops 1031830016 | bytes 118382056 | solution.py:147
  1071.6 24.5 %reduce-scatter.11.cloned.1.call-done = bf16[256,768]{1,0:T(8,128)(2,1)} async-done(((bf16[1024,768]{1,0:T(8,128)(2,1)}), bf16[256,768]{1,0:T(8,128)(2,1)}) %reduce-scatter.11.cloned.1.call-update) | async-done | bytes 393232 | tf_op jit(solution)/shard_map/while/body/eval_jaxpr/reduce_scatter | solution.py:291
  1150.1 34.2 %reduce-scatter.9.cloned.1.call-done = bf16[256,768]{1,0:T(8,128)(2,1)} async-done(((bf16[1024,768]{1,0:T(8,128)(2,1)}), bf16[256,768]{1,0:T(8,128)(2,1)}) %reduce-scatter.9.cloned.1.call-update) | async-done | bytes 393232 | tf_op jit(solution)/shard_map/while/body/eval_jaxpr/reduce_scatter | solution.py:258
  1216.4 47.4 %while.163 = (s32[]{:T(128)}, f32[1024,3,64]{0,2,1:T(8,128)}, f32[1024,3,64]{0,2,1:T(8,128)}, f32[2,512,3,64]{1,0,3,2:T(2,128)}, bf16[2,512,3,64]{1,3,2,0:T(8,12...) while((s32[]{:T(128)}, f32[1024,3,64]{0,2,1:T(8,128)}, ...), condition=%wide.region_22.22_spmd.clone, body=%wide.region_20.21_spmd.clone.sunk | while | flops 1031830016 | bytes 118382056 | solution.py:147
  1281.3 24.5 %reduce-scatter.11.cloned.1.call-done = bf16[256,768]{1,0:T(8,128)(2,1)} async-done(((bf16[1024,768]{1,0:T(8,128)(2,1)}), bf16[256,768]{1,0:T(8,128)(2,1)}) %reduce-scatter.11.cloned.1.call-update) | async-done | bytes 393232 | tf_op jit(solution)/shard_map/while/body/eval_jaxpr/reduce_scatter | solution.py:291
  1328.7 20.5 %all-gather.9.cloned.1.call-done = bf16[1024,768]{1,0:T(8,128)(2,1)} async-done(((bf16[256,768]{1,0:T(8,128)(2,1)}), bf16[1024,768]{1,0:T(8,128)(2,1)}) %all-gather.9.cloned.1.call-update) | async-done | bytes 1572880 | tf_op jit(solution)/shard_map/while/body/eval_jaxpr/all_gather | solution.py:254
  1359.7 34.2 %reduce-scatter.9.cloned.1.call-done = bf16[256,768]{1,0:T(8,128)(2,1)} async-done(((bf16[1024,768]{1,0:T(8,128)(2,1)}), bf16[256,768]{1,0:T(8,128)(2,1)}) %reduce-scatter.9.cloned.1.call-update) | async-done | bytes 393232 | tf_op jit(solution)/shard_map/while/body/eval_jaxpr/reduce_scatter | solution.py:258
  1426.1 47.4 %while.163 = (s32[]{:T(128)}, f32[1024,3,64]{0,2,1:T(8,128)}, f32[1024,3,64]{0,2,1:T(8,128)}, f32[2,512,3,64]{1,0,3,2:T(2,128)}, bf16[2,512,3,64]{1,3,2,0:T(8,12...) while((s32[]{:T(128)}, f32[1024,3,64]{0,2,1:T(8,128)}, ...), condition=%wide.region_22.22_spmd.clone, body=%wide.region_20.21_spmd.clone.sunk | while | flops 1031830016 | bytes 118382056 | solution.py:147
  1490.9 24.5 %reduce-scatter.11.cloned.1.call-done = bf16[256,768]{1,0:T(8,128)(2,1)} async-done(((bf16[1024,768]{1,0:T(8,128)(2,1)}), bf16[256,768]{1,0:T(8,128)(2,1)}) %reduce-scatter.11.cloned.1.call-update) | async-done | bytes 393232 | tf_op jit(solution)/shard_map/while/body/eval_jaxpr/reduce_scatter | solution.py:291
  1573.0 156.2 %psum.55 = bf16[2,4608]{1,0:T(2,128)(2,1)S(1)} all-reduce(bf16[2,4608]{1,0:T(2,128)(2,1)S(1)} %pad_maximum_fusion.7), channel_id=1, replica_groups=mesh['dp'=8,'section'=4,'tensor'=4] {'dp','section'}, use_global_device_ids=true, to_apply=%region_40.41 | all-reduce | flops 9216 | bytes 36864 | tf_op jit(solution)/shard_map/psum | solution.py:415
  1729.8 194.3 %all-reduce.3.cloned.1.call-done = (bf16[2,768,576]{1,2,0:T(8,128)(2,1)}, bf16[2,192,768]{2,1,0:T(8,128)(2,1)}, bf16[2,768,768]{2,1,0:T(8,128)(2,1)}, bf16[2,768,768]{2,1,0:T(8,128)(2,1)}, bf16[2,128,4608]{2,1,0:T(8,128)(2,1)}) async-done(((bf16[2,768,576]{1,2,0:T(8,128)(2,1)}, bf16[2,192,768]{2,1,0:T(8,128)(2,1)}, bf16[2,768,768]{2,1,0:T(8,128)(2,1)}, bf16[2,768,768]{2,1,0:T(8,128)(2,1)}, ...) | async-done | bytes 9437200 | tf_op jit(solution)/shard_map/psum | solution.py:410
  (1287 shorter events, 1167.5 us)
Async XLA Ops:
  37.2 80.3 %reduce-scatter.5.cloned.1.call-start = ((), (), s32[]{:S(2)}) async-start(), calls=%async_computation.6 | async-start | bytes 1966080 | tf_op jit(solution)/shard_map/while/body/eval_jaxpr/reduce_scatter | solution.py:199
  82.9 62.6 %all-gather.7.cloned.1.call-start = ((), (), s32[]{:S(2)}) async-start(), calls=%async_computation.7 | async-start | bytes 1966080 | tf_op jit(solution)/shard_map/while/body/eval_jaxpr/all_gather | solution.py:208
  122.3 66.9 %reduce-scatter.7.cloned.1.call-start = ((), (), s32[]{:S(2)}) async-start(), calls=%async_computation.8 | async-start | bytes 1966080 | tf_op jit(solution)/shard_map/while/body/eval_jaxpr/reduce_scatter | solution.py:211
  205.5 80.9 %reduce-scatter.5.cloned.1.call-start = ((), (), s32[]{:S(2)}) async-start(), calls=%async_computation.6 | async-start | bytes 1966080 | tf_op jit(solution)/shard_map/while/body/eval_jaxpr/reduce_scatter | solution.py:199
  251.8 62.6 %all-gather.7.cloned.1.call-start = ((), (), s32[]{:S(2)}) async-start(), calls=%async_computation.7 | async-start | bytes 1966080 | tf_op jit(solution)/shard_map/while/body/eval_jaxpr/all_gather | solution.py:208
  291.2 66.9 %reduce-scatter.7.cloned.1.call-start = ((), (), s32[]{:S(2)}) async-start(), calls=%async_computation.8 | async-start | bytes 1966080 | tf_op jit(solution)/shard_map/while/body/eval_jaxpr/reduce_scatter | solution.py:211
  374.5 80.9 %reduce-scatter.5.cloned.1.call-start = ((), (), s32[]{:S(2)}) async-start(), calls=%async_computation.6 | async-start | bytes 1966080 | tf_op jit(solution)/shard_map/while/body/eval_jaxpr/reduce_scatter | solution.py:199
  420.7 62.6 %all-gather.7.cloned.1.call-start = ((), (), s32[]{:S(2)}) async-start(), calls=%async_computation.7 | async-start | bytes 1966080 | tf_op jit(solution)/shard_map/while/body/eval_jaxpr/all_gather | solution.py:208
  460.1 66.9 %reduce-scatter.7.cloned.1.call-start = ((), (), s32[]{:S(2)}) async-start(), calls=%async_computation.8 | async-start | bytes 1966080 | tf_op jit(solution)/shard_map/while/body/eval_jaxpr/reduce_scatter | solution.py:211
  543.4 80.9 %reduce-scatter.5.cloned.1.call-start = ((), (), s32[]{:S(2)}) async-start(), calls=%async_computation.6 | async-start | bytes 1966080 | tf_op jit(solution)/shard_map/while/body/eval_jaxpr/reduce_scatter | solution.py:199
  589.7 62.6 %all-gather.7.cloned.1.call-start = ((), (), s32[]{:S(2)}) async-start(), calls=%async_computation.7 | async-start | bytes 1966080 | tf_op jit(solution)/shard_map/while/body/eval_jaxpr/all_gather | solution.py:208
  629.0 67.0 %reduce-scatter.7.cloned.1.call-start = ((), (), s32[]{:S(2)}) async-start(), calls=%async_computation.8 | async-start | bytes 1966080 | tf_op jit(solution)/shard_map/while/body/eval_jaxpr/reduce_scatter | solution.py:211
  712.4 80.9 %reduce-scatter.5.cloned.1.call-start = ((), (), s32[]{:S(2)}) async-start(), calls=%async_computation.6 | async-start | bytes 1966080 | tf_op jit(solution)/shard_map/while/body/eval_jaxpr/reduce_scatter | solution.py:199
  798.0 67.0 %reduce-scatter.7.cloned.1.call-start = ((), (), s32[]{:S(2)}) async-start(), calls=%async_computation.8 | async-start | bytes 1966080 | tf_op jit(solution)/shard_map/while/body/eval_jaxpr/reduce_scatter | solution.py:211
  905.8 68.7 %reduce-scatter.9.cloned.1.call-start = ((), (), s32[]{:S(2)}) async-start(), calls=%async_computation.10 | async-start | bytes 1966080 | tf_op jit(solution)/shard_map/while/body/eval_jaxpr/reduce_scatter | solution.py:258
  939.9 64.3 %all-gather.11.cloned.1.call-start = ((), (), s32[]{:S(2)}) async-start(), calls=%async_computation.11 | async-start | bytes 1966080 | tf_op jit(solution)/shard_map/while/body/eval_jaxpr/all_gather | solution.py:270
  981.0 115.0 %reduce-scatter.11.cloned.1.call-start = ((), (), s32[]{:S(2)}) async-start(), calls=%async_computation.12 | async-start | bytes 1966080 | tf_op jit(solution)/shard_map/while/body/eval_jaxpr/reduce_scatter | solution.py:291
  1116.3 68.0 %reduce-scatter.9.cloned.1.call-start = ((), (), s32[]{:S(2)}) async-start(), calls=%async_computation.10 | async-start | bytes 1966080 | tf_op jit(solution)/shard_map/while/body/eval_jaxpr/reduce_scatter | solution.py:258
  1149.6 64.3 %all-gather.11.cloned.1.call-start = ((), (), s32[]{:S(2)}) async-start(), calls=%async_computation.11 | async-start | bytes 1966080 | tf_op jit(solution)/shard_map/while/body/eval_jaxpr/all_gather | solution.py:270
  1190.7 115.1 %reduce-scatter.11.cloned.1.call-start = ((), (), s32[]{:S(2)}) async-start(), calls=%async_computation.12 | async-start | bytes 1966080 | tf_op jit(solution)/shard_map/while/body/eval_jaxpr/reduce_scatter | solution.py:291
  1326.0 68.0 %reduce-scatter.9.cloned.1.call-start = ((), (), s32[]{:S(2)}) async-start(), calls=%async_computation.10 | async-start | bytes 1966080 | tf_op jit(solution)/shard_map/while/body/eval_jaxpr/reduce_scatter | solution.py:258
  1359.3 64.3 %all-gather.11.cloned.1.call-start = ((), (), s32[]{:S(2)}) async-start(), calls=%async_computation.11 | async-start | bytes 1966080 | tf_op jit(solution)/shard_map/while/body/eval_jaxpr/all_gather | solution.py:270
  1400.4 115.0 %reduce-scatter.11.cloned.1.call-start = ((), (), s32[]{:S(2)}) async-start(), calls=%async_computation.12 | async-start | bytes 1966080 | tf_op jit(solution)/shard_map/while/body/eval_jaxpr/reduce_scatter | solution.py:291
  1532.2 391.9 %all-reduce.3.cloned.1.call-start = ((), (), s32[]{:S(2)}) async-start(), calls=%async_computation.4 | async-start | bytes 18874368 | tf_op jit(solution)/shard_map/psum | solution.py:410
  (319 other events, 2043.9 us)
Sparse Core Ops, SparseCore 0:
  37.4 23.1 all-gather.4
  83.0 34.4 reduce-scatter.4
  154.7 34.4 reduce-scatter.6
  205.7 23.8 all-gather.4
  251.9 34.4 reduce-scatter.4
  291.3 23.1 all-gather.6
  323.6 34.4 reduce-scatter.6
  374.6 23.8 all-gather.4
  420.9 34.4 reduce-scatter.4
  460.2 23.1 all-gather.6
  492.6 34.4 reduce-scatter.6
  543.5 23.7 all-gather.4
  589.8 34.4 reduce-scatter.4
  661.5 34.4 reduce-scatter.6
  712.5 23.8 all-gather.4
  758.8 34.4 reduce-scatter.4
  830.4 34.4 reduce-scatter.6
  906.0 23.7 all-gather.8
  940.1 34.4 reduce-scatter.8
  1061.5 34.4 reduce-scatter.10
  1149.7 34.4 reduce-scatter.8
  1271.2 34.4 reduce-scatter.10
  1359.4 34.4 reduce-scatter.8
  1480.9 34.4 reduce-scatter.10
  (8 shorter events, 184.3 us)
Sparse Core Ops, SparseCore 1:
  1572.9 351.2 all-reduce.2
where the time goes:
time: 1960 us; the launch traced here: 1940 us
  waiting for transfers between devices  974 us (50%)
  local copies, waits for them, and re-layouts  257 us (13%)
  matrix products  247 us (13%)
  other arithmetic  235 us (12%)
  blocking collectives  172 us (9%)
  starting transfers between devices  23.7 us (1%)
  loops' own time  20.1 us (1%)
    psum x1, waiting for transfers between devices, on_device(): lax.psum(slotted(grad_qkv).astype(jnp.bfloat16), ('dp', 'section'))  194 us
    psum x1, blocking collectives, on_device(): lax.psum(slotted(grad_bias).astype(jnp.bfloat16), ('dp', 'section'))  156 us
    reduce_scatter x5, waiting for transfers between devices, forward_one(): lax.psum_scatter(jnp.dot(mixed_heads, wout_own, preferred_element_type=jn...  155 us
    dynamic_slice x62, local copies, waits for them, and re-layouts, take_row(): return lax.dynamic_index_in_dim(array, position, 0, keepdims=False)  110 us
    all_gather x5, waiting for transfers between devices, forward_one(): gathered_a = lax.all_gather(scaled_a, 'tensor', axis=0, tiled=True)  103 us
    reduce_scatter x3, waiting for transfers between devices, backward_one(): lax.psum_scatter(jnp.dot(d_pre, wup_own.T, preferred_element_type=jnp.flo...  103 us
    all_gather x5, waiting for transfers between devices, forward_one(): gathered_b = lax.all_gather(scaled_b, 'tensor', axis=0, tiled=True)  97.3 us
    dynamic_update_slice x57, other arithmetic, put_row(): return lax.dynamic_update_index_in_dim(buffer, merged, position, 0)  93.7 us
  transfers between devices with their start and end apart: 41, of which 41 were waited for; matrix products, arithmetic and copies ran while one was open for 11% of the time, Pallas kernels for 0%

commit v1 on v0

v1 whole, which is shorter than its diff:
```python
import functools

import jax
import jax.numpy as jnp
import numpy as np
from jax import lax
from jax.experimental import pallas as pl
from jax.experimental.pallas import tpu as pltpu
from jax.sharding import PartitionSpec as P

MESH = pl.DeviceIdType.MESH
BF = jnp.bfloat16
F32 = jnp.float32
highest = lax.Precision.HIGHEST
EPS = 1e-06
D = 768
TOK = 128
SEQ = 1024
ANY = pl.BlockSpec(memory_space=pl.ANY)
VM = pl.BlockSpec(memory_space=pltpu.VMEM)
ROWS = 2304
PACK = (0, 6, 1, 7, 2, 8, 3, 4, 5)
UNPACK = tuple(PACK.index(g) for g in range(9))


def here():
    dp = lax.axis_index("dp")
    t = lax.axis_index("tensor")
    return dp // 2, dp % 2, lax.axis_index("section"), t // 2, t % 2


def dev(x, ylo, z, yhi, c):
    return (2 * x + ylo, z, 2 * yhi + c)


def push(src, dst, send_sem, recv_sem, where):
    return pltpu.make_async_remote_copy(
        src_ref=src,
        dst_ref=dst,
        send_sem=send_sem,
        recv_sem=recv_sem,
        device_id=where,
        device_id_type=MESH,
    )


def greet(devices):
    barrier = pltpu.get_barrier_semaphore()
    for where in devices:
        pl.semaphore_signal(barrier, inc=1, device_id=where, device_id_type=MESH)
    return lambda: pl.semaphore_wait(barrier, len(devices))


def nn(a, b):
    return lax.dot_general(a, b, (((1,), (0,)), ((), ())), preferred_element_type=F32)


def nt(a, b):
    return lax.dot_general(a, b, (((1,), (1,)), ((), ())), preferred_element_type=F32)


def tn(a, b):
    return lax.dot_general(a, b, (((0,), (0,)), ((), ())), preferred_element_type=F32)


def normalize(values):
    centred = values - jnp.mean(values, axis=-1, keepdims=True)
    inverse = lax.rsqrt(jnp.mean(centred * centred, axis=-1, keepdims=True) + EPS)
    return centred * inverse, inverse


def norm_back(gradient, normed, inverse):
    return inverse * (
        gradient
        - jnp.mean(gradient, axis=-1, keepdims=True)
        - normed * jnp.mean(gradient * normed, axis=-1, keepdims=True)
    )


def lanes(shape):
    return lax.broadcasted_iota(jnp.int32, shape, len(shape) - 1)


def swap(x):
    return pltpu.roll(x, 64, 1)


def turn(x, cosine, sine):
    low = (lanes(x.shape) % 64) < 32
    other = jnp.where(low, pltpu.roll(x, 96, 1), pltpu.roll(x, 32, 1))
    return x * cosine + other * sine


def spread(buf, ss, rs, between=None):
    x, ylo, z, yhi, c = here()
    everything = slice(None)

    def at(dims, part, by):
        pos = {"y": ylo, "x": x, "z": z}
        for key, value in by.items():
            pos[key] = value
        return buf.at[tuple(everything if key in dims else pos[key] for key in "yxz") + (part,)]

    def peer(dim, o):
        if dim == "y":
            return dev(x, 1 - ylo, z, yhi, c), 1 - ylo
        if dim == "x":
            return dev((x + o) % 4, ylo, z, yhi, c), (x - o + 4) % 4
        return dev(x, ylo, (z + o) % 4, yhi, c), (z - o + 4) % 4

    orders = ("zyx", "xzy", "yxz")
    for phase in range(3):
        sent, got = [], []
        for part in range(3):
            dim, done = orders[part][phase], orders[part][:phase]
            for o in (1,) if dim == "y" else (2, 1, 3):
                where, origin = peer(dim, o)
                n = (phase * 3 + part) * 3 + o - 1
                cp = push(at(done, part, {}), at(done, part, {}), ss.at[n], rs.at[n], where)
                cp.start()
                sent.append(cp)
                back = at(done, part, {dim: origin})
                got.append((push(back, back, ss.at[n], rs.at[n], where), back))
        if between is not None:
            between(phase, [at(orders[p][:phase], p, {}) for p in range(3)], None)
        for cp, back in got:
            cp.wait_recv()
            if between is not None:
                between(phase, None, back)
        for cp in sent:
            cp.wait_send()


def chips_around():
    x, ylo, z, yhi, c = here()
    found = [dev((x + o) % 4, ylo, z, yhi, c) for o in (1, 2, 3)]
    found += [dev(x, ylo, (z + o) % 4, yhi, c) for o in (1, 2, 3)]
    return found + [dev(x, 1 - ylo, z, yhi, c)]


def prepare_kernel(hid, cot, wloc, x0, cots, w_all, hs, hr, cs, cr, ss, rs, ps, pr, lsem):
    x, ylo, z, yhi, c = here()
    t = 2 * yhi + c
    dp = 2 * x + ylo
    cross = dev(x, 1 - ylo, z, 1 - yhi, c)
    partner = dev(x, ylo, z, yhi, 1 - c)
    group = [(dp, (z + a) % 4, (t + b) % 4) for a in range(4) for b in range(4) if a or b]
    greet(group + [dev((x + o) % 4, ylo, z, yhi, c) for o in (1, 2, 3)] + [dev(x, 1 - ylo, z, yhi, c), cross])()

    own = pltpu.make_async_copy(wloc, w_all.at[t], lsem.at[0])
    own.start()
    first = push(wloc.at[1 - ylo, x, z], w_all.at[t, 1 - ylo, x, z], ps.at[0], pr.at[0], cross)
    first.start()
    side = push(wloc, w_all.at[t], ps.at[1], pr.at[1], partner)
    side.start()

    for b in range(4):
        target = (dp, z, b)
        holder = (t == z) & (t != b)

        @pl.when(holder)
        def _(b=b, target=target):
            push(hid.at[b // 2, b % 2], x0, hs.at[b], hr.at[0], target).start()

        @pl.when((t == z) & (t == b))
        def _(b=b):
            pltpu.make_async_copy(hid.at[b // 2, b % 2], x0, lsem.at[1]).start()

        there = (dp, t, b)
        mine = (t == z) & (t == b)

        @pl.when(jnp.logical_not(mine))
        def _(b=b, there=there):
            push(cot.at[b // 2, b % 2], cots.at[z], cs.at[b], cr.at[z], there).start()

        @pl.when(mine)
        def _(b=b):
            pltpu.make_async_copy(cot.at[b // 2, b % 2], cots.at[z], lsem.at[2]).start()

    other = 2 * (1 - yhi) + c
    buf = w_all.at[other]
    landed = buf.at[ylo, x, z]
    push(landed, landed, ps.at[0], pr.at[0], cross).wait_recv()
    handed = []

    def between(phase, held, back):
        if phase < 2:
            return
        for ref in held if held is not None else [back]:
            n = 2 + len(handed)
            cp = push(ref, ref, ps.at[n], pr.at[n], partner)
            cp.start()
            handed.append(cp)

    spread(buf, ss, rs, between)
    for cp in handed:
        cp.wait_send()
        cp.wait_recv()
    first.wait_send()
    side.wait_send()
    side.wait_recv()
    own.wait()

    for b in range(4):

        @pl.when((t == z) & (t != b))
        def _(b=b):
            push(hid.at[b // 2, b % 2], x0, hs.at[b], hr.at[0], (dp, z, b)).wait_send()

        @pl.when(jnp.logical_not((t == z) & (t == b)))
        def _(b=b):
            push(cot.at[b // 2, b % 2], cots.at[z], cs.at[b], cr.at[z], (dp, t, b)).wait_send()

        mine = (t == z) & (z == b)

        @pl.when(jnp.logical_not(mine))
        def _(b=b):
            push(cots.at[b], cots.at[b], cs.at[b], cr.at[b], partner).wait_recv()

        @pl.when(mine)
        def _(b=b):
            pltpu.make_async_copy(cot.at[b // 2, b % 2], cots.at[z], lsem.at[2]).wait()
            pltpu.make_async_copy(hid.at[b // 2, b % 2], x0, lsem.at[1]).wait()

    @pl.when(t != z)
    def _():
        push(x0, x0, hs.at[0], hr.at[0], partner).wait_recv()


def prepare(hid, cot, wloc):
    dma = pltpu.SemaphoreType.DMA
    return pl.pallas_call(
        prepare_kernel,
        out_shape=(
            jax.ShapeDtypeStruct((TOK, D), BF),
            jax.ShapeDtypeStruct((4, TOK, D), BF),
            jax.ShapeDtypeStruct((4,) + wloc.shape, BF),
        ),
        in_specs=[ANY] * 3,
        out_specs=(ANY,) * 3,
        scratch_shapes=[
            dma((4,)),
            dma((1,)),
            dma((4,)),
            dma((4,)),
            dma((27,)),
            dma((27,)),
            dma((16,)),
            dma((16,)),
            dma((3,)),
        ],
        compiler_params=pltpu.CompilerParams(collective_id=1, has_side_effects=True),
        name="prepare",
    )(hid, cot, wloc)


def fetch(layer, w_all, wq, wo, wu, wd, sem):
    def plan(kind):
        moves = []
        for t in range(4):
            src = w_all.at[t, layer]
            if kind == 0:
                moves.append((src.at[pl.ds(0, 512)], wq.at[pl.ds(512 * t, 512)], 2 * t))
                moves.append((src.at[pl.ds(512, 64)], wq.at[pl.ds(2048 + 64 * t, 64)], 2 * t + 1))
            if kind == 1:
                moves.append((src.at[pl.ds(576, 128)], wo.at[pl.ds(128 * t, 128)], 8 + 2 * t))
                moves.append((src.at[pl.ds(704, 64)], wo.at[pl.ds(512 + 64 * t, 64)], 9 + 2 * t))
            if kind == 2:
                moves.append((src.at[pl.ds(768, 768)], wu.at[t], 16 + t))
            if kind == 3:
                moves.append((src.at[pl.ds(1536, 768)], wd.at[t], 20 + t))
        return [pltpu.make_async_copy(a, b, sem.at[n]) for a, b, n in moves]

    plans = [plan(kind) for kind in range(4)]

    def wait(kind):
        for cp in plans[kind]:
            cp.wait()

    def start(kind):
        for cp in plans[kind]:
            cp.start()

    return start, wait


def weight_scratch():
    return [
        pltpu.VMEM((2304, D), BF),
        pltpu.VMEM((D, D), BF),
        pltpu.VMEM((4, D, D), BF),
        pltpu.VMEM((4, D, D), BF),
        pltpu.SemaphoreType.DMA((24,)),
    ]


def row_group():
    x, ylo, z, yhi, c = here()
    return [(2 * a + b, dev(x, ylo, a, yhi, b)) for a in range(4) for b in range(2)], 2 * z + c


def greet_row():
    x, ylo, z, yhi, c = here()
    me = 2 * z + c
    others = []
    for o in range(1, 8):
        j = (me + o) % 8
        others.append(dev(x, ylo, j // 2, yhi, j % 2))
    return greet(others)


def deal(j, where, me, src, dst, ss, rs):
    @pl.when(me != j)
    def _():
        push(src, dst, ss.at[j], rs.at[me], where).start()

    @pl.when(me == j)
    def _():
        pltpu.make_async_copy(src, dst, ss.at[j]).start()


def dealt(j, where, me, src, dst, ss, rs):
    @pl.when(me != j)
    def _():
        cp = push(src, dst, ss.at[j], rs.at[j], where)
        cp.wait_send()
        cp.wait_recv()

    @pl.when(me == j)
    def _():
        pltpu.make_async_copy(src, dst, ss.at[j]).wait()


def forward_kernel(
    layer, a_ref, b_ref, mod, segc, segr, cosine, sine, w_all,
    y_ref, qkv, lse, att, ba, mid, pre, bb,
    sbuf, obuf, rbuf, wq, wo, wu, wd, wsem, ss, rs, ss2, rs2,
):
    x, ylo, z, yhi, c = here()
    places, me = row_group()
    entered = greet_row()
    start, wait = fetch(layer, w_all, wq, wo, wu, wd, wsem)
    for kind in range(4):
        start(kind)

    v = a_ref[...].astype(F32) + b_ref[...].astype(F32)
    hat, _ = normalize(v)
    normed = (hat * (1.0 + mod[1:2, :]) + mod[0:1, :]).astype(BF)
    cos_here, sin_here = cosine[...], sine[...]
    low = lanes((TOK, 128)) < 64
    wait(0)
    entered()
    last = nt(normed, wq[2048:2304, :])
    for t in range(4):
        got = nt(normed, wq[512 * t : 512 * (t + 1), :])
        q02, k02, v02, qk1 = (got[:, 128 * i : 128 * (i + 1)] for i in range(4))
        v1 = last[:, 128 * (t // 2) : 128 * (t // 2) + 128]
        if t % 2:
            v1 = swap(v1)
        for head, (q, k, w) in enumerate(
            (
                (q02, k02, v02),
                (jnp.where(low, qk1, q02), jnp.where(low, swap(qk1), k02), jnp.where(low, v1, v02)),
            )
        ):
            j = 2 * t + head
            sbuf[j, :, 0:128] = (turn(q, cos_here, sin_here).astype(BF).astype(F32) * 0.125).astype(BF)
            sbuf[j, :, 128:256] = turn(k, cos_here, sin_here).astype(BF)
            sbuf[j, :, 256:384] = w.astype(BF)
            deal(j, places[j][1], me, sbuf.at[j], qkv.at[me], ss, rs)
    for j, where in places:
        dealt(j, where, me, sbuf.at[j], qkv.at[j], ss, rs)

    keys = qkv[:, :, 128:256].reshape(SEQ, 128)
    values = qkv[:, :, 256:384].reshape(SEQ, 128)
    seg_keys = segr[...]

    def softmax(q, seg_q):
        scores = jnp.where(seg_q == seg_keys, nt(q, keys), -1e30)
        largest = jnp.max(scores, axis=-1, keepdims=True)
        raised = jnp.exp(scores - largest)
        total = jnp.sum(raised, axis=-1, keepdims=True)
        mixed = nn(raised.astype(BF), values) * (1.0 / total)
        return mixed, largest + jnp.log(total)

    def flat(column):
        wide = jnp.broadcast_to(column, (column.shape[0], 128))
        return jnp.transpose(wide)[0:8, :]

    for a in range(4):
        q = qkv[2 * a : 2 * a + 2, :, 0:128].reshape(256, 128)
        q = jnp.where(lanes((256, 128)) < 64, q, 0).astype(BF)
        mixed, total = softmax(q, segc[256 * a : 256 * (a + 1), :])
        q2 = jnp.where(low, 0, qkv[2 * a + c, :, 0:128]).astype(BF)
        mixed2, total2 = softmax(q2, segc[pl.ds(256 * a + TOK * c, TOK), :])
        lse[a, :, 0:256] = flat(total)
        lse[a, :, 256:384] = flat(total2)
        for b in range(2):
            j = 2 * a + b
            part = mixed[TOK * b : TOK * (b + 1)]
            obuf[j] = jnp.where(low | (c != b), part, mixed2).astype(BF)
            deal(j, places[j][1], me, obuf.at[j], rbuf.at[me], ss2, rs2)
    for j, where in places:
        dealt(j, where, me, obuf.at[j], rbuf.at[j], ss2, rs2)

    shared = []
    for t in range(4):
        first, second = rbuf[2 * t].astype(F32), rbuf[2 * t + 1].astype(F32)
        att[:, 128 * t : 128 * (t + 1)] = jnp.where(low, first, swap(second)).astype(BF)
        shared.append(rbuf[2 * t + c].astype(F32))
    att[:, 512:640] = jnp.where(low, swap(shared[0]), shared[1]).astype(BF)
    att[:, 640:768] = jnp.where(low, swap(shared[2]), shared[3]).astype(BF)
    wait(1)
    branch_a = nn(att[...], wo[...])
    ba[...] = branch_a
    middle = v + mod[2:3, :] * branch_a
    mid[...] = middle
    hat_b, _ = normalize(middle)
    normed_b = (hat_b * (1.0 + mod[4:5, :]) + mod[3:4, :]).astype(BF)
    wait(2)
    wait(3)
    total_b = jnp.zeros((TOK, D), F32)
    for t in range(4):
        before = nn(normed_b, wu[t])
        pre[:, D * t : D * (t + 1)] = before
        total_b = total_b + nn(jax.nn.gelu(before, approximate=True).astype(BF), wd[t])
    bb[...] = total_b
    y_ref[...] = (middle + mod[5:6, :] * total_b).astype(BF)


def forward(layer, a, b, mod, segc, segr, cosine, sine, w_all):
    dma = pltpu.SemaphoreType.DMA
    return pl.pallas_call(
        functools.partial(forward_kernel, layer),
        out_shape=(
            jax.ShapeDtypeStruct((TOK, D), BF),
            jax.ShapeDtypeStruct((8, TOK, 384), BF),
            jax.ShapeDtypeStruct((4, 8, 384), F32),
            jax.ShapeDtypeStruct((TOK, D), BF),
            jax.ShapeDtypeStruct((TOK, D), F32),
            jax.ShapeDtypeStruct((TOK, D), F32),
            jax.ShapeDtypeStruct((TOK, 4 * D), F32),
            jax.ShapeDtypeStruct((TOK, D), F32),
        ),
        in_specs=[VM] * 7 + [ANY],
        out_specs=(VM,) * 8,
        scratch_shapes=[
            pltpu.VMEM((8, TOK, 384), BF),
            pltpu.VMEM((8, TOK, 128), BF),
            pltpu.VMEM((8, TOK, 128), BF),
        ]
        + weight_scratch()
        + [dma((8,)), dma((8,)), dma((8,)), dma((8,))],
        compiler_params=pltpu.CompilerParams(
            collective_id=2 + layer, has_side_effects=True, vmem_limit_bytes=56 * 2**20
        ),
        name="forward",
    )(a, b, mod, segc, segr, cosine, sine, w_all)


def gelu_parts(u):
    k = 0.7978845608028654
    square = u * u
    th = jnp.tanh(k * u * (1.0 + 0.044715 * square))
    half = 0.5 * (1.0 + th)
    slope = half + 0.5 * u * (1.0 - th * th) * (k * (1.0 + 0.134145 * square))
    return u * half, slope


def backward_kernel(
    layer, a0, b0, a1, b1, dy0, dy1, mod, segc, segr, cosine, sine,
    qkv0, qkv1, lse0, lse1, att0, att1, ba0, ba1, mid0, mid1, pre0, pre1, bb0, bb1, w_all,
    din, dmod, na_o, at_o, nb_o, dba_o, dbb_o, act_o, dpre_o, dpj_o, dv1_o,
    na_p, at_p, nb_p, dba_p, dbb_p, act_p, dpre_p, dpj_p, dv1_p,
    sbuf, rbuf, sbig, rbig, dmid, dnb, k_own, k_sh, v_own, v_sh,
    wq, wo, wu, wd, wsem, ss, rs, ss2, rs2, xs, xr,
):
    x, ylo, z, yhi, c = here()
    places, me = row_group()
    partner = dev(x, ylo, z, yhi, 1 - c)
    entered = greet_row()
    start, wait = fetch(layer, w_all, wq, wo, wu, wd, wsem)
    for kind in (3, 2, 1, 0):
        start(kind)
    scale_a, gate_a = mod[1:2, :], mod[2:3, :]
    scale_b, gate_b = mod[4:5, :], mod[5:6, :]
    a_refs, b_refs, dys = (a0, a1), (b0, b1), (dy0, dy1)
    qkvs, lses, bas, mids, pres, bbs = (qkv0, qkv1), (lse0, lse1), (ba0, ba1), (mid0, mid1), (pre0, pre1), (bb0, bb1)
    low = lanes((TOK, 128)) < 64
    exchanged = []

    def hand(src, dst):
        n = len(exchanged)
        cp = push(src, dst, xs.at[n], xr.at[n], partner)
        cp.start()
        exchanged.append(cp)

    dgate_b = jnp.zeros((1, D), F32)
    for e in range(2):
        rows = slice(TOK * e, TOK * (e + 1))
        dy = dys[e][...]
        dgate_b = dgate_b + jnp.sum(dy * bbs[e][...], axis=0, keepdims=True)
        dbb_o[rows, :] = (gate_b * dy).astype(BF)
        hat_b, _ = normalize(mids[e][...])
        nb_o[rows, :] = (hat_b * (1.0 + scale_b) + mod[3:4, :]).astype(BF)
        hat_a, _ = normalize(a_refs[e][...].astype(F32) + b_refs[e][...].astype(F32))
        na_o[rows, :] = (hat_a * (1.0 + scale_a) + mod[0:1, :]).astype(BF)
        at_o[rows, :] = (att0, att1)[e][...]
    entered()
    hand(dbb_o, dbb_p)
    hand(nb_o, nb_p)
    hand(na_o, na_p)
    hand(at_o, at_p)

    wait(3)
    wait(2)
    for t in range(4):
        d_act = nt(dbb_o[...], wd[t])
        for e in range(2):
            rows = slice(TOK * e, TOK * (e + 1))
            act, slope = gelu_parts(pres[e][:, D * t : D * (t + 1)])
            act_o[t, rows, :] = act.astype(BF)
            dpre_o[t, rows, :] = (d_act[rows] * slope).astype(BF)
        more = nt(dpre_o[t], wu[t])
        dnb[...] = more if t == 0 else dnb[...] + more
    for h in range(2):
        hand(act_o.at[2 * h + 1 - c], act_p.at[h])
        hand(dpre_o.at[2 * h + 1 - c], dpre_p.at[h])

    dgate_a = jnp.zeros((1, D), F32)
    dscale_b = jnp.zeros((1, D), F32)
    dshift_b = jnp.zeros((1, D), F32)
    for e in range(2):
        rows = slice(TOK * e, TOK * (e + 1))
        hat_b, inv_b = normalize(mids[e][...])
        g = dnb[rows, :]
        dscale_b = dscale_b + jnp.sum(g * hat_b, axis=0, keepdims=True)
        dshift_b = dshift_b + jnp.sum(g, axis=0, keepdims=True)
        d_middle = dys[e][...] + norm_back(g * (1.0 + scale_b), hat_b, inv_b)
        dmid[rows, :] = d_middle
        dgate_a = dgate_a + jnp.sum(d_middle * bas[e][...], axis=0, keepdims=True)
        dba_o[rows, :] = (gate_a * d_middle).astype(BF)
    hand(dba_o, dba_p)
    wait(1)
    d_att = nt(dba_o[...], wo[...])
    for t in range(4):
        for e in range(2):
            rows = slice(TOK * e, TOK * (e + 1))
            own = d_att[rows, 128 * t : 128 * (t + 1)]
            extra = d_att[rows, 512 + 128 * (t // 2) : 640 + 128 * (t // 2)]
            if t % 2 == 0:
                extra = swap(extra)
            sbuf[2 * t, e] = jnp.where(low, own, extra).astype(BF)
            sbuf[2 * t + 1, e] = jnp.where(low, swap(own), extra).astype(BF)
        for b in range(2):
            j = 2 * t + b
            deal(j, places[j][1], me, sbuf.at[j], rbuf.at[me], ss, rs)
    for j, where in places:
        dealt(j, where, me, sbuf.at[j], rbuf.at[j], ss, rs)

    seg_keys = segc[...]
    wide = lanes((256, 128)) < 64
    for e in range(2):
        qkv, lse = qkvs[e], lses[e]
        for ref in (k_own, k_sh, v_own, v_sh):
            ref[...] = jnp.zeros_like(ref)

        def one(q, go, seg_q, total, k_sum, v_sum, qkv=qkv):
            keys = qkv[:, :, 128:256].reshape(SEQ, 128)
            values = qkv[:, :, 256:384].reshape(SEQ, 128)
            scores = jnp.where(seg_keys == seg_q, nt(keys, q), -1e30)
            p = jnp.exp(scores - total)
            d_p = nt(values, go)
            centre = jnp.sum(d_p * p, axis=0, keepdims=True)
            d_s = (p * (d_p - centre)).astype(BF)
            v_sum[...] += nn(p.astype(BF), go)
            k_sum[...] += nn(d_s, q)
            return tn(d_s, keys) * 0.125

        for a in range(4):
            q = qkv[2 * a : 2 * a + 2, :, 0:128].reshape(256, 128)
            go = rbuf[2 * a : 2 * a + 2, e].reshape(256, 128)
            dq = one(
                jnp.where(wide, q, 0).astype(BF),
                jnp.where(wide, go, 0).astype(BF),
                segr[0:1, 256 * a : 256 * (a + 1)],
                lse[a, 0:1, 0:256],
                k_own,
                v_own,
            )
            q2 = jnp.where(low, 0, qkv[2 * a + c, :, 0:128]).astype(BF)
            go2 = jnp.where(low, 0, rbuf[2 * a + c, e]).astype(BF)
            seg2 = jnp.where(
                c == 0,
                segr[0:1, 256 * a : 256 * a + 128],
                segr[0:1, 256 * a + 128 : 256 * a + 256],
            )
            dq2 = one(q2, go2, seg2, lse[a, 0:1, 256:384], k_sh, v_sh)
            for b in range(2):
                rows = slice(256 * a + TOK * b, 256 * a + TOK * (b + 1))
                whole = jnp.where(low, dq[TOK * b : TOK * (b + 1)], jnp.where(c == b, dq2, 0.0))
                sbig[2 * a + b, e, :, 0:128] = turn(whole, cosine[rows, :], -sine[rows, :]).astype(BF)
        for j in range(8):
            rows = slice(TOK * j, TOK * (j + 1))
            whole = jnp.where(low, k_own[rows, :], k_sh[rows, :])
            sbig[j, e, :, 128:256] = turn(whole, cosine[rows, :], -sine[rows, :]).astype(BF)
            sbig[j, e, :, 256:384] = jnp.where(low, v_own[rows, :], v_sh[rows, :]).astype(BF)
    for j, where in places:
        deal(j, where, me, sbig.at[j], rbig.at[me], ss2, rs2)
    for j, where in places:
        dealt(j, where, me, sbig.at[j], rbig.at[j], ss2, rs2)

    for e in range(2):
        rows = slice(TOK * e, TOK * (e + 1))
        ones = []
        for t in range(4):
            q0, k0, v0 = (rbig[2 * t, e, :, 128 * i : 128 * (i + 1)].astype(F32) for i in range(3))
            q1, k1, v1 = (rbig[2 * t + 1, e, :, 128 * i : 128 * (i + 1)].astype(F32) for i in range(3))
            dpj_o[t, rows, 0:128] = jnp.where(low, q0, q0 + q1).astype(BF)
            dpj_o[t, rows, 128:256] = jnp.where(low, k0, k0 + k1).astype(BF)
            dpj_o[t, rows, 256:384] = jnp.where(low, v0, v0 + v1).astype(BF)
            dpj_o[t, rows, 384:512] = jnp.where(low, q1, swap(k1)).astype(BF)
            ones.append(v1)
        dv1_o[rows, 0:128] = jnp.where(low, ones[0], swap(ones[1])).astype(BF)
        dv1_o[rows, 128:256] = jnp.where(low, ones[2], swap(ones[3])).astype(BF)
    for h in range(2):
        hand(dpj_o.at[2 * h + 1 - c], dpj_p.at[h])
    hand(dv1_o, dv1_p)
    wait(0)
    dna = nn(dv1_o[...], wq[2048:2304, :])
    for t in range(4):
        dna = dna + nn(dpj_o[t], wq[512 * t : 512 * (t + 1), :])
    dscale_a = jnp.zeros((1, D), F32)
    dshift_a = jnp.zeros((1, D), F32)
    for e in range(2):
        rows = slice(TOK * e, TOK * (e + 1))
        hat_a, inv_a = normalize(a_refs[e][...].astype(F32) + b_refs[e][...].astype(F32))
        g = dna[rows]
        dscale_a = dscale_a + jnp.sum(g * hat_a, axis=0, keepdims=True)
        dshift_a = dshift_a + jnp.sum(g, axis=0, keepdims=True)
        din[e] = dmid[rows, :] + norm_back(g * (1.0 + scale_a), hat_a, inv_a)
    for i, part in enumerate((dshift_a, dscale_a, dgate_a, dshift_b, dscale_b, dgate_b)):
        dmod[i : i + 1, :] = part
    dmod[6:8, :] = jnp.zeros((2, D), F32)
    for cp in exchanged:
        cp.wait_send()
        cp.wait_recv()


def backward(layer, *operands):
    dma = pltpu.SemaphoreType.DMA
    both = 2 * TOK

    def shape(*dims):
        return jax.ShapeDtypeStruct(dims, BF)

    own = [shape(both, D)] * 5 + [shape(4, both, D)] * 2 + [shape(4, both, 512), shape(both, 256)]
    got = [shape(both, D)] * 5 + [shape(2, both, D)] * 2 + [shape(2, both, 512), shape(both, 256)]
    outs = [
        jax.ShapeDtypeStruct((2, TOK, D), F32),
        jax.ShapeDtypeStruct((8, D), F32),
    ] + own + got
    return pl.pallas_call(
        functools.partial(backward_kernel, layer),
        out_shape=tuple(outs),
        in_specs=[VM] * 25 + [ANY],
        out_specs=(VM,) * len(outs),
        scratch_shapes=[
            pltpu.VMEM((8, 2, TOK, 128), BF),
            pltpu.VMEM((8, 2, TOK, 128), BF),
            pltpu.VMEM((8, 2, TOK, 384), BF),
            pltpu.VMEM((8, 2, TOK, 384), BF),
            pltpu.VMEM((both, D), F32),
            pltpu.VMEM((both, D), F32),
        ]
        + [pltpu.VMEM((SEQ, 128), F32)] * 4
        + weight_scratch()
        + [dma((8,)), dma((8,)), dma((8,)), dma((8,)), dma((12,)), dma((12,))],
        compiler_params=pltpu.CompilerParams(
            collective_id=4 + layer, has_side_effects=True, vmem_limit_bytes=60 * 2**20
        ),
        name="backward",
    )(*operands)


def weights_kernel(
    na_o, at_o, nb_o, dba_o, dbb_o, act_o, dpre_o, dpj_o, dv1_o,
    na_p, at_p, nb_p, dba_p, dbb_p, act_p, dpre_p, dpj_p, dv1_p,
    grads, tall,
):
    c = lax.axis_index("tensor") % 2
    tall[...] = (tn(dv1_o[...], na_o[...]) + tn(dv1_p[...], na_p[...])).astype(BF)
    for h in range(2):
        t = 2 * h + c
        grads[h, 0:512, :] = (tn(dpj_o[t], na_o[...]) + tn(dpj_p[h], na_p[...])).astype(BF)
        grads[h, 512:576, :] = tall[pl.ds(pl.multiple_of(64 * t, 64), 64), :]
    tall[...] = (tn(at_o[:, 512:768], dba_o[...]) + tn(at_p[:, 512:768], dba_p[...])).astype(BF)
    for h in range(2):
        t = 2 * h + c
        cols = pl.ds(pl.multiple_of(128 * t, 128), 128)
        grads[h, 576:704, :] = (tn(at_o[:, cols], dba_o[...]) + tn(at_p[:, cols], dba_p[...])).astype(BF)
        grads[h, 704:768, :] = tall[pl.ds(pl.multiple_of(64 * t, 64), 64), :]
        grads[h, 768:1536, :] = (tn(nb_o[...], dpre_o[t]) + tn(nb_p[...], dpre_p[h])).astype(BF)
        grads[h, 1536:2304, :] = (tn(act_o[t], dbb_o[...]) + tn(act_p[h], dbb_p[...])).astype(BF)


def weight_grads(*operands):
    return pl.pallas_call(
        weights_kernel,
        out_shape=jax.ShapeDtypeStruct((2, ROWS, D), BF),
        in_specs=[VM] * 18,
        out_specs=VM,
        scratch_shapes=[pltpu.VMEM((256, D), BF)],
        compiler_params=pltpu.CompilerParams(vmem_limit_bytes=56 * 2**20),
        name="weight_grads",
    )(*operands)


def reduce_kernel(
    g0, g1, ys, gs, out, y_out, g_out,
    own0, own1, own2, in0, in1, in2, sum0, sum1, sum2,
    mid0, mid1, mid2, tot0, tot1, tot2, end0, end1, end2, fin,
    osem, ss, rs, ss2, rs2, ss3, rs3, gss, grs, ys_s, ys_r, gs_s, gs_r, fsem,
):
    x, ylo, z, yhi, c = here()
    t = 2 * yhi + c
    dp = 2 * x + ylo
    y = 2 * yhi + ylo
    gl = (g0, g1)
    group = [(dp, (z + a) % 4, (t + b) % 4) for a in range(4) for b in range(4) if a or b]
    ymates = [dev(x, 1 - ylo, z, yhi, c), dev(x, 1 - ylo, z, 1 - yhi, c)]
    greet(group + [dev((x + o) % 4, ylo, z, yhi, c) for o in (1, 2, 3)] + ymates)()

    def xpeer(o):
        return dev((x + o) % 4, ylo, z, yhi, c), (x + o) % 4

    def zpeer(o):
        return dev(x, ylo, (z + o) % 4, yhi, c), (z + o) % 4

    def ypeer(o):
        to = (y + o) % 4
        return dev(x, to % 2, z, to // 2, c), to

    copies = []
    for l in range(2):
        copies.append(pltpu.make_async_copy(gl[l].at[:, x, :, 0], own0.at[l], osem.at[l]))
        copies.append(pltpu.make_async_copy(gl[l].at[:, :, z, 2], own2.at[l], osem.at[2 + l]))
        copies[-1].start()
        copies[-2].start()

        @pl.when(ylo == l)
        def _(l=l):
            pltpu.make_async_copy(gl[l].at[yhi, :, :, 1], own1, osem.at[4]).start()

    def first(o, begin):
        for l in range(2):
            where, to = xpeer(o)
            a = push(gl[l].at[:, to, :, 0], in0.at[o - 1, l], ss.at[0, o - 1, l], rs.at[0, o - 1, l], where)
            where, to = zpeer(o)
            b = push(gl[l].at[:, :, to, 2], in2.at[o - 1, l], ss.at[2, o - 1, l], rs.at[2, o - 1, l], where)
            where, to = ypeer(o)
            d = push(gl[l].at[to // 2, :, :, 1], in1.at[o - 1], ss.at[1, o - 1, 0], rs.at[1, o - 1, 0], where)
            if begin:
                a.start()
                b.start()

                @pl.when(to % 2 == l)
                def _():
                    d.start()
            else:
                a.wait()
                b.wait()
                if l == 0:
                    d.wait()

    for o in (2, 1, 3):
        first(o, True)

    def scatter(src, dst, s_sem, r_sem, begin):
        for s in range(4):
            mine = (z == s) & (t == z)

            @pl.when(jnp.logical_not(mine))
            def _(s=s):
                cp = push(src.at[s], dst.at[yhi, c], s_sem.at[s], r_sem.at[t], (dp, s, z))
                if begin:
                    cp.start()
                else:
                    cp.wait_send()

            @pl.when(mine)
            def _(s=s):
                cp = pltpu.make_async_copy(src.at[s], dst.at[yhi, c], s_sem.at[s])
                if begin:
                    cp.start()
                else:
                    cp.wait()

        if not begin:
            for b in range(4):

                @pl.when(jnp.logical_not((t == z) & (t == b)))
                def _(b=b):
                    spot = dst.at[b // 2, b % 2]
                    push(spot, spot, s_sem.at[b], r_sem.at[b], (dp, z, (t + 1) % 4)).wait_recv()

    scatter(ys, y_out, ys_s, ys_r, True)
    scatter(gs, g_out, gs_s, gs_r, True)

    for cp in copies:
        cp.wait()
    pltpu.make_async_copy(g0.at[yhi, :, :, 1], own1, osem.at[4]).wait()
    for o in (2, 1, 3):
        first(o, False)

    def add(dst, refs, count):
        def body(i, carry):
            total = refs[0](i).astype(F32)
            for ref in refs[1:]:
                total = total + ref(i).astype(F32)
            dst(i, total)
            return carry

        lax.fori_loop(0, count, body, 0)

    def at0(ref):
        return lambda i: ref[i // 8, (i // 4) % 2, i % 4]

    def put(ref, split):
        def store(i, total):
            ref[split(i)] = total.astype(BF)

        return store

    add(
        put(sum0, lambda i: (i // 8, (i // 4) % 2, i % 4)),
        [at0(own0), at0(in0.at[0]), at0(in0.at[1]), at0(in0.at[2])],
        16,
    )
    add(
        put(sum1, lambda i: (i // 4, i % 4)),
        [(lambda i, r=r: r[i // 4, i % 4]) for r in (own1, in1.at[0], in1.at[1], in1.at[2])],
        16,
    )
    add(
        put(sum2, lambda i: (i // 8, (i // 4) % 2, i % 4)),
        [at0(own2), at0(in2.at[0]), at0(in2.at[1]), at0(in2.at[2])],
        16,
    )

    def second(o):
        where, to = ypeer(o)
        a = push(sum0.at[to % 2, to // 2], mid0.at[o - 1], ss2.at[0, o - 1], rs2.at[0, o - 1], where)
        where, to = zpeer(o)
        b = push(sum1.at[:, to], mid1.at[o - 1], ss2.at[1, o - 1], rs2.at[1, o - 1], where)
        where, to = xpeer(o)
        d = push(sum2.at[:, :, to], mid2.at[o - 1], ss2.at[2, o - 1], rs2.at[2, o - 1], where)
        return a, b, d

    moved = [cp for o in (2, 1, 3) for cp in second(o)]
    for cp in moved:
        cp.start()
    for cp in moved:
        cp.wait()
    add(
        put(tot0, lambda i: i),
        [lambda i: sum0[ylo, yhi, i]] + [(lambda i, r=mid0.at[n]: r[i]) for n in range(3)],
        4,
    )
    add(
        put(tot1, lambda i: i),
        [lambda i: sum1[i, z]] + [(lambda i, r=mid1.at[n]: r[i]) for n in range(3)],
        4,
    )
    add(
        put(tot2, lambda i: (i // 2, i % 2)),
        [lambda i: sum2[i // 2, i % 2, x]] + [(lambda i, r=mid2.at[n]: r[i // 2, i % 2]) for n in range(3)],
        4,
    )

    def third(o):
        where, to = zpeer(o)
        a = push(tot0.at[to], end0.at[o - 1], ss3.at[0, o - 1], rs3.at[0, o - 1], where)
        where, to = xpeer(o)
        b = push(tot1.at[to], end1.at[o - 1], ss3.at[1, o - 1], rs3.at[1, o - 1], where)
        where, to = ypeer(o)
        d = push(tot2.at[to % 2, to // 2], end2.at[o - 1], ss3.at[2, o - 1], rs3.at[2, o - 1], where)
        return a, b, d

    moved = [cp for o in (2, 1, 3) for cp in third(o)]
    for cp in moved:
        cp.start()
    for cp in moved:
        cp.wait()
    for p, (last, ends) in enumerate(((tot0[z], end0), (tot1[x], end1), (tot2[ylo, yhi], end2))):
        total = last.astype(F32)
        for n in range(3):
            total = total + ends[n].astype(F32)
        fin[p] = total.astype(BF)
    cp = pltpu.make_async_copy(fin, out.at[ylo, x, z], fsem.at[0])
    cp.start()
    cp.wait()
    spread(out, gss, grs)
    scatter(ys, y_out, ys_s, ys_r, False)
    scatter(gs, g_out, gs_s, gs_r, False)


def reduce_all(g0, g1, ys, gs):
    dma = pltpu.SemaphoreType.DMA

    def buf(*dims):
        return pltpu.VMEM(dims + (48, D), BF)

    return pl.pallas_call(
        reduce_kernel,
        out_shape=(
            jax.ShapeDtypeStruct((2, 4, 4, 3, 48, D), BF),
            jax.ShapeDtypeStruct((2, 2, TOK, D), BF),
            jax.ShapeDtypeStruct((2, 2, TOK, D), BF),
        ),
        in_specs=[ANY] * 4,
        out_specs=(ANY,) * 3,
        scratch_shapes=[
            buf(2, 2, 4),
            buf(4, 4),
            buf(2, 2, 4),
            buf(3, 2, 2, 4),
            buf(3, 4, 4),
            buf(3, 2, 2, 4),
            buf(2, 2, 4),
            buf(4, 4),
            buf(2, 2, 4),
            buf(3, 4),
            buf(3, 4),
            buf(3, 2, 2),
            buf(4),
            buf(4),
            buf(2, 2),
            buf(3),
            buf(3),
            buf(3),
            buf(3),
            dma((5,)),
            dma((3, 3, 2)),
            dma((3, 3, 2)),
            dma((3, 3)),
            dma((3, 3)),
            dma((3, 3)),
            dma((3, 3)),
            dma((27,)),
            dma((27,)),
            dma((4,)),
            dma((4,)),
            dma((4,)),
            dma((4,)),
            dma((1,)),
        ],
        compiler_params=pltpu.CompilerParams(
            collective_id=6, has_side_effects=True, vmem_limit_bytes=50 * 2**20
        ),
        name="reduce_all",
    )(g0, g1, ys, gs)


def rotary(count):
    frequency = np.exp(-np.log(10000.0) * np.arange(32) / 32)
    angles = np.arange(count)[:, None] * frequency[None, :]
    cos, sin = np.cos(angles), np.sin(angles)
    return (
        np.concatenate([cos] * 4, axis=1).astype(np.float32),
        np.concatenate([-sin, sin, -sin, sin], axis=1).astype(np.float32),
    )


def time_features(step_values, feature_count):
    half_count = feature_count // 2
    frequency = jnp.exp(-np.log(10000.0) * jnp.arange(half_count, dtype=F32) / half_count)
    angles = step_values.astype(F32)[:, None] * frequency[None, :]
    return jnp.concatenate([jnp.cos(angles), jnp.sin(angles)], axis=1)


def on_device(hidden_in, segments, timestep, w_qkv, w_out, w_up, w_down, w_mod, b_mod, cotangent):
    x, ylo, z, yhi, c = here()
    tall = jnp.swapaxes(w_qkv, 1, 2).reshape(2, 9, 64, D)
    tall = jnp.concatenate([tall[:, g] for g in PACK], axis=1)
    wloc = jnp.concatenate([tall, w_out, w_up, w_down], axis=1).reshape(2, 4, 4, 3, 48, D)
    x0, cots, w_all = prepare(
        hidden_in.reshape(2, 2, TOK, D), cotangent.reshape(2, 2, TOK, D), wloc
    )
    w_all = w_all.reshape(4, 2, ROWS, D)

    features = time_features(timestep, w_mod.shape[1])
    mine = lax.dynamic_slice_in_dim(features, yhi, 1, 0)
    modulation = jnp.einsum(
        "rf,lfm->lrm", mine, w_mod.astype(F32), precision=highest
    ) + b_mod.astype(F32)[:, None, :]
    modulation = modulation.reshape(2, 6, D)
    mods = (modulation[0], modulation[1])
    seg = lax.dynamic_slice_in_dim(segments, yhi, 1, 0)
    segc, segr = seg.reshape(SEQ, 1), seg
    cosine, sine = (jnp.asarray(v) for v in rotary(SEQ))
    place = (2 * z + c) * TOK
    cos_here = lax.dynamic_slice_in_dim(cosine, place, TOK, 0)
    sin_here = lax.dynamic_slice_in_dim(sine, place, TOK, 0)

    none = jnp.zeros_like(x0)
    ins, kept, ys = [], [], []
    for s in range(4):
        a = x0 if s == 0 else ys[-1]
        b = x0 if s == 2 else none
        y, *saved = forward(s % 2, a, b, mods[s % 2], segc, segr, cos_here, sin_here, w_all)
        ins.append((a, b))
        kept.append(saved)
        ys.append(y)

    def stage(layer, dy0, dy1):
        e0, e1 = layer, layer + 2
        pairs = [item for pair in zip(kept[e0], kept[e1]) for item in pair]
        return backward(
            layer, *ins[e0], *ins[e1], dy0, dy1, mods[layer], segc, segr, cosine, sine, *pairs, w_all
        )

    din1, dmod1, *parts1 = stage(1, cots[1].astype(F32), cots[3].astype(F32))
    din0, dmod0, *parts0 = stage(
        0, cots[0].astype(F32) + din1[0], cots[2].astype(F32) + din1[1]
    )
    units = (2, 4, 4, 3, 48, D)
    g1 = weight_grads(*parts1).reshape(units)
    g0 = weight_grads(*parts0).reshape(units)

    d_mod = jnp.stack([dmod0[:6].reshape(-1), dmod1[:6].reshape(-1)])
    d_rows = jnp.where((jnp.arange(2) == yhi)[:, None, None], d_mod[None], 0.0)
    d_rows = lax.psum(d_rows, ("section", "tensor"))
    sent = jnp.concatenate([d_rows.reshape(2, -1), features], axis=1)
    sent = lax.all_gather(sent, "dp", axis=0, tiled=True)
    d_all, features_all = sent[:, : 2 * 6 * D].reshape(-1, 2, 6 * D), sent[:, 2 * 6 * D :]
    grad_mod = jnp.einsum("rf,rlm->lfm", features_all, d_all, precision=highest)
    grad_bias = jnp.sum(d_all, axis=0)

    y_all = jnp.stack(ys)
    d_ins = jnp.stack([din0[0], din1[0], din0[1], din1[1]]).astype(BF)
    out, y_out, g_out = reduce_all(g0, g1, y_all, d_ins)
    out = out.reshape(2, ROWS, D)
    groups = out[:, :576].reshape(2, 9, 64, D)
    grad_qkv = jnp.concatenate([groups[:, g] for g in UNPACK], axis=1).swapaxes(1, 2)
    return (
        y_out.reshape(1, 2, 2 * TOK, D),
        g_out.reshape(1, 2, 2 * TOK, D).astype(F32),
        grad_qkv.astype(F32),
        out[:, 576:768].astype(F32),
        out[:, 768:1536].astype(F32),
        out[:, 1536:2304].astype(F32),
        grad_mod,
        grad_bias,
    )


def solution(mesh):
    placed = (
        P("dp", "tensor", None),
        P("dp", None),
        P("dp"),
        P(None, None, "tensor"),
        P(None, "tensor", None),
        P(None, None, "tensor"),
        P(None, "tensor", None),
        P(),
        P(),
        P("section", "dp", "tensor", None),
    )
    return jax.shard_map(
        on_device,
        mesh=mesh,
        in_specs=placed,
        out_specs=(
            P("section", "dp", "tensor", None),
            P("section", "dp", "tensor", None),
            P(None, None, "tensor"),
            P(None, "tensor", None),
            P(None, None, "tensor"),
            P(None, "tensor", None),
            P(),
            P(),
        ),
        check_vma=False,
    )
```

time: 1960 us -> 775 us (0.40)
  waiting for transfers between devices: 974 us -> 0.02 us
  Pallas kernels: 0 us -> 653 us
  matrix products: 247 us -> 10.2 us
  local copies, waits for them, and re-layouts: 257 us -> 38.9 us
  other arithmetic: 235 us -> 18.9 us
  blocking collectives: 172 us -> 29.2 us
  starting transfers between devices: 23.7 us -> 0.04 us
  loops' own time: 20.1 us -> 0 us
    pallas_call x0 -> x10, Pallas kernels: none -> 653 us  [the longest x1 220 us: prepare(): pl.pallas_call(prepare_kernel, out_shape=(jax.ShapeDtypeStruct((TOK, D),...]
    reduce_scatter x16 -> x0, waiting for transfers between devices: 412 us -> none  [the longest x5 155 us: forward_one(): lax.psum_scatter(jnp.dot(mixed_heads, wout_own, preferred_element_type=jn...]
    all_gather x16 -> x0, waiting for transfers between devices: 312 us -> none  [the longest x5 103 us: forward_one(): gathered_a = lax.all_gather(scaled_a, 'tensor', axis=0, tiled=True)]
    dot_general x88 -> x2, matrix products: 247 us -> 10.2 us  [the longest x1 9.17 us: on_device(): grad_mod = jnp.einsum('rf,rlm->lfm', features_all, d_all, precision=highest)]
    psum x1, waiting for transfers between devices: 194 us -> 0.01 us  [on_device(): d_rows = lax.psum(d_rows, ('section', 'tensor'))]
    psum x2 -> x0, blocking collectives: 172 us -> none  [the longest x1 156 us: on_device(): lax.psum(slotted(grad_bias).astype(jnp.bfloat16), ('dp', 'section'))]
    dynamic_slice x78 -> x2, local copies, waits for them, and re-layouts: 111 us -> 2.97 us  [the longest x1 1.53 us: on_device(): sin_here = lax.dynamic_slice_in_dim(sine, place, TOK, 0)]
    dynamic_update_slice x67 -> x0, other arithmetic: 93.9 us -> none  [the longest x57 93.7 us: put_row(): return lax.dynamic_update_index_in_dim(buffer, merged, position, 0)]
  transfers between devices with their start and end apart: 41 -> 1, of which waited for: 41 -> 0; matrix products, arithmetic and copies ran while one was open for 11% -> 2% of each run, Pallas kernels for 0% -> 25%
where the time goes in v1:
time: 775 us; the launch traced here: 765 us
  Pallas kernels  653 us (84%)
  local copies, waits for them, and re-layouts  38.9 us (5%)
  blocking collectives  29.2 us (4%)
  other arithmetic  18.9 us (2%)
  between operations  14.9 us (2%)
  matrix products  10.2 us (1%)
    pallas_call x1, Pallas kernels, prepare(): pl.pallas_call(prepare_kernel, out_shape=(jax.ShapeDtypeStruct((TOK, D),...  220 us
    pallas_call x1, Pallas kernels, reduce_all(): pl.pallas_call(reduce_kernel, out_shape=(jax.ShapeDtypeStruct((2, 4, 4, 3...  170 us
    pallas_call x4, Pallas kernels, forward(): pl.pallas_call(functools.partial(forward_kernel, layer), out_shape=(jax.S...  121 us
    pallas_call x2, Pallas kernels, backward(): pl.pallas_call(functools.partial(backward_kernel, layer), out_shape=tuple...  120 us
    all_gather x1, blocking collectives, on_device(): sent = lax.all_gather(sent, 'dp', axis=0, tiled=True)  29.2 us
    unnamed x53, local copies, waits for them, and re-layouts  27.3 us
    pallas_call x2, Pallas kernels, weight_grads(): pl.pallas_call(weights_kernel, out_shape=jax.ShapeDtypeStruct((2, ROWS, D...  22 us
  transfers between devices with their start and end apart: 1, of which 0 were waited for; matrix products, arithmetic and copies ran while one was open for 2% of the time, Pallas kernels for 25%

profile of v1, /device:TPU:16, one launch (start us, length us, event | category | flops | bytes accessed | tf_op | source)
XLA Modules:
  0.0 765.5 jit_solution(3420222779201009165)
XLA Ops:
  13.7 1.8 fusion.19
  17.1 1.6 fusion.17
  18.7 1.6 fusion.16
  20.3 1.6 fusion.15
  21.9 1.6 fusion.14
  23.6 1.6 fusion.13
  33.4 220.5 %prepare.1 = (bf16[128,768]{1,0:T(8,128)(2,1)}, bf16[4,128,768]{2,1,0:T(8,128)(2,1)}, bf16[4,2,4,4,3,48,768]{6,5,4,3,2,1,0:T(8,128)(2,1)}) custom-call(bf16[2,2,128,768]{3,2,1,0:T(8,128)(2,1)} %bitcast.186, bf16[2,2,128,768]{3,2,1,0:T(8,128)(2,1)} %bitcast.187, bf16[2,4,4,3,48,768]{5,4,3,2,1,0:T(8,128)(2,1)} %bitcast.14.wloc), custom_call_target="tpu_custom_call" | custom-call | tf_op jit(solution)/shard_map/prepare/pallas_call | solution.py:232
  253.8 2.0 bitcast_convert_fusion
  258.0 38.5 %forward.4 = (bf16[128,768]{1,0:T(8,128)(2,1)}, bf16[8,128,384]{2,1,0:T(8,128)(2,1)}, f32[4,8,384]{2,1,0:T(8,128)}, bf16[128,768]{1,0:T(8,128)(2,1)}, f32[128,76...) custom-call(bf16[128,768]{1,0:T(8,128)(2,1)} %get-tuple-element.86.a_ref.b_ref.a0.b1, ...), custom_call_target="tpu_custom_call" | custom-call | tf_op jit(solution)/shard_map/forward/pallas_call | solution.py:433
  296.5 27.6 %forward.5 = (bf16[128,768]{1,0:T(8,128)(2,1)}, bf16[8,128,384]{2,1,0:T(8,128)(2,1)}, f32[4,8,384]{2,1,0:T(8,128)}, bf16[128,768]{1,0:T(8,128)(2,1)}, f32[128,76...) custom-call(bf16[128,768]{1,0:T(8,128)(2,1)} %get-tuple-element.88.a_ref.a0, ...), custom_call_target="tpu_custom_call" | custom-call | tf_op jit(solution)/shard_map/forward/pallas_call | solution.py:433
  324.1 27.6 %forward.6 = (bf16[128,768]{1,0:T(8,128)(2,1)}, bf16[8,128,384]{2,1,0:T(8,128)(2,1)}, f32[4,8,384]{2,1,0:T(8,128)}, bf16[128,768]{1,0:T(8,128)(2,1)}, f32[128,76...) custom-call(bf16[128,768]{1,0:T(8,128)(2,1)} %get-tuple-element.89.a_ref.a1, ...), custom_call_target="tpu_custom_call" | custom-call | tf_op jit(solution)/shard_map/forward/pallas_call | solution.py:433
  351.7 27.0 %forward.7 = (bf16[128,768]{1,0:T(8,128)(2,1)}, bf16[8,128,384]{2,1,0:T(8,128)(2,1)}, f32[4,8,384]{2,1,0:T(8,128)}, bf16[128,768]{1,0:T(8,128)(2,1)}, f32[128,76...) custom-call(bf16[128,768]{1,0:T(8,128)(2,1)} %get-tuple-element.91.a_ref.a1, ...), custom_call_target="tpu_custom_call" | custom-call | tf_op jit(solution)/shard_map/forward/pallas_call | solution.py:433
  378.7 60.5 %backward.2 = (f32[2,128,768]{2,1,0:T(8,128)}, f32[8,768]{1,0:T(8,128)}, bf16[256,768]{1,0:T(8,128)(2,1)}, bf16[256,768]{1,0:T(8,128)(2,1)}, bf16[256,768]{1,0:T...) custom-call(bf16[128,768]{1,0:T(8,128)(2,1)} %get-tuple-element.88.a, ...), custom_call_target="tpu_custom_call" | custom-call | tf_op jit(solution)/shard_map/backward/pallas_call | solution.py:663
  439.2 2.1 add_bitcast_fusion
  441.3 59.7 %backward.3 = (f32[2,128,768]{2,1,0:T(8,128)}, f32[8,768]{1,0:T(8,128)}, bf16[256,768]{1,0:T(8,128)(2,1)}, bf16[256,768]{1,0:T(8,128)(2,1)}, bf16[256,768]{1,0:T...) custom-call(bf16[128,768]{1,0:T(8,128)(2,1)} %get-tuple-element.86.a, ...), custom_call_target="tpu_custom_call" | custom-call | tf_op jit(solution)/shard_map/backward/pallas_call | solution.py:663
  504.3 10.9 %weight_grads.3 = bf16[2,2304,768]{2,1,0:T(8,128)(2,1)} custom-call(bf16[256,768]{1,0:T(8,128)(2,1)} %get-tuple-element.139.na_o, bf16[256,768]{1,0:T(8,128)(2,1)} %get-tuple-element.140.at_o, bf16[256,768]{1,0:T(8,128)(2,1)} %get-tuple-element.141.nb_o, bf16[256,768]{1,0:T(8,128)(2,1)} %get-tuple-element.142.dba_o, ...), custom_call_target="tpu_custom_call" | custom-call | tf_op jit(solution)/shard_map/weight_grads/pallas_call | solution.py:708
  515.2 11.0 %weight_grads.2 = bf16[2,2304,768]{2,1,0:T(8,128)(2,1)} custom-call(bf16[256,768]{1,0:T(8,128)(2,1)} %get-tuple-element.121.na_o, bf16[256,768]{1,0:T(8,128)(2,1)} %get-tuple-element.122.at_o, bf16[256,768]{1,0:T(8,128)(2,1)} %get-tuple-element.123.nb_o, bf16[256,768]{1,0:T(8,128)(2,1)} %get-tuple-element.124.dba_o, ...), custom_call_target="tpu_custom_call" | custom-call | tf_op jit(solution)/shard_map/weight_grads/pallas_call | solution.py:708
  526.2 170.2 %reduce_all.1 = (bf16[2,4,4,3,48,768]{5,4,3,2,1,0:T(8,128)(2,1)}, bf16[2,2,128,768]{3,2,1,0:T(8,128)(2,1)S(1)}, bf16[2,2,128,768]{3,2,1,0:T(8,128)(2,1)S(1)}) custom-call(bf16[2,4,4,3,48,768]{5,4,3,2,1,0:T(8,128)(2,1)} %bitcast.160, bf16[2,4,4,3,48,768]{5,4,3,2,1,0:T(8,128)(2,1)} %bitcast.159, bf16[4,128,768]{2,1,0:T(8,128)(2,1)S(1)} %pad_maximum_fusion.ys, ...), custom_call_target="tpu_custom_call" | custom-call | tf_op jit(solution)/shard_map/reduce_all/pallas_call | solution.py:914
  698.0 6.9 slice_convert_fusion
  705.1 2.1 convert_bitcast_fusion
  707.2 2.2 slice_convert_fusion.2
  711.6 29.2 %all-gather = f32[8,2,9344]{2,1,0:T(2,128)S(1)} all-gather(f32[1,2,9344]{2,1,0:T(2,128)S(1)} %bitcast.188), channel_id=1, replica_groups=mesh['dp'=8,'section'=4,'tensor'=4] {'dp'}, dimensions={0}, use_global_device_ids=true | all-gather | bytes 672768 | tf_op jit(solution)/shard_map/all_gather | solution.py:1035
  741.9 9.2 %convolution_bitcast_fusion = f32[2,128,4608]{1,2,0:T(8,128)} fusion(f32[2,2,8,4608]{3,2,1,0:T(8,128)S(1)} %bitcast.173, f32[16,9344]{1,0:T(8,128)S(1)} %reshape.123), kind=kOutput, calls=%fused_computation | convolution fusion | flops 226492416 | bytes 5316608 | tf_op jit(solution)/shard_map/rf,rlm->lfm/dot_general | solution.py:1037
  751.1 6.2 copy.64
  (78 shorter events, 27.6 us)
Async XLA Ops:
  7.2 3.1 copy-start
  7.2 4.1 copy-start.12
  7.2 703.4 %all-reduce.2.cloned.1.call-start = ((), (), s32[]{:S(2)}) async-start(), calls=%async_computation | async-start | bytes 147456 | tf_op jit(solution)/shard_map/psum | solution.py:1033
  11.3 17.1 %copy-start.9 = (bf16[2,192,768]{2,1,0:T(8,128)(2,1)S(1)}, bf16[2,192,768]{2,1,0:T(8,128)(2,1)}, u32[]{:S(2)}) copy-start(bf16[2,192,768]{2,1,0:T(8,128)(2,1)} %param.16) | copy-start | bytes 1769476
  13.7 15.6 %copy-start.2 = (bf16[2,768,768]{2,1,0:T(8,128)(2,1)S(1)}, bf16[2,768,768]{2,1,0:T(8,128)(2,1)}, u32[]{:S(2)}) copy-start(bf16[2,768,768]{2,1,0:T(8,128)(2,1)} %param.17) | copy-start | bytes 7077892
  29.3 2.5 copy-start.3
  378.7 60.5 %copy-start.8 = (bf16[4,128,768]{2,1,0:T(8,128)(2,1)S(1)}, bf16[4,128,768]{2,1,0:T(8,128)(2,1)}, u32[]{:S(2)}) copy-start(bf16[4,128,768]{2,1,0:T(8,128)(2,1)} %get-tuple-element.90) | copy-start | bytes 2359300
  441.3 60.5 %copy-start.11 = (f32[8,768]{1,0:T(8,128)S(1)}, f32[8,768]{1,0:T(8,128)}, u32[]{:S(2)}) copy-start(f32[8,768]{1,0:T(8,128)} %get-tuple-element.163) | copy-start | bytes 73732
  441.3 61.4 %copy-start.7 = (f32[2,128,768]{2,1,0:T(8,128)S(1)}, f32[2,128,768]{2,1,0:T(8,128)}, u32[]{:S(2)}) copy-start(f32[2,128,768]{2,1,0:T(8,128)} %get-tuple-element.106) | copy-start | bytes 2359300
  501.0 3.0 copy-start.4
  501.0 3.0 copy-start.5
  501.0 3.0 copy-start.6
  501.0 3.0 copy-start.10
  751.1 7.1 copy-start.1
Sparse Core Ops, SparseCore 0:
  502.8 126.0 all-reduce.1

commit v2 on v1

v2 whole, which is shorter than its diff:
```python
import functools

import jax
import jax.numpy as jnp
import numpy as np
from jax import lax
from jax.experimental import pallas as pl
from jax.experimental.pallas import tpu as pltpu
from jax.sharding import PartitionSpec as P

MESH = pl.DeviceIdType.MESH
BF = jnp.bfloat16
F32 = jnp.float32
highest = lax.Precision.HIGHEST
EPS = 1e-06
D = 768
TOK = 128
SEQ = 1024
ANY = pl.BlockSpec(memory_space=pl.ANY)
VM = pl.BlockSpec(memory_space=pltpu.VMEM)
HALF = 384
ATTN = (4, 4, 3, 16, D)
MLP = (4, 4, 3, 32, D)
UNIT = (4, 4, 3, 48, D)


def here():
    dp = lax.axis_index("dp")
    t = lax.axis_index("tensor")
    return dp // 2, dp % 2, lax.axis_index("section"), t // 2, t % 2


def dev(x, ylo, z, yhi, c):
    return (2 * x + ylo, z, 2 * yhi + c)


def push(src, dst, send_sem, recv_sem, where):
    return pltpu.make_async_remote_copy(
        src_ref=src,
        dst_ref=dst,
        send_sem=send_sem,
        recv_sem=recv_sem,
        device_id=where,
        device_id_type=MESH,
    )


def greet(devices):
    barrier = pltpu.get_barrier_semaphore()
    for where in devices:
        pl.semaphore_signal(barrier, inc=1, device_id=where, device_id_type=MESH)
    return lambda: pl.semaphore_wait(barrier, len(devices))


def nn(a, b):
    return lax.dot_general(a, b, (((1,), (0,)), ((), ())), preferred_element_type=F32)


def nt(a, b):
    return lax.dot_general(a, b, (((1,), (1,)), ((), ())), preferred_element_type=F32)


def tn(a, b):
    return lax.dot_general(a, b, (((0,), (0,)), ((), ())), preferred_element_type=F32)


def normalize(values):
    centred = values - jnp.mean(values, axis=-1, keepdims=True)
    inverse = lax.rsqrt(jnp.mean(centred * centred, axis=-1, keepdims=True) + EPS)
    return centred * inverse, inverse


def norm_back(gradient, normed, inverse):
    return inverse * (
        gradient
        - jnp.mean(gradient, axis=-1, keepdims=True)
        - normed * jnp.mean(gradient * normed, axis=-1, keepdims=True)
    )


def lanes(shape):
    return lax.broadcasted_iota(jnp.int32, shape, len(shape) - 1)


def swap(x):
    return pltpu.roll(x, 64, 1)


def turn(x, cosine, sine):
    low = (lanes(x.shape) % 64) < 32
    other = jnp.where(low, pltpu.roll(x, 96, 1), pltpu.roll(x, 32, 1))
    return x * cosine + other * sine


def half(ylo):
    return pl.ds(pl.multiple_of(HALF * ylo, 128), HALF)


class Spread:
    orders = ("zyx", "xzy", "yxz")

    def __init__(self, buf, ss, rs):
        self.buf, self.ss, self.rs = buf, ss, rs
        self.running = None

    def at(self, dims, part, by):
        x, ylo, z, yhi, c = here()
        everything = slice(None)
        i = everything if "x" in dims else by.get("x", x)
        j = everything if "z" in dims else by.get("z", z)
        k = everything if "y" in dims else half(by.get("y", ylo))
        return self.buf.at[i, j, part, :, k]

    def peer(self, dim, o):
        x, ylo, z, yhi, c = here()
        if dim == "y":
            return dev(x, 1 - ylo, z, yhi, c), 1 - ylo
        if dim == "x":
            return dev((x + o) % 4, ylo, z, yhi, c), (x - o + 4) % 4
        return dev(x, ylo, (z + o) % 4, yhi, c), (z - o + 4) % 4

    def start(self, phase):
        sent, got = [], []
        for part in range(3):
            dim, done = self.orders[part][phase], self.orders[part][:phase]
            for o in (1,) if dim == "y" else (2, 1, 3):
                where, origin = self.peer(dim, o)
                n = (phase * 3 + part) * 3 + o - 1
                here_now = self.at(done, part, {})
                cp = push(here_now, here_now, self.ss.at[n], self.rs.at[n], where)
                cp.start()
                sent.append(cp)
                back = self.at(done, part, {dim: origin})
                got.append((push(back, back, self.ss.at[n], self.rs.at[n], where), back))
        self.running = sent, got

    def finish(self, each=None):
        sent, got = self.running
        for cp, back in got:
            cp.wait_recv()
            if each is not None:
                each(back)
        for cp in sent:
            cp.wait_send()

    def held(self):
        return [self.at(self.orders[p][:2], p, {}) for p in range(3)]


class Gather:
    def __init__(self, wv, pieces, ss, rs, ps, pr, ls):
        x, ylo, z, yhi, c = here()
        self.wv, self.pieces = wv, pieces
        self.ps, self.pr, self.ls = ps, pr, ls
        self.t = 2 * yhi + c
        self.other = 2 * (1 - yhi) + c
        self.partner = dev(x, ylo, z, yhi, 1 - c)
        self.cross = dev(x, 1 - ylo, z, 1 - yhi, c)
        self.spread = Spread(wv.at[self.other], ss, rs)
        self.handed = []

    def side(self, n):
        ref, first = self.pieces[n]
        spot = self.wv.at[self.t, pl.ds(first, ref.shape[0])]
        return (
            pltpu.make_async_copy(ref, spot, self.ls.at[n]),
            push(ref, spot, self.ps.at[n], self.pr.at[n], self.partner),
        )

    def s0(self):
        x, ylo, z, yhi, c = here()
        for ref, first in self.pieces:

            @pl.when((x >= first) & (x < first + ref.shape[0]))
            def _(ref=ref, first=first):
                push(
                    ref.at[x - first, z, :, :, half(1 - ylo)],
                    self.wv.at[self.t, x, z, :, :, half(1 - ylo)],
                    self.ps.at[2],
                    self.pr.at[2],
                    self.cross,
                ).start()

        for n in range(len(self.pieces)):
            for cp in self.side(n):
                cp.start()

    def s1(self):
        x, ylo, z, yhi, c = here()
        landed = self.wv.at[self.other, x, z, :, :, half(ylo)]
        cp = push(landed, landed, self.ps.at[2], self.pr.at[2], self.cross)
        cp.wait_recv()
        cp.wait_send()
        self.spread.start(0)

    def s2(self):
        self.spread.finish()
        self.spread.start(1)

    def hand(self, ref):
        n = 3 + len(self.handed)
        cp = push(ref, ref, self.ps.at[n], self.pr.at[n], self.partner)
        cp.start()
        self.handed.append(cp)

    def s3(self):
        self.spread.finish()
        self.spread.start(2)
        for ref in self.spread.held():
            self.hand(ref)

    def s4(self):
        self.spread.finish(self.hand)

    def s5(self):
        for n in range(len(self.pieces)):
            local, cp = self.side(n)
            local.wait()
            cp.wait_send()
            cp.wait_recv()
        for cp in self.handed:
            cp.wait_send()
            cp.wait_recv()


def gather_scratch():
    dma = pltpu.SemaphoreType.DMA
    return [dma((27,)), dma((27,)), dma((13,)), dma((13,)), dma((2,))]


def chips_around():
    x, ylo, z, yhi, c = here()
    return [dev((x + o) % 4, ylo, z, yhi, c) for o in (1, 2, 3)] + [
        dev(x, 1 - ylo, z, yhi, c),
        dev(x, 1 - ylo, z, 1 - yhi, c),
    ]


def dp_group():
    x, ylo, z, yhi, c = here()
    t = 2 * yhi + c
    return [(2 * x + ylo, (z + a) % 4, (t + b) % 4) for a in range(4) for b in range(4) if a or b]


def row_places():
    x, ylo, z, yhi, c = here()
    return [(2 * a + b, dev(x, ylo, a, yhi, b)) for a in range(4) for b in range(2)], 2 * z + c


def row_mates():
    x, ylo, z, yhi, c = here()
    me = 2 * z + c
    return [dev(x, ylo, ((me + o) % 8) // 2, yhi, (me + o) % 2) for o in range(1, 8)]


def deal(j, where, me, src, dst, s, r):
    @pl.when(me != j)
    def _():
        push(src, dst, s(j), r(me), where).start()

    @pl.when(me == j)
    def _():
        pltpu.make_async_copy(src, dst, s(j)).start()


def dealt(j, where, me, src, dst, s, r):
    @pl.when(me != j)
    def _():
        cp = push(src, dst, s(j), r(j), where)
        cp.wait_send()
        cp.wait_recv()

    @pl.when(me == j)
    def _():
        pltpu.make_async_copy(src, dst, s(j)).wait()


def place_of(sem):
    return lambda j: sem.at[j]


def attn_rows(wa, t, low, high):
    first, last = low // 192, -(-high // 192)
    whole = wa[t, first:last].reshape(192 * (last - first), D)
    return whole[low - 192 * first : high - 192 * first]


def up_rows(wt):
    return wt[0:2].reshape(D, D)


def down_rows(wt):
    return wt[2:4].reshape(D, D)


class Inputs:
    def __init__(self, hid, cot, x0, cots, hs, hr, cs, cr, ls):
        self.refs = hid, cot, x0, cots
        self.sems = hs, hr, cs, cr, ls

    def move(self, begin):
        hid, cot, x0, cots = self.refs
        hs, hr, cs, cr, ls = self.sems
        x, ylo, z, yhi, c = here()
        t = 2 * yhi + c
        dp = 2 * x + ylo
        for b in range(4):

            @pl.when((t == z) & (t != b))
            def _(b=b):
                cp = push(hid.at[b // 2, b % 2], x0, hs.at[b], hr.at[0], (dp, z, b))
                if begin:
                    cp.start()
                else:
                    cp.wait_send()

            @pl.when(jnp.logical_not((t == z) & (t == b)))
            def _(b=b):
                cp = push(cot.at[b // 2, b % 2], cots.at[z], cs.at[b], cr.at[z], (dp, t, b))
                if begin:
                    cp.start()
                else:
                    cp.wait_send()

            @pl.when((t == z) & (t == b))
            def _(b=b):
                first = pltpu.make_async_copy(hid.at[b // 2, b % 2], x0, ls.at[0])
                second = pltpu.make_async_copy(cot.at[b // 2, b % 2], cots.at[z], ls.at[1])
                if begin:
                    first.start()
                    second.start()
                else:
                    second.wait()

            if not begin:

                @pl.when(jnp.logical_not((t == z) & (z == b)))
                def _(b=b):
                    push(cots.at[b], cots.at[b], cs.at[b], cr.at[b], (dp, z, (t + 1) % 4)).wait_recv()

    def tokens(self):
        hid, cot, x0, cots = self.refs
        hs, hr, cs, cr, ls = self.sems
        x, ylo, z, yhi, c = here()
        t = 2 * yhi + c

        @pl.when(t != z)
        def _():
            push(x0, x0, hs.at[0], hr.at[0], (2 * x + ylo, z, (t + 1) % 4)).wait_recv()

        @pl.when(t == z)
        def _():
            pltpu.make_async_copy(hid.at[0, 0], x0, ls.at[0]).wait()


def forward_kernel(app, *refs):
    refs = list(refs)

    def take(count):
        got = refs[:count]
        del refs[:count]
        return got

    if app == 0:
        hid, cot = take(2)
    else:
        (a_ref,) = take(1)
        b_ref = take(1)[0] if app == 2 else None
    mod, segc, segr, cosine, sine = take(5)
    if app == 0:
        attn_loc, up_loc, down_loc = take(3)
    elif app == 1:
        wa_in, up_loc, down_loc = take(3)
    else:
        wa_in, wm_in = take(2)
    y_ref, qkv, lse, att, ba, mid, pre, bb = take(8)
    if app == 0:
        x0, cots, wa_out, wm_out, wa1_out = take(5)
    elif app == 1:
        (wm_out,) = take(1)
    sbuf, obuf, rbuf, wa, wm, wsem, ss, rs, ss2, rs2 = take(10)
    x, ylo, z, yhi, c = here()
    places, me = row_places()
    saved = []

    def save(src, dst):
        cp = pltpu.make_async_copy(src, dst, wsem.at[8 + len(saved)])
        cp.start()
        saved.append(cp)

    fetches = []
    if app == 0:
        (wa1,) = take(1)
        g_attn = Gather(wa, [(attn_loc.at[0], 0)], *take(5))
        g_mlp = Gather(wm, [(up_loc.at[0], 0), (down_loc.at[0], 2)], *take(5))
        g_next = Gather(wa1, [(attn_loc.at[1], 0)], *take(5))
        inputs = Inputs(hid, cot, x0, cots, *take(5))
        greet(dp_group() + chips_around())()
        inputs.move(True)
        g_attn.s0()
        g_mlp.s0()
        g_attn.s1()
        g_attn.s2()
        g_mlp.s1()
        g_attn.s3()
        inputs.tokens()
        a_ref, b_ref = x0, None
        entered = lambda: None
    else:
        if app == 1:
            g_mlp = Gather(wm, [(up_loc.at[1], 0), (down_loc.at[1], 2)], *take(5))
            entered = greet(row_mates() + chips_around())
        else:
            entered = greet(row_mates())
        fetches.append(pltpu.make_async_copy(wa_in, wa, wsem.at[0]))
        if app > 1:
            for t in range(4):
                fetches.append(pltpu.make_async_copy(wm_in.at[t], wm.at[t], wsem.at[1 + t]))
        for cp in fetches:
            cp.start()

    v = a_ref[...].astype(F32)
    if b_ref is not None:
        v = v + b_ref[...].astype(F32)
    hat, _ = normalize(v)
    normed = (hat * (1.0 + mod[1:2, :]) + mod[0:1, :]).astype(BF)
    cos_here, sin_here = cosine[...], sine[...]
    low = lanes((TOK, 128)) < 64
    if app == 0:
        g_attn.s4()
        g_mlp.s2()
        g_attn.s5()
        save(wa, wa_out)
    else:
        entered()
        if app == 1:
            g_mlp.s0()
        fetches[0].wait()
    for t in range(4):
        got = nt(normed, attn_rows(wa, t, 0, 640))
        t0, t1, t2, t3, t4 = (got[:, 128 * i : 128 * (i + 1)] for i in range(5))
        s0, s1, s2, s3, s4 = (swap(u) for u in (t0, t1, t2, t3, t4))
        for head, (q, k, w) in enumerate(
            (
                (jnp.where(low, t0, s3), jnp.where(low, s0, t3), jnp.where(low, t1, s4)),
                (jnp.where(low, s1, s3), jnp.where(low, t2, t3), jnp.where(low, s2, s4)),
            )
        ):
            j = 2 * t + head
            sbuf[j, :, 0:128] = (turn(q, cos_here, sin_here).astype(BF).astype(F32) * 0.125).astype(BF)
            sbuf[j, :, 128:256] = turn(k, cos_here, sin_here).astype(BF)
            sbuf[j, :, 256:384] = w.astype(BF)
            deal(j, places[j][1], me, sbuf.at[j], qkv.at[me], place_of(ss), place_of(rs))
    if app == 0:
        g_mlp.s3()
        g_next.s0()
    if app == 1:
        g_mlp.s1()
    for j, where in places:
        dealt(j, where, me, sbuf.at[j], qkv.at[j], place_of(ss), place_of(rs))
    if app == 1:
        g_mlp.s2()

    keys = qkv[:, :, 128:256].reshape(SEQ, 128)
    values = qkv[:, :, 256:384].reshape(SEQ, 128)
    seg_keys = segr[...]

    def softmax(q, seg_q):
        scores = jnp.where(seg_q == seg_keys, nt(q, keys), -1e30)
        largest = jnp.max(scores, axis=-1, keepdims=True)
        raised = jnp.exp(scores - largest)
        total = jnp.sum(raised, axis=-1, keepdims=True)
        mixed = nn(raised.astype(BF), values) * (1.0 / total)
        return mixed, largest + jnp.log(total)

    def flat(column):
        wide = jnp.broadcast_to(column, (column.shape[0], 128))
        return jnp.transpose(wide)[0:8, :]

    for a in range(4):
        if app == 0 and a == 1:
            g_next.s1()
        if app == 1 and a == 2:
            g_mlp.s3()
        q = qkv[2 * a : 2 * a + 2, :, 0:128].reshape(256, 128)
        q = jnp.where(lanes((256, 128)) < 64, q, 0).astype(BF)
        mixed, total = softmax(q, segc[256 * a : 256 * (a + 1), :])
        q2 = jnp.where(low, 0, qkv[2 * a + c, :, 0:128]).astype(BF)
        mixed2, total2 = softmax(q2, segc[pl.ds(256 * a + TOK * c, TOK), :])
        lse[a, :, 0:256] = flat(total)
        lse[a, :, 256:384] = flat(total2)
        for b in range(2):
            j = 2 * a + b
            part = mixed[TOK * b : TOK * (b + 1)]
            obuf[j] = jnp.where(low | (c != b), part, mixed2).astype(BF)
            deal(j, places[j][1], me, obuf.at[j], rbuf.at[me], place_of(ss2), place_of(rs2))
    if app < 2:
        g_mlp.s4()
    if app == 0:
        g_next.s2()
    for j, where in places:
        dealt(j, where, me, obuf.at[j], rbuf.at[j], place_of(ss2), place_of(rs2))

    branch_a = jnp.zeros((TOK, D), F32)
    for t in range(4):
        first, second = rbuf[2 * t], rbuf[2 * t + 1]
        own = jnp.where(low, first.astype(F32), swap(second.astype(F32))).astype(BF)
        extra = jnp.where(low, 0, rbuf[2 * t + c]).astype(BF)
        att[:, 128 * t : 128 * (t + 1)] = own
        att[:, 512 + 128 * t : 512 + 128 * (t + 1)] = extra
        branch_a = branch_a + nn(own, attn_rows(wa, t, 576, 704)) + nn(extra, attn_rows(wa, t, 640, 768))
    ba[...] = branch_a
    middle = v + mod[2:3, :] * branch_a
    mid[...] = middle
    hat_b, _ = normalize(middle)
    normed_b = (hat_b * (1.0 + mod[4:5, :]) + mod[3:4, :]).astype(BF)
    if app < 2:
        g_mlp.s5()
        save(wm, wm_out)
    if app == 0:
        g_next.s3()
    for cp in fetches[1:]:
        cp.wait()
    total_b = jnp.zeros((TOK, D), F32)
    for t in range(4):
        before = nn(normed_b, up_rows(wm.at[t]))
        pre[:, D * t : D * (t + 1)] = before.astype(pre.dtype)
        total_b = total_b + nn(jax.nn.gelu(before, approximate=True).astype(BF), down_rows(wm.at[t]))
    bb[...] = total_b
    y_ref[...] = (middle + mod[5:6, :] * total_b).astype(BF)
    if app == 0:
        g_next.s4()
        g_next.s5()
        save(wa1, wa1_out)
        inputs.move(False)
    for cp in saved:
        cp.wait()


def forward(app, *operands):
    dma = pltpu.SemaphoreType.DMA

    def shape(*dims, dtype=BF):
        return jax.ShapeDtypeStruct(dims, dtype)

    outs = [
        shape(TOK, D),
        shape(8, TOK, 384),
        shape(4, 8, 384, dtype=F32),
        shape(TOK, 1024),
        shape(TOK, D, dtype=F32),
        shape(TOK, D, dtype=F32),
        shape(TOK, 4 * D, dtype=F32),
        shape(TOK, D, dtype=F32),
    ]
    out_specs = [VM] * 8
    scratch = [
        pltpu.VMEM((8, TOK, 384), BF),
        pltpu.VMEM((8, TOK, 128), BF),
        pltpu.VMEM((8, TOK, 128), BF),
        pltpu.VMEM((4,) + ATTN, BF),
        pltpu.VMEM((4,) + MLP, BF),
        dma((11,)),
    ] + [dma((8,))] * 4
    if app == 0:
        in_specs = [ANY] * 2 + [VM] * 5 + [ANY] * 3
        outs += [shape(TOK, D), shape(4, TOK, D), shape(4, *ATTN), shape(4, *MLP), shape(4, *ATTN)]
        out_specs += [VM] + [ANY] * 4
        scratch.append(pltpu.VMEM((4,) + ATTN, BF))
        for _ in range(3):
            scratch += gather_scratch()
        scratch += [dma((4,)), dma((1,)), dma((4,)), dma((4,)), dma((2,))]
    elif app == 1:
        in_specs = [VM] * 6 + [ANY] * 3
        outs.append(shape(4, *MLP))
        out_specs.append(ANY)
        scratch += gather_scratch()
    else:
        in_specs = [VM] * (7 if app == 2 else 6) + [ANY] * 2
    return pl.pallas_call(
        functools.partial(forward_kernel, app),
        out_shape=tuple(outs),
        in_specs=in_specs,
        out_specs=tuple(out_specs),
        scratch_shapes=scratch,
        compiler_params=pltpu.CompilerParams(
            collective_id=1 + app, has_side_effects=True, vmem_limit_bytes=52 * 2**20
        ),
        name=f"forward_{app}",
    )(*operands)


class Reduce:
    def __init__(self, grads, refs):
        self.grads = grads
        (
            self.own0, self.own1, self.own2, self.in0, self.in1, self.in2,
            self.mid0, self.mid1, self.mid2, self.tot0, self.tot1, self.tot2,
            self.end0, self.end1, self.end2,
            self.ls, self.ss, self.rs, self.ss2, self.rs2, self.ss3, self.rs3,
        ) = refs

    @staticmethod
    def scratch():
        dma = pltpu.SemaphoreType.DMA

        def buf(*dims):
            return pltpu.VMEM(dims, BF)

        return [
            buf(2, 4, 48, D), buf(4, 4, 48, HALF), buf(2, 4, 48, D),
            buf(3, 2, 4, 48, D), buf(3, 4, 4, 48, HALF), buf(3, 2, 4, 48, D),
            buf(3, 4, 48, HALF), buf(3, 4, 48, HALF), buf(3, 2, 48, D),
            buf(4, 48, HALF), buf(4, 48, HALF), buf(2, 48, D),
            buf(3, 48, HALF), buf(3, 48, HALF), buf(3, 48, HALF),
            dma((3,)), dma((9,)), dma((9,)), dma((9,)), dma((9,)), dma((9,)), dma((9,)),
        ]

    @staticmethod
    def greeted():
        x, ylo, z, yhi, c = here()
        y = 2 * yhi + ylo
        found = [dev((x + o) % 4, ylo, z, yhi, c) for o in (1, 2, 3)]
        found += [dev(x, (y + o) % 2, z, ((y + o) % 4) // 2, c) for o in (1, 2, 3)]
        return found

    def xpeer(self, o):
        x, ylo, z, yhi, c = here()
        return dev((x + o) % 4, ylo, z, yhi, c), (x + o) % 4

    def zpeer(self, o):
        x, ylo, z, yhi, c = here()
        return dev(x, ylo, (z + o) % 4, yhi, c), (z + o) % 4

    def ypeer(self, o):
        x, ylo, z, yhi, c = here()
        to = (2 * yhi + ylo + o) % 4
        return dev(x, to % 2, z, to // 2, c), to

    def load(self):
        x, ylo, z, yhi, c = here()
        g = self.grads
        pairs = (
            (g.at[:, x, :, 0], self.own0),
            (g.at[yhi, :, :, 1, :, half(ylo)], self.own1),
            (g.at[:, :, z, 2], self.own2),
        )
        return [pltpu.make_async_copy(a, b, self.ls.at[n]) for n, (a, b) in enumerate(pairs)]

    def first(self):
        g, found = self.grads, []
        for o in (2, 1, 3):
            n = o - 1
            where, to = self.xpeer(o)
            found.append(push(g.at[:, to, :, 0], self.in0.at[n], self.ss.at[n], self.rs.at[n], where))
            where, to = self.ypeer(o)
            found.append(
                push(g.at[to // 2, :, :, 1, :, half(to % 2)], self.in1.at[n], self.ss.at[3 + n], self.rs.at[3 + n], where)
            )
            where, to = self.zpeer(o)
            found.append(push(g.at[:, :, to, 2], self.in2.at[n], self.ss.at[6 + n], self.rs.at[6 + n], where))
        return found

    def second(self):
        found = []
        for o in (2, 1, 3):
            n = o - 1
            where, to = self.ypeer(o)
            found.append(
                push(self.own0.at[to // 2, :, :, half(to % 2)], self.mid0.at[n], self.ss2.at[n], self.rs2.at[n], where)
            )
            where, to = self.zpeer(o)
            found.append(push(self.own1.at[:, to], self.mid1.at[n], self.ss2.at[3 + n], self.rs2.at[3 + n], where))
            where, to = self.xpeer(o)
            found.append(push(self.own2.at[:, to], self.mid2.at[n], self.ss2.at[6 + n], self.rs2.at[6 + n], where))
        return found

    def third(self):
        found = []
        for o in (2, 1, 3):
            n = o - 1
            where, to = self.zpeer(o)
            found.append(push(self.tot0.at[to], self.end0.at[n], self.ss3.at[n], self.rs3.at[n], where))
            where, to = self.xpeer(o)
            found.append(push(self.tot1.at[to], self.end1.at[n], self.ss3.at[3 + n], self.rs3.at[3 + n], where))
            where, to = self.ypeer(o)
            found.append(
                push(self.tot2.at[to // 2, :, half(to % 2)], self.end2.at[n], self.ss3.at[6 + n], self.rs3.at[6 + n], where)
            )
        return found

    def begin(self):
        for cp in self.load() + self.first():
            cp.start()

    def sum_first(self):
        for cp in self.load() + self.first():
            cp.wait()

        def body(i, carry):
            j, k = i // 4, i % 4
            for own, more in ((self.own0, self.in0), (self.own2, self.in2)):
                total = own[j, k].astype(F32)
                for n in range(3):
                    total = total + more[n, j, k].astype(F32)
                own[j, k] = total.astype(BF)
            for row in (j, j + 2):
                total = self.own1[row, k].astype(F32)
                for n in range(3):
                    total = total + self.in1[n, row, k].astype(F32)
                self.own1[row, k] = total.astype(BF)
            return carry

        lax.fori_loop(0, 8, body, 0)
        for cp in self.second():
            cp.start()

    def sum_second(self):
        x, ylo, z, yhi, c = here()
        for cp in self.second():
            cp.wait()
        for i in range(4):
            first = self.own0[yhi, i, :, half(ylo)].astype(F32)
            other = self.own1[i, z].astype(F32)
            for n in range(3):
                first = first + self.mid0[n, i].astype(F32)
                other = other + self.mid1[n, i].astype(F32)
            self.tot0[i] = first.astype(BF)
            self.tot1[i] = other.astype(BF)
        for i in range(2):
            total = self.own2[i, x].astype(F32)
            for n in range(3):
                total = total + self.mid2[n, i].astype(F32)
            self.tot2[i] = total.astype(BF)
        for cp in self.third():
            cp.start()

    def sum_third(self, fin):
        x, ylo, z, yhi, c = here()
        for cp in self.third():
            cp.wait()
        lasts = (self.tot0[z], self.tot1[x], self.tot2[yhi, :, half(ylo)])
        for p, (last, ends) in enumerate(zip(lasts, (self.end0, self.end1, self.end2))):
            total = last.astype(F32)
            for n in range(3):
                total = total + ends[n].astype(F32)
            fin[p] = total.astype(BF)


def gelu_parts(u):
    k = 0.7978845608028654
    square = u * u
    th = jnp.tanh(k * u * (1.0 + 0.044715 * square))
    half_up = 0.5 * (1.0 + th)
    slope = half_up + 0.5 * u * (1.0 - th * th) * (k * (1.0 + 0.134145 * square))
    return u * half_up, slope


def backward_kernel(layer, *refs):
    refs = list(refs)

    def take(count):
        got = refs[:count]
        del refs[:count]
        return got

    a_refs = take(2)
    b_refs = [None, take(1)[0]] if layer == 0 else [None, None]
    (cots,) = take(1)
    more_dy = take(1)[0] if layer == 0 else None
    mod, segc, segr, cosine, sine = take(5)
    qkvs, lses, atts, bas, mids, pres, bbs = (take(2) for _ in range(7))
    wa_in, wm_in = take(2)
    before = take(1)[0] if layer == 0 else None
    din, dinb, dmod, grads = take(4)
    fin = take(1)[0] if layer == 0 else None
    own_na, own_nb, own_dba, own_dbb, own_act, own_dpre, own_dpj = take(7)
    got_na, got_nb, got_dba, got_dbb, got_at, got_act, got_dpre, got_dpj = take(8)
    sbuf, rbuf, sbig, rbig, dmid, dnb, k_own, k_sh, v_own, v_sh = take(10)
    wa, wm, stage_up, stage_down, stage_attn = take(5)
    wsem, gsem, ss, rs, ss2, rs2, xs, xr = take(8)
    rows_of = [slice(TOK * e, TOK * (e + 1)) for e in range(2)]
    x, ylo, z, yhi, c = here()
    places, me = row_places()
    partner = dev(x, ylo, z, yhi, 1 - c)
    reduce = Reduce(before, take(22)) if layer == 0 else None
    entered = greet(row_mates() + (Reduce.greeted() if layer == 0 else []))

    def wm_fetch(t):
        return pltpu.make_async_copy(wm_in.at[t], wm.at[t % 2], wsem.at[1 + t])

    wm_fetch(0).start()
    wm_fetch(1).start()
    wa_fetch = pltpu.make_async_copy(wa_in, wa, wsem.at[0])
    wa_fetch.start()
    scale_a, gate_a = mod[1:2, :], mod[2:3, :]
    scale_b, gate_b = mod[4:5, :], mod[5:6, :]
    low = lanes((TOK, 128)) < 64
    exchanged = {}

    def hand(name, src, dst):
        n = len(exchanged)
        cp = push(src, dst, xs.at[n], xr.at[n], partner)
        cp.start()
        exchanged[name] = cp

    def have(*names):
        for name in names:
            exchanged[name].wait_send()
            exchanged[name].wait_recv()

    def gradient(e):
        dy = cots[layer + 2 * e].astype(F32)
        return dy if more_dy is None else dy + more_dy[e]

    def entry(e):
        v = a_refs[e][...].astype(F32)
        return v if b_refs[e] is None else v + b_refs[e][...].astype(F32)

    dgate_b = jnp.zeros((1, D), F32)
    for e in range(2):
        dy = gradient(e)
        dgate_b = dgate_b + jnp.sum(dy * bbs[e][...], axis=0, keepdims=True)
        own_dbb[rows_of[e], :] = (gate_b * dy).astype(BF)
        hat_b, _ = normalize(mids[e][...])
        own_nb[rows_of[e], :] = (hat_b * (1.0 + scale_b) + mod[3:4, :]).astype(BF)
        hat_a, _ = normalize(entry(e))
        own_na[rows_of[e], :] = (hat_a * (1.0 + scale_a) + mod[0:1, :]).astype(BF)
    entered()
    hand("dbb", own_dbb, got_dbb)
    hand("nb", own_nb, got_nb)
    hand("na", own_na, got_na)
    for e in range(2):
        hand(f"at{e}", atts[e], got_at.at[e])
    if reduce is not None:
        reduce.begin()

    for t in range(4):
        wm_fetch(t).wait()
        d_act = nt(own_dbb[...], down_rows(wm.at[t % 2]))
        for e in range(2):
            act, slope = gelu_parts(pres[e][:, D * t : D * (t + 1)])
            own_act[t, rows_of[e], :] = act.astype(BF)
            own_dpre[t, rows_of[e], :] = (d_act[rows_of[e]] * slope).astype(BF)
        more = nt(own_dpre[t], up_rows(wm.at[t % 2]))
        dnb[...] = more if t == 0 else dnb[...] + more
        if t < 2:
            wm_fetch(t + 2).start()
    for h in range(2):
        hand(f"act{h}", own_act.at[2 * h + 1 - c], got_act.at[h])
        hand(f"dpre{h}", own_dpre.at[2 * h + 1 - c], got_dpre.at[h])

    dgate_a = jnp.zeros((1, D), F32)
    dscale_b = jnp.zeros((1, D), F32)
    dshift_b = jnp.zeros((1, D), F32)
    for e in range(2):
        hat_b, inv_b = normalize(mids[e][...])
        g = dnb[rows_of[e], :]
        dscale_b = dscale_b + jnp.sum(g * hat_b, axis=0, keepdims=True)
        dshift_b = dshift_b + jnp.sum(g, axis=0, keepdims=True)
        d_middle = gradient(e) + norm_back(g * (1.0 + scale_b), hat_b, inv_b)
        dmid[rows_of[e], :] = d_middle
        dgate_a = dgate_a + jnp.sum(d_middle * bas[e][...], axis=0, keepdims=True)
        own_dba[rows_of[e], :] = (gate_a * d_middle).astype(BF)
    hand("dba", own_dba, got_dba)
    wa_fetch.wait()
    for t in range(4):
        first = nt(own_dba[...], attn_rows(wa, t, 576, 704))
        second = nt(own_dba[...], attn_rows(wa, t, 640, 768))
        for e in range(2):
            sbuf[2 * t, e] = jnp.where(low, first[rows_of[e]], second[rows_of[e]]).astype(BF)
            sbuf[2 * t + 1, e] = second[rows_of[e]].astype(BF)
        for b in range(2):
            j = 2 * t + b
            deal(j, places[j][1], me, sbuf.at[j], rbuf.at[me], place_of(ss), place_of(rs))

    have("dbb", "nb", "act0", "dpre0", "act1", "dpre1")

    def staged(n, stage, dst):
        return pltpu.make_async_copy(stage, dst, gsem.at[n])

    for h in range(2):
        t = 2 * h + c
        up_copy = staged(0, stage_up, grads.at[h, 0:2, :, :, 16:48])
        down_copy = staged(1, stage_down, grads.at[h, 2:4, :, :, 16:48])
        if h:
            up_copy.wait()
        total = tn(own_nb[...], own_dpre[t]) + tn(got_nb[...], got_dpre[h])
        stage_up[...] = total.astype(BF).reshape(2, 4, 3, 32, D)
        up_copy.start()
        if h:
            down_copy.wait()
        total = tn(own_act[t], own_dbb[...]) + tn(got_act[h], got_dbb[...])
        stage_down[...] = total.astype(BF).reshape(2, 4, 3, 32, D)
        down_copy.start()
    for j, where in places:
        dealt(j, where, me, sbuf.at[j], rbuf.at[j], place_of(ss), place_of(rs))

    seg_keys = segc[...]
    wide = lanes((256, 128)) < 64
    for e in range(2):
        qkv, lse = qkvs[e], lses[e]
        for ref in (k_own, k_sh, v_own, v_sh):
            ref[...] = jnp.zeros_like(ref)

        def one(q, go, seg_q, total, k_sum, v_sum, qkv=qkv):
            keys = qkv[:, :, 128:256].reshape(SEQ, 128)
            values = qkv[:, :, 256:384].reshape(SEQ, 128)
            scores = jnp.where(seg_keys == seg_q, nt(keys, q), -1e30)
            p = jnp.exp(scores - total)
            d_p = nt(values, go)
            centre = jnp.sum(d_p * p, axis=0, keepdims=True)
            d_s = (p * (d_p - centre)).astype(BF)
            v_sum[...] += nn(p.astype(BF), go)
            k_sum[...] += nn(d_s, q)
            return tn(d_s, keys) * 0.125

        for a in range(4):
            q = qkv[2 * a : 2 * a + 2, :, 0:128].reshape(256, 128)
            go = rbuf[2 * a : 2 * a + 2, e].reshape(256, 128)
            dq = one(
                jnp.where(wide, q, 0).astype(BF),
                jnp.where(wide, go, 0).astype(BF),
                segr[0:1, 256 * a : 256 * (a + 1)],
                lse[a, 0:1, 0:256],
                k_own,
                v_own,
            )
            q2 = jnp.where(low, 0, qkv[2 * a + c, :, 0:128]).astype(BF)
            go2 = jnp.where(low, 0, rbuf[2 * a + c, e]).astype(BF)
            seg2 = jnp.where(
                c == 0,
                segr[0:1, 256 * a : 256 * a + 128],
                segr[0:1, 256 * a + 128 : 256 * a + 256],
            )
            dq2 = one(q2, go2, seg2, lse[a, 0:1, 256:384], k_sh, v_sh)
            for b in range(2):
                rows = slice(256 * a + TOK * b, 256 * a + TOK * (b + 1))
                whole = jnp.where(low, dq[TOK * b : TOK * (b + 1)], jnp.where(c == b, dq2, 0.0))
                sbig[2 * a + b, e, :, 0:128] = turn(whole, cosine[rows, :], -sine[rows, :]).astype(BF)
        for j, where in places:
            rows = slice(TOK * j, TOK * (j + 1))
            whole = jnp.where(low, k_own[rows, :], k_sh[rows, :])
            sbig[j, e, :, 128:256] = turn(whole, cosine[rows, :], -sine[rows, :]).astype(BF)
            sbig[j, e, :, 256:384] = jnp.where(low, v_own[rows, :], v_sh[rows, :]).astype(BF)
            deal(
                j, where, me, sbig.at[j, e], rbig.at[me, e],
                lambda i, e=e: ss2.at[e, i], lambda i, e=e: rs2.at[e, i],
            )
        if reduce is not None:
            (reduce.sum_first, reduce.sum_second)[e]()
    for e in range(2):
        for j, where in places:
            dealt(
                j, where, me, sbig.at[j, e], rbig.at[j, e],
                lambda i, e=e: ss2.at[e, i], lambda i, e=e: rs2.at[e, i],
            )
        for t in range(4):
            q0, k0, v0 = (rbig[2 * t, e, :, 128 * i : 128 * (i + 1)].astype(F32) for i in range(3))
            q1, k1, v1 = (rbig[2 * t + 1, e, :, 128 * i : 128 * (i + 1)].astype(F32) for i in range(3))
            tiles = (
                jnp.where(low, q0, swap(k0)),
                jnp.where(low, v0, swap(q1)),
                jnp.where(low, k1, swap(v1)),
                jnp.where(low, swap(q0 + q1), k0 + k1),
                jnp.where(low, swap(v0 + v1), 0.0),
            )
            for i, tile in enumerate(tiles):
                own_dpj[t, rows_of[e], 128 * i : 128 * (i + 1)] = tile.astype(BF)
    for h in range(2):
        hand(f"dpj{h}", own_dpj.at[2 * h + 1 - c], got_dpj.at[h])
    dna = jnp.zeros((2 * TOK, D), F32)
    for t in range(4):
        dna = dna + nn(own_dpj[t], attn_rows(wa, t, 0, 640))
    dscale_a = jnp.zeros((1, D), F32)
    dshift_a = jnp.zeros((1, D), F32)
    for e in range(2):
        hat_a, inv_a = normalize(entry(e))
        g = dna[rows_of[e]]
        dscale_a = dscale_a + jnp.sum(g * hat_a, axis=0, keepdims=True)
        dshift_a = dshift_a + jnp.sum(g, axis=0, keepdims=True)
        total = dmid[rows_of[e], :] + norm_back(g * (1.0 + scale_a), hat_a, inv_a)
        din[e] = total
        dinb[e] = total.astype(BF)
    for i, part in enumerate((dshift_a, dscale_a, dgate_a, dshift_b, dscale_b, dgate_b)):
        dmod[i : i + 1, :] = part
    dmod[6:8, :] = jnp.zeros((2, D), F32)

    have("na", "at0", "at1", "dba", "dpj0", "dpj1")
    for h in range(2):
        t = 2 * h + c
        copy = staged(2, stage_attn, grads.at[h, :, :, :, 0:16])
        if h:
            copy.wait()
        total = tn(own_dpj[t], own_na[...]) + tn(got_dpj[h], got_na[...])
        stage_attn[0:3] = total[0:576].astype(BF).reshape(3, 4, 3, 16, D)
        parts = []
        for first in (0, 512):
            cols = pl.ds(pl.multiple_of(first + 128 * t, 128), 128)
            total = jnp.zeros((128, D), F32)
            for e in range(2):
                total = total + tn(atts[e][:, cols], own_dba[rows_of[e], :])
                total = total + tn(got_at[e, :, cols], got_dba[rows_of[e], :])
            parts.append(total)
        total = jnp.concatenate([parts[0], parts[1][64:128]], axis=0)
        stage_attn[3] = total.astype(BF).reshape(4, 3, 16, D)
        copy.start()
    if reduce is not None:
        reduce.sum_third(fin)
    staged(0, stage_up, grads.at[1, 0:2, :, :, 16:48]).wait()
    staged(1, stage_down, grads.at[1, 2:4, :, :, 16:48]).wait()
    staged(2, stage_attn, grads.at[1, :, :, :, 0:16]).wait()


def backward(layer, *operands):
    dma = pltpu.SemaphoreType.DMA
    both = 2 * TOK

    def buf(*dims, dtype=BF):
        return pltpu.VMEM(dims, dtype)

    outs = [
        jax.ShapeDtypeStruct((2, TOK, D), F32),
        jax.ShapeDtypeStruct((2, TOK, D), BF),
        jax.ShapeDtypeStruct((8, D), F32),
        jax.ShapeDtypeStruct((2,) + UNIT, BF),
    ]
    out_specs = [VM, VM, VM, ANY]
    if layer == 0:
        outs.append(jax.ShapeDtypeStruct((3, 48, HALF), BF))
        out_specs.append(VM)
    scratch = [buf(both, D)] * 4 + [buf(4, both, D)] * 2 + [buf(4, both, 640)]
    scratch += [buf(both, D)] * 4 + [buf(2, TOK, 1024)] + [buf(2, both, D)] * 2 + [buf(2, both, 640)]
    scratch += [buf(8, 2, TOK, 128)] * 2 + [buf(8, 2, TOK, 384)] * 2
    scratch += [buf(both, D, dtype=F32)] * 2 + [buf(SEQ, 128, dtype=F32)] * 4
    scratch += [buf(4, *ATTN), buf(2, *MLP), buf(2, 4, 3, 32, D), buf(2, 4, 3, 32, D), buf(*ATTN)]
    scratch += [dma((5,)), dma((3,)), dma((8,)), dma((8,)), dma((2, 8)), dma((2, 8)), dma((12,)), dma((12,))]
    if layer == 0:
        scratch += Reduce.scratch()
    vmem_in = len(operands) - (3 if layer == 0 else 2)
    return pl.pallas_call(
        functools.partial(backward_kernel, layer),
        out_shape=tuple(outs),
        in_specs=[VM] * vmem_in + [ANY] * (len(operands) - vmem_in),
        out_specs=tuple(out_specs),
        scratch_shapes=scratch,
        compiler_params=pltpu.CompilerParams(
            collective_id=5 + layer, has_side_effects=True, vmem_limit_bytes=62 * 2**20
        ),
        name=f"backward_{layer}",
    )(*operands)


def finish_kernel(
    g0, fin1, dm0, dm1, feat, y0, y1, y2, y3, db0, db1,
    out0, out1, y_out, g_out, rows_out,
    fin0, dm_in, dsum, *rest,
):
    rest = list(rest)
    reduce = Reduce(g0, rest[:22])
    ss_a, rs_a, ss_b, rs_b, ys_s, ys_r, gs_s, gs_r, ms, mr, ms2, mr2, fsem = rest[22:]
    x, ylo, z, yhi, c = here()
    t = 2 * yhi + c
    dp = 2 * x + ylo
    places, me = row_places()
    row = 2 * dp + yhi
    others = []
    for o in range(1, 16):
        r = (row + o) % 16
        others.append(dev(r // 4, (r // 2) % 2, z, r % 2, c))
    far = []
    for o in range(1, 8):
        g = (dp + o) % 8
        far += [(g, z, 2 * b + c) for b in range(2)]
    greet(dp_group() + far)()
    reduce.begin()

    first = pltpu.make_async_copy(fin1, out1.at[x, z, :, :, half(ylo)], fsem.at[0])
    first.start()
    for j, where in places:

        @pl.when(me != j)
        def _(j=j, where=where):
            push(dm0, dm_in.at[me, 0], ms.at[0, j], mr.at[0, me], where).start()
            push(dm1, dm_in.at[me, 1], ms.at[1, j], mr.at[1, me], where).start()

    y_src = (y0, y1, y2, y3)
    g_src = (db0.at[0], db1.at[0], db0.at[1], db1.at[1])

    def scatter(src, dst, s_sem, r_sem, begin):
        for s in range(4):
            mine = (z == s) & (t == z)

            @pl.when(jnp.logical_not(mine))
            def _(s=s):
                cp = push(src[s], dst.at[yhi, c], s_sem.at[s], r_sem.at[t], (dp, s, z))
                if begin:
                    cp.start()
                else:
                    cp.wait_send()

            @pl.when(mine)
            def _(s=s):
                cp = pltpu.make_async_copy(src[s], dst.at[yhi, c], s_sem.at[s])
                if begin:
                    cp.start()
                else:
                    cp.wait()

        if not begin:
            for b in range(4):

                @pl.when(jnp.logical_not((t == z) & (t == b)))
                def _(b=b):
                    spot = dst.at[b // 2, b % 2]
                    push(spot, spot, s_sem.at[b], r_sem.at[b], (dp, z, (t + 1) % 4)).wait_recv()

    scatter(y_src, y_out, ys_s, ys_r, True)
    scatter(g_src, g_out, gs_s, gs_r, True)
    ag1, ag0 = Spread(out1, ss_a, rs_a), Spread(out0, ss_b, rs_b)
    first.wait()
    ag1.start(0)

    for j, where in places:

        @pl.when(me != j)
        def _(j=j, where=where):
            for l, ref in enumerate((dm0, dm1)):
                cp = push(ref, dm_in.at[j, l], ms.at[l, j], mr.at[l, j], where)
                cp.wait_send()
                cp.wait_recv()

        @pl.when(me == j)
        def _(j=j):
            dm_in[j, 0] = dm0[...]
            dm_in[j, 1] = dm1[...]

    total = dm_in[0]
    for j in range(1, 8):
        total = total + dm_in[j]
    dsum[...] = total
    dsum[0, 6:7, 0:128] = feat[...]
    moved = [
        push(dsum, rows_out.at[row], ms2.at[o], mr2.at[o], where) for o, where in enumerate(others)
    ]
    for cp in moved:
        cp.start()
    keep = pltpu.make_async_copy(dsum, rows_out.at[row], fsem.at[1])
    keep.start()
    ag1.finish()
    ag1.start(1)

    reduce.sum_first()
    ag1.finish()
    reduce.sum_second()
    ag1.start(2)
    reduce.sum_third(fin0)
    last = pltpu.make_async_copy(fin0, out0.at[x, z, :, :, half(ylo)], fsem.at[2])
    last.start()
    last.wait()
    for phase in range(3):
        ag0.start(phase)
        ag0.finish()
    ag1.finish()
    keep.wait()
    for cp in moved:
        cp.wait()
    scatter(y_src, y_out, ys_s, ys_r, False)
    scatter(g_src, g_out, gs_s, gs_r, False)


def finish(*operands):
    dma = pltpu.SemaphoreType.DMA
    return pl.pallas_call(
        finish_kernel,
        out_shape=(
            jax.ShapeDtypeStruct(UNIT, BF),
            jax.ShapeDtypeStruct(UNIT, BF),
            jax.ShapeDtypeStruct((2, 2, TOK, D), BF),
            jax.ShapeDtypeStruct((2, 2, TOK, D), BF),
            jax.ShapeDtypeStruct((16, 2, 8, D), F32),
        ),
        in_specs=[ANY] + [VM] * 4 + [ANY] * 6,
        out_specs=(ANY,) * 5,
        scratch_shapes=[
            pltpu.VMEM((3, 48, HALF), BF),
            pltpu.VMEM((8, 2, 8, D), F32),
            pltpu.VMEM((2, 8, D), F32),
        ]
        + Reduce.scratch()
        + [dma((27,)), dma((27,)), dma((27,)), dma((27,))]
        + [dma((4,)), dma((4,)), dma((4,)), dma((4,))]
        + [dma((2, 8)), dma((2, 8)), dma((15,)), dma((15,)), dma((3,))],
        compiler_params=pltpu.CompilerParams(
            collective_id=7, has_side_effects=True, vmem_limit_bytes=40 * 2**20
        ),
        name="finish",
    )(*operands)


def modulation_kernel(rows, grad_mod, grad_bias):
    features = rows[:, 0, 6, 0:128]
    for l in range(2):
        for i in range(6):
            cols = slice(D * i, D * (i + 1))
            d = rows[:, l, i, :]
            grad_mod[l, :, cols] = lax.dot_general(
                features, d, (((0,), (0,)), ((), ())), precision=highest, preferred_element_type=F32
            )
            grad_bias[l : l + 1, cols] = jnp.sum(d, axis=0, keepdims=True)


def modulation_grads(rows):
    return pl.pallas_call(
        modulation_kernel,
        out_shape=(
            jax.ShapeDtypeStruct((2, 128, 6 * D), F32),
            jax.ShapeDtypeStruct((2, 6 * D), F32),
        ),
        in_specs=[VM],
        out_specs=(VM, VM),
        compiler_params=pltpu.CompilerParams(vmem_limit_bytes=30 * 2**20),
        name="modulation_grads",
    )(rows)


def rotary(count):
    frequency = np.exp(-np.log(10000.0) * np.arange(32) / 32)
    angles = np.arange(count)[:, None] * frequency[None, :]
    cos, sin = np.cos(angles), np.sin(angles)
    return (
        np.concatenate([cos] * 4, axis=1).astype(np.float32),
        np.concatenate([-sin, sin, -sin, sin], axis=1).astype(np.float32),
    )


def time_features(step_values, feature_count):
    half_count = feature_count // 2
    frequency = jnp.exp(-np.log(10000.0) * jnp.arange(half_count, dtype=F32) / half_count)
    angles = step_values.astype(F32)[:, None] * frequency[None, :]
    return jnp.concatenate([jnp.cos(angles), jnp.sin(angles)], axis=1)


def on_device(hidden_in, segments, timestep, w_qkv, w_out, w_up, w_down, w_mod, b_mod, cotangent):
    x, ylo, z, yhi, c = here()
    attn_loc = jnp.concatenate([jnp.swapaxes(w_qkv, 1, 2), w_out], axis=1).reshape((2,) + ATTN)
    up_loc = w_up.reshape(2, 2, 4, 3, 32, D)
    down_loc = w_down.reshape(2, 2, 4, 3, 32, D)

    mine = lax.dynamic_slice_in_dim(timestep, yhi, 1, 0)
    features = time_features(mine, w_mod.shape[1])
    modulation = jnp.einsum(
        "rf,lfm->lrm", features, w_mod.astype(F32), precision=highest
    ) + b_mod.astype(F32)[:, None, :]
    modulation = modulation.reshape(2, 6, D)
    mods = (modulation[0], modulation[1])
    seg = lax.dynamic_slice_in_dim(segments, yhi, 1, 0)
    segc, segr = seg.reshape(SEQ, 1), seg
    cosine, sine = (jnp.asarray(v) for v in rotary(SEQ))
    place = (2 * z + c) * TOK
    cos_here = lax.dynamic_slice_in_dim(cosine, place, TOK, 0)
    sin_here = lax.dynamic_slice_in_dim(sine, place, TOK, 0)

    shared = (segc, segr, cos_here, sin_here)
    y0, *rest = forward(
        0,
        hidden_in.reshape(2, 2, TOK, D),
        cotangent.reshape(2, 2, TOK, D),
        mods[0],
        *shared,
        attn_loc,
        up_loc,
        down_loc,
    )
    kept0, (x0, cots, wa0, wm0, wa1) = rest[:7], rest[7:]
    y1, *rest = forward(1, y0, mods[1], *shared, wa1, up_loc, down_loc)
    kept1, (wm1,) = rest[:7], rest[7:]
    y2, *kept2 = forward(2, x0, y1, mods[0], *shared, wa0, wm0)
    y3, *kept3 = forward(3, y2, mods[1], *shared, wa1, wm1)

    def pairs(one, two):
        return [item for pair in zip(one, two) for item in pair]

    tables = (segc, segr, cosine, sine)
    din1, dinb1, dm1, g1 = backward(1, y0, y2, cots, mods[1], *tables, *pairs(kept1, kept3), wa1, wm1)
    din0, dinb0, dm0, g0, fin1 = backward(
        0, x0, x0, y1, cots, din1, mods[0], *tables, *pairs(kept0, kept2), wa0, wm0, g1
    )
    out0, out1, y_out, g_out, rows = finish(g0, fin1, dm0, dm1, features, y0, y1, y2, y3, dinb0, dinb1)
    grad_mod, grad_bias = modulation_grads(rows)

    out = jnp.stack([out0, out1])
    attn = out[:, :, :, :, 0:16].reshape(2, D, D)
    mlp = out[:, :, :, :, 16:48].reshape(2, 2 * D, D)
    return (
        y_out.reshape(1, 2, 2 * TOK, D),
        g_out.reshape(1, 2, 2 * TOK, D).astype(F32),
        attn[:, 0:576].swapaxes(1, 2).astype(F32),
        attn[:, 576:768].astype(F32),
        mlp[:, 0:768].astype(F32),
        mlp[:, 768:1536].astype(F32),
        grad_mod,
        grad_bias,
    )


def solution(mesh):
    placed = (
        P("dp", "tensor", None),
        P("dp", None),
        P("dp"),
        P(None, None, "tensor"),
        P(None, "tensor", None),
        P(None, None, "tensor"),
        P(None, "tensor", None),
        P(),
        P(),
        P("section", "dp", "tensor", None),
    )
    return jax.shard_map(
        on_device,
        mesh=mesh,
        in_specs=placed,
        out_specs=(
            P("section", "dp", "tensor", None),
            P("section", "dp", "tensor", None),
            P(None, None, "tensor"),
            P(None, "tensor", None),
            P(None, None, "tensor"),
            P(None, "tensor", None),
            P(),
            P(),
        ),
        check_vma=False,
    )
```

time: 775 us -> 503 us (0.65)
  the two profiles are of different devices: /device:TPU:16 before, /device:TPU:0 now
where the time goes in v2:
time: 503 us; the launch traced here: 494 us
  Pallas kernels  460 us (91%)
  local copies, waits for them, and re-layouts  16.3 us (3%)
  other arithmetic  12.2 us (2%)
    pallas_call x4, Pallas kernels, forward(): pl.pallas_call(functools.partial(forward_kernel, app), out_shape=tuple(ou...  180 us
    pallas_call x2, Pallas kernels, backward(): pl.pallas_call(functools.partial(backward_kernel, layer), out_shape=tuple...  137 us
    pallas_call x1, Pallas kernels, finish(): pl.pallas_call(finish_kernel, out_shape=(jax.ShapeDtypeStruct(UNIT, BF),...  136 us
    unnamed x71, local copies, waits for them, and re-layouts  12.9 us

profile of v2, /device:TPU:0, one launch (start us, length us, event | category | flops | bytes accessed | tf_op | source)
XLA Modules:
  0.0 493.7 jit_solution(4821779859616036124)
XLA Ops:
  0.7 1.4 dynamic_slice.12
  2.9 2.7 fusion
  5.6 0.8 bitcast_add_fusion
  6.5 0.9 constant_dynamic-slice_fusion
  7.4 1.0 copy.20.refs_3_.refs_2_.refs_4_.refs_6_
  8.4 1.6 pad_maximum_fusion.2
  10.0 81.4 %forward_0.1 = (bf16[128,768]{1,0:T(8,128)(2,1)S(1)}, bf16[8,128,384]{2,1,0:T(8,128)(2,1)}, f32[4,8,384]{2,1,0:T(8,128)S(1)}, bf16[128,1024]{1,0:T(8,128)(2,1)S(...) custom-call(bf16[2,2,128,768]{3,2,1,0:T(8,128)(2,1)} %bitcast.41, ...), custom_call_target="tpu_custom_call" | custom-call | tf_op jit(solution)/shard_map/forward_0/pallas_call | solution.py:580
  92.2 0.8 copy-done.16
  94.3 44.5 %forward_1.1 = (bf16[128,768]{1,0:T(8,128)(2,1)S(1)}, bf16[8,128,384]{2,1,0:T(8,128)(2,1)}, f32[4,8,384]{2,1,0:T(8,128)S(1)}, bf16[128,1024]{1,0:T(8,128)(2,1)S(...) custom-call(bf16[128,768]{1,0:T(8,128)(2,1)S(1)} %get-tuple-element., ...), custom_call_target="tpu_custom_call" | custom-call | tf_op jit(solution)/shard_map/forward_1/pallas_call | solution.py:580
  140.3 27.1 %forward_2.1 = (bf16[128,768]{1,0:T(8,128)(2,1)S(1)}, bf16[8,128,384]{2,1,0:T(8,128)(2,1)}, f32[4,8,384]{2,1,0:T(8,128)S(1)}, bf16[128,1024]{1,0:T(8,128)(2,1)S(...) custom-call(bf16[128,768]{1,0:T(8,128)(2,1)S(1)} %get-tuple-element.61.refs_0_.r, ...), custom_call_target="tpu_custom_call" | custom-call | tf_op jit(solution)/shard_map/forward_2/pallas_call | solution.py:580
  168.2 0.8 copy-done.18
  169.7 27.3 %forward_3.1 = (bf16[128,768]{1,0:T(8,128)(2,1)S(1)}, bf16[8,128,384]{2,1,0:T(8,128)(2,1)}, f32[4,8,384]{2,1,0:T(8,128)S(1)}, bf16[128,1024]{1,0:T(8,128)(2,1)S(...) custom-call(bf16[128,768]{1,0:T(8,128)(2,1)S(1)} %get-tuple-element.68.refs_0_.r, ...), custom_call_target="tpu_custom_call" | custom-call | tf_op jit(solution)/shard_map/forward_3/pallas_call | solution.py:580
  197.8 0.7 copy-done.14
  199.8 55.1 %backward_1.1 = (f32[2,128,768]{2,1,0:T(8,128)}, bf16[2,128,768]{2,1,0:T(8,128)(2,1)}, f32[8,768]{1,0:T(8,128)}, bf16[2,4,4,3,48,768]{5,4,3,2,1,0:T(8,128)(2,1)}) custom-call(bf16[128,768]{1,0:T(8,128)(2,1)} %copy-done.4, bf16[128,768]{1,0:T(8,128)(2,1)} %copy-done.2, bf16[4,128,768]{2,1,0:T(8,128)(2,1)} %get-tuple-element.65.refs_2_.refs_3_, ...), custom_call_target="tpu_custom_call" | custom-call | tf_op jit(solution)/shard_map/backward_1/pallas_call | solution.py:1041
  255.0 82.4 %backward_0.1 = (f32[2,128,768]{2,1,0:T(8,128)}, bf16[2,128,768]{2,1,0:T(8,128)(2,1)}, f32[8,768]{1,0:T(8,128)}, bf16[2,4,4,3,48,768]{5,4,3,2,1,0:T(8,128)(2,1)}, bf16[3,48,384]{2,1,0:T(8,128)(2,1)}) custom-call(bf16[128,768]{1,0:T(8,128)(2,1)} %copy-done.8, bf16[128,768]{1,0:T(8,128)(2,1)} %copy-done.8, bf16[128,768]{1,0:T(8,128)(2,1)} %copy-done.6, ...), custom_call_target="tpu_custom_call" | custom-call | tf_op jit(solution)/shard_map/backward_0/pallas_call | solution.py:1041
  337.4 1.0 copy-done.10
  338.4 0.9 copy-done.26
  340.1 136.3 %finish.1 = (bf16[4,4,3,48,768]{4,3,2,1,0:T(8,128)(2,1)S(1)}, bf16[4,4,3,48,768]{4,3,2,1,0:T(8,128)(2,1)S(1)}, bf16[2,2,128,768]{3,2,1,0:T(8,128)(2,1)S(1)}, bf1...) custom-call(bf16[2,4,4,3,48,768]{5,4,3,2,1,0:T(8,128)(2,1)} %get-tuple-element.100.g0, ...), custom_call_target="tpu_custom_call" | custom-call | tf_op jit(solution)/shard_map/finish/pallas_call | solution.py:1174
  476.4 1.3 convert.2
  478.5 1.1 slice_convert_fusion.2
  479.6 2.1 convert_bitcast_fusion
  481.6 4.6 slice_convert_fusion
  486.2 6.1 %modulation_grads.1 = (f32[2,128,4608]{2,1,0:T(8,128)}, f32[2,4608]{1,0:T(2,128)}) custom-call(f32[16,2,8,768]{3,2,1,0:T(8,128)S(1)} %get-tuple-element.111.rows), custom_call_target="tpu_custom_call" | custom-call | tf_op jit(solution)/shard_map/modulation_grads/pallas_call | solution.py:1214
  492.3 0.9 copy.29
  (74 shorter events, 8.9 us)
Async XLA Ops:
  0.6 2.2 copy-start
  0.7 7.8 %copy-start.34 = (bf16[2,192,768]{2,1,0:T(8,128)(2,1)S(1)}, bf16[2,192,768]{2,1,0:T(8,128)(2,1)}, u32[]{:S(2)}) copy-start(bf16[2,192,768]{2,1,0:T(8,128)(2,1)} %param.16) | copy-start | bytes 1769476
  0.7 7.8 %copy-start.33 = (bf16[2,768,576]{1,2,0:T(8,128)(2,1)S(1)}, bf16[2,768,576]{1,2,0:T(8,128)(2,1)}, u32[]{:S(2)}) copy-start(bf16[2,768,576]{1,2,0:T(8,128)(2,1)} %param.15) | copy-start | bytes 5308420
  2.9 166.7 %copy-start.25 = (s32[1,1024]{1,0:T(1,128)}, s32[1,1024]{1,0:T(1,128)S(1)}, u32[]{:S(2)}) copy-start(s32[1,1024]{1,0:T(1,128)S(1)} %constant_dynamic-slice_fusion.2.refs_4_.refs_3_.refs_5_.refs_7_) | copy-start | bytes 12292
  6.5 163.2 %copy-start.19 = (f32[6,768]{1,0:T(8,128)}, f32[6,768]{1,0:T(8,128)S(1)}, u32[]{:S(2)}) copy-start(f32[6,768]{1,0:T(8,128)S(1)} %squeeze.7.refs_1_.refs_3_) | copy-start | bytes 55300
  6.5 133.8 %copy-start.20 = (f32[6,768]{1,0:T(8,128)}, f32[6,768]{1,0:T(8,128)S(1)}, u32[]{:S(2)}) copy-start(f32[6,768]{1,0:T(8,128)S(1)} %squeeze.6.refs_2_.refs_5_) | copy-start | bytes 55300
  91.5 0.7 copy-start.15
  92.2 0.8 copy-start.16
  94.3 44.5 %copy-start.4 = (bf16[128,768]{1,0:T(8,128)(2,1)}, bf16[128,768]{1,0:T(8,128)(2,1)S(1)}, u32[]{:S(2)}) copy-start(bf16[128,768]{1,0:T(8,128)(2,1)S(1)} %get-tuple-element.62.refs_0_.y0) | copy-start | bytes 589828
  94.3 46.0 %copy-start.8 = (bf16[128,768]{1,0:T(8,128)(2,1)}, bf16[128,768]{1,0:T(8,128)(2,1)S(1)}, u32[]{:S(2)}) copy-start(bf16[128,768]{1,0:T(8,128)(2,1)S(1)} %get-tuple-element.61.refs_0_.refs_1_) | copy-start | bytes 589828
  140.3 27.1 %copy-start.6 = (bf16[128,768]{1,0:T(8,128)(2,1)}, bf16[128,768]{1,0:T(8,128)(2,1)S(1)}, u32[]{:S(2)}) copy-start(bf16[128,768]{1,0:T(8,128)(2,1)S(1)} %get-tuple-element.64.refs_1_.refs_2_.y1) | copy-start | bytes 589828
  140.3 27.1 %copy-start.12 = (f32[128,768]{1,0:T(8,128)}, f32[128,768]{1,0:T(8,128)S(1)}, u32[]{:S(2)}) copy-start(f32[128,768]{1,0:T(8,128)S(1)} %get-tuple-element.78.refs_16_) | copy-start | bytes 1179652
  140.3 27.1 %copy-start.27 = (f32[4,8,384]{2,1,0:T(8,128)}, f32[4,8,384]{2,1,0:T(8,128)S(1)}, u32[]{:S(2)}) copy-start(f32[4,8,384]{2,1,0:T(8,128)S(1)} %get-tuple-element.72.refs_10_) | copy-start | bytes 147460
  168.2 0.8 copy-start.18
  169.6 27.4 %copy-start.2 = (bf16[128,768]{1,0:T(8,128)(2,1)}, bf16[128,768]{1,0:T(8,128)(2,1)S(1)}, u32[]{:S(2)}) copy-start(bf16[128,768]{1,0:T(8,128)(2,1)S(1)} %get-tuple-element.68.refs_0_.refs_1_.y2) | copy-start | bytes 589828
  169.6 27.4 %copy-start.30 = (f32[4,8,384]{2,1,0:T(8,128)}, f32[4,8,384]{2,1,0:T(8,128)S(1)}, u32[]{:S(2)}) copy-start(f32[4,8,384]{2,1,0:T(8,128)S(1)} %get-tuple-element.88.refs_13_) | copy-start | bytes 147460
  254.9 82.5 %copy-start.3 = (bf16[128,768]{1,0:T(8,128)(2,1)S(1)}, bf16[128,768]{1,0:T(8,128)(2,1)}, u32[]{:S(2)}) copy-start(bf16[128,768]{1,0:T(8,128)(2,1)} %copy-done.2) | copy-start | bytes 589828
  254.9 82.5 %copy-start.5 = (bf16[128,768]{1,0:T(8,128)(2,1)S(1)}, bf16[128,768]{1,0:T(8,128)(2,1)}, u32[]{:S(2)}) copy-start(bf16[128,768]{1,0:T(8,128)(2,1)} %copy-done.4) | copy-start | bytes 589828
  254.9 82.5 %copy-start.7 = (bf16[128,768]{1,0:T(8,128)(2,1)S(1)}, bf16[128,768]{1,0:T(8,128)(2,1)}, u32[]{:S(2)}) copy-start(bf16[128,768]{1,0:T(8,128)(2,1)} %copy-done.6) | copy-start | bytes 589828
  254.9 82.5 %copy-start.9 = (bf16[2,128,768]{2,1,0:T(8,128)(2,1)S(1)}, bf16[2,128,768]{2,1,0:T(8,128)(2,1)}, u32[]{:S(2)}) copy-start(bf16[2,128,768]{2,1,0:T(8,128)(2,1)} %get-tuple-element.106.db1) | copy-start | bytes 1179652
  255.0 82.5 %copy-start.31 = (f32[8,768]{1,0:T(8,128)S(1)}, f32[8,768]{1,0:T(8,128)}, u32[]{:S(2)}) copy-start(f32[8,768]{1,0:T(8,128)} %get-tuple-element.103.dm1) | copy-start | bytes 73732
  337.4 1.0 copy-start.10
  338.4 0.9 copy-start.26
  481.6 11.5 %copy-start.1 = (s32[2,1024]{1,0:T(2,128)S(1)}, s32[2,1024]{1,0:T(2,128)}, u32[]{:S(2)}) copy-start(s32[2,1024]{1,0:T(2,128)} %param.13) | copy-start | bytes 24580
  (11 other events, 7.8 us)

commit v3 on v2

v3 whole, which is shorter than its diff:
```python
import functools

import jax
import jax.numpy as jnp
import numpy as np
from jax import lax
from jax.experimental import pallas as pl
from jax.experimental.pallas import tpu as pltpu
from jax.sharding import PartitionSpec as P

MESH = pl.DeviceIdType.MESH
BF = jnp.bfloat16
F32 = jnp.float32
highest = lax.Precision.HIGHEST
EPS = 1e-06
D = 768
TOK = 128
SEQ = 1024
ANY = pl.BlockSpec(memory_space=pl.ANY)
VM = pl.BlockSpec(memory_space=pltpu.VMEM)
HALF = 384
ATTN = (4, 4, 3, 16, D)
MLP = (4, 4, 2, 48, D)


def here():
    dp = lax.axis_index("dp")
    t = lax.axis_index("tensor")
    return dp // 2, dp % 2, lax.axis_index("section"), t // 2, t % 2


def dev(x, ylo, z, yhi, c):
    return (2 * x + ylo, z, 2 * yhi + c)


def push(src, dst, send_sem, recv_sem, where):
    return pltpu.make_async_remote_copy(
        src_ref=src,
        dst_ref=dst,
        send_sem=send_sem,
        recv_sem=recv_sem,
        device_id=where,
        device_id_type=MESH,
    )


def greet(devices):
    barrier = pltpu.get_barrier_semaphore()
    for where in devices:
        pl.semaphore_signal(barrier, inc=1, device_id=where, device_id_type=MESH)
    return lambda: pl.semaphore_wait(barrier, len(devices))


def nn(a, b):
    return lax.dot_general(a, b, (((1,), (0,)), ((), ())), preferred_element_type=F32)


def nt(a, b):
    return lax.dot_general(a, b, (((1,), (1,)), ((), ())), preferred_element_type=F32)


def tn(a, b):
    return lax.dot_general(a, b, (((0,), (0,)), ((), ())), preferred_element_type=F32)


def normalize(values):
    centred = values - jnp.mean(values, axis=-1, keepdims=True)
    inverse = lax.rsqrt(jnp.mean(centred * centred, axis=-1, keepdims=True) + EPS)
    return centred * inverse, inverse


def norm_back(gradient, normed, inverse):
    return inverse * (
        gradient
        - jnp.mean(gradient, axis=-1, keepdims=True)
        - normed * jnp.mean(gradient * normed, axis=-1, keepdims=True)
    )


def lanes(shape):
    return lax.broadcasted_iota(jnp.int32, shape, len(shape) - 1)


def swap(x):
    return pltpu.roll(x, 64, 1)


def turn(x, cosine, sine):
    low = (lanes(x.shape) % 64) < 32
    other = jnp.where(low, pltpu.roll(x, 96, 1), pltpu.roll(x, 32, 1))
    return x * cosine + other * sine


def half(ylo):
    return pl.ds(pl.multiple_of(HALF * ylo, 128), HALF)


class Spread:
    def __init__(self, buf, orders, ss, rs):
        self.buf, self.orders, self.ss, self.rs = buf, orders, ss, rs
        self.running = None

    def at(self, dims, part, by):
        x, ylo, z, yhi, c = here()
        everything = slice(None)
        i = everything if "x" in dims else by.get("x", x)
        j = everything if "z" in dims else by.get("z", z)
        k = everything if "y" in dims else half(by.get("y", ylo))
        return self.buf.at[i, j, part, :, k]

    def peer(self, dim, o):
        x, ylo, z, yhi, c = here()
        if dim == "y":
            return dev(x, 1 - ylo, z, yhi, c), 1 - ylo
        if dim == "x":
            return dev((x + o) % 4, ylo, z, yhi, c), (x - o + 4) % 4
        return dev(x, ylo, (z + o) % 4, yhi, c), (z - o + 4) % 4

    def start(self, phase):
        sent, got = [], []
        for part in range(len(self.orders)):
            dim, done = self.orders[part][phase], self.orders[part][:phase]
            for o in (1,) if dim == "y" else (2, 1, 3):
                where, origin = self.peer(dim, o)
                n = (phase * 3 + part) * 3 + o - 1
                here_now = self.at(done, part, {})
                cp = push(here_now, here_now, self.ss.at[n], self.rs.at[n], where)
                cp.start()
                sent.append(cp)
                back = self.at(done, part, {dim: origin})
                got.append((push(back, back, self.ss.at[n], self.rs.at[n], where), back))
        self.running = sent, got

    def finish(self, each=None):
        sent, got = self.running
        for cp, back in got:
            cp.wait_recv()
            if each is not None:
                each(back)
        for cp in sent:
            cp.wait_send()

    def held(self):
        return [self.at(self.orders[p][:2], p, {}) for p in range(len(self.orders))]


class Gather:
    def __init__(self, wv, pieces, orders, ss, rs, ps, pr, ls):
        x, ylo, z, yhi, c = here()
        self.wv, self.pieces = wv, pieces
        self.ps, self.pr, self.ls = ps, pr, ls
        self.t = 2 * yhi + c
        self.other = 2 * (1 - yhi) + c
        self.partner = dev(x, ylo, z, yhi, 1 - c)
        self.cross = dev(x, 1 - ylo, z, 1 - yhi, c)
        self.spread = Spread(wv.at[self.other], orders, ss, rs)
        self.handed = []

    def side(self, n):
        ref, first = self.pieces[n]
        spot = self.wv.at[self.t, pl.ds(first, ref.shape[0])]
        return (
            pltpu.make_async_copy(ref, spot, self.ls.at[n]),
            push(ref, spot, self.ps.at[n], self.pr.at[n], self.partner),
        )

    def s0(self):
        x, ylo, z, yhi, c = here()
        for ref, first in self.pieces:

            @pl.when((x >= first) & (x < first + ref.shape[0]))
            def _(ref=ref, first=first):
                push(
                    ref.at[x - first, z, :, :, half(1 - ylo)],
                    self.wv.at[self.t, x, z, :, :, half(1 - ylo)],
                    self.ps.at[2],
                    self.pr.at[2],
                    self.cross,
                ).start()

        for n in range(len(self.pieces)):
            for cp in self.side(n):
                cp.start()

    def s1(self):
        x, ylo, z, yhi, c = here()
        landed = self.wv.at[self.other, x, z, :, :, half(ylo)]
        cp = push(landed, landed, self.ps.at[2], self.pr.at[2], self.cross)
        cp.wait_recv()
        cp.wait_send()
        self.spread.start(0)

    def s2(self):
        self.spread.finish()
        self.spread.start(1)

    def hand(self, ref):
        n = 3 + len(self.handed)
        cp = push(ref, ref, self.ps.at[n], self.pr.at[n], self.partner)
        cp.start()
        self.handed.append(cp)

    def s3(self):
        self.spread.finish()
        self.spread.start(2)
        for ref in self.spread.held():
            self.hand(ref)

    def s4(self):
        self.spread.finish(self.hand)

    def s5(self):
        for n in range(len(self.pieces)):
            local, cp = self.side(n)
            local.wait()
            cp.wait_send()
            cp.wait_recv()
        for cp in self.handed:
            cp.wait_send()
            cp.wait_recv()


def gather_scratch():
    dma = pltpu.SemaphoreType.DMA
    return [dma((27,)), dma((27,)), dma((13,)), dma((13,)), dma((2,))]


def chips_around():
    x, ylo, z, yhi, c = here()
    return [dev((x + o) % 4, ylo, z, yhi, c) for o in (1, 2, 3)] + [
        dev(x, 1 - ylo, z, yhi, c),
        dev(x, 1 - ylo, z, 1 - yhi, c),
    ]


def dp_group():
    x, ylo, z, yhi, c = here()
    t = 2 * yhi + c
    return [(2 * x + ylo, (z + a) % 4, (t + b) % 4) for a in range(4) for b in range(4) if a or b]


def row_places():
    x, ylo, z, yhi, c = here()
    return [(2 * a + b, dev(x, ylo, a, yhi, b)) for a in range(4) for b in range(2)], 2 * z + c


def row_mates():
    x, ylo, z, yhi, c = here()
    me = 2 * z + c
    return [dev(x, ylo, ((me + o) % 8) // 2, yhi, (me + o) % 2) for o in range(1, 8)]


def deal(j, where, me, src, dst, s, r):
    @pl.when(me != j)
    def _():
        push(src, dst, s(j), r(me), where).start()

    @pl.when(me == j)
    def _():
        dst[...] = src[...]


def dealt(j, where, me, src, dst, s, r):
    @pl.when(me != j)
    def _():
        cp = push(src, dst, s(j), r(j), where)
        cp.wait_send()
        cp.wait_recv()


def place_of(sem):
    return lambda j: sem.at[j]


def attn_rows(wa, t, low, high):
    first, last = low // 192, -(-high // 192)
    whole = wa[t, first:last].reshape(192 * (last - first), D)
    return whole[low - 192 * first : high - 192 * first]


def up_rows(wt):
    return wt[0:2].reshape(D, D)


def down_rows(wt):
    return wt[2:4].reshape(D, D)


class Tokens:
    def __init__(self, hid, x0, hs, hr, ls):
        self.refs = hid, x0, hs, hr, ls

    def start(self):
        hid, x0, hs, hr, ls = self.refs
        x, ylo, z, yhi, c = here()
        t = 2 * yhi + c
        for b in range(4):

            @pl.when((t == z) & (t != b))
            def _(b=b):
                push(hid.at[b // 2, b % 2], x0, hs.at[b], hr.at[0], (2 * x + ylo, z, b)).start()

            @pl.when((t == z) & (t == b))
            def _(b=b):
                pltpu.make_async_copy(hid.at[b // 2, b % 2], x0, ls.at[0]).start()

    def arrive(self):
        hid, x0, hs, hr, ls = self.refs
        x, ylo, z, yhi, c = here()
        t = 2 * yhi + c

        @pl.when(t != z)
        def _():
            push(x0, x0, hs.at[0], hr.at[0], (2 * x + ylo, z, (t + 1) % 4)).wait_recv()

        @pl.when(t == z)
        def _():
            pltpu.make_async_copy(hid.at[0, 0], x0, ls.at[0]).wait()

    def sent(self):
        hid, x0, hs, hr, ls = self.refs
        x, ylo, z, yhi, c = here()
        t = 2 * yhi + c
        for b in range(4):

            @pl.when((t == z) & (t != b))
            def _(b=b):
                push(hid.at[b // 2, b % 2], x0, hs.at[b], hr.at[0], (2 * x + ylo, z, b)).wait_send()


class Cotangents:
    def __init__(self, cot, cots, over, cs, cr, ls):
        self.refs = cot, cots, over, cs, cr, ls

    def load(self, begin):
        cot, cots, over, cs, cr, ls = self.refs
        x, ylo, z, yhi, c = here()

        @pl.when(2 * yhi + c == z)
        def _():
            cp = pltpu.make_async_copy(cot.at[yhi, c], over, ls.at[0])
            if begin:
                cp.start()
            else:
                cp.wait()

    def move(self, step, begin):
        cot, cots, over, cs, cr, ls = self.refs
        x, ylo, z, yhi, c = here()
        t = 2 * yhi + c
        dp = 2 * x + ylo
        b = (step + z) % 4

        @pl.when((t != z) | (t != b))
        def _():
            cp = push(cot.at[b // 2, b % 2], cots.at[z], cs.at[step], cr.at[z], (dp, t, b))
            if begin:
                cp.start()
            else:
                cp.wait_send()

        @pl.when((t == z) & (t == b))
        def _():
            cp = pltpu.make_async_copy(over, cots.at[z], ls.at[1])
            if begin:
                cp.start()
            else:
                cp.wait()

        if not begin:

            @pl.when((t != z) | (z != step))
            def _():
                spot = cots.at[step]
                push(spot, spot, cs.at[step], cr.at[step], (dp, z, (t + 1) % 4)).wait_recv()


class Scatter:
    def __init__(self, dst, s_sem, r_sem):
        self.dst, self.s_sem, self.r_sem = dst, s_sem, r_sem

    def send(self, s, src, begin):
        x, ylo, z, yhi, c = here()
        t = 2 * yhi + c
        mine = (z == s) & (t == z)

        @pl.when(jnp.logical_not(mine))
        def _():
            where = (2 * x + ylo, s, z)
            cp = push(src, self.dst.at[yhi, c], self.s_sem.at[s], self.r_sem.at[t], where)
            if begin:
                cp.start()
            else:
                cp.wait_send()

        @pl.when(mine)
        def _():
            cp = pltpu.make_async_copy(src, self.dst.at[yhi, c], self.s_sem.at[s])
            if begin:
                cp.start()
            else:
                cp.wait()

    def received(self, s):
        x, ylo, z, yhi, c = here()
        t = 2 * yhi + c
        for b in range(4):

            @pl.when((z == s) & ((t != b) | (t != z)))
            def _(b=b):
                spot = self.dst.at[b // 2, b % 2]
                where = (2 * x + ylo, z, (t + 1) % 4)
                push(spot, spot, self.s_sem.at[b], self.r_sem.at[b], where).wait_recv()


STATE = ("y", "qkv", "lse", "att", "ba", "mid", "pre", "bb")


def state_shapes():
    return (
        ((TOK, D), BF),
        ((8, TOK, 384), BF),
        ((4, 8, 384), F32),
        ((TOK, 1024), BF),
        ((TOK, D), F32),
        ((TOK, D), F32),
        ((TOK, 4 * D), F32),
        ((TOK, D), F32),
    )


def forward_kernel(*refs):
    refs = list(refs)

    def take(count):
        got = refs[:count]
        del refs[:count]
        return got

    hid, cot, mods, segc, segr, cosine, sine, attn_loc, up_loc, down_loc = take(10)
    outs = dict(zip(STATE, take(8)))
    x0, cots, *weights_out = take(6)
    held = dict(zip(STATE, take(8)))
    sbuf, obuf, rbuf, wa0, wa1, wm0, wm1 = take(7)
    wsem, ksem, ss, rs, ss2, rs2 = take(6)
    x, ylo, z, yhi, c = here()
    places, me = row_places()
    saved = []

    def save(src, dst):
        cp = pltpu.make_async_copy(src, dst, wsem.at[len(saved)])
        cp.start()
        saved.append(cp)

    beside = ("zyx", "zxy")
    a0 = Gather(wa0, [(attn_loc.at[0], 0)], ("zyx", "xzy", "yxz"), *take(5))
    m0 = Gather(wm0, [(up_loc.at[0], 0), (down_loc.at[0], 2)], beside, *take(5))
    a1 = Gather(wa1, [(attn_loc.at[1], 0)], ("zyx", "zxy", "zyx"), *take(5))
    m1 = Gather(wm1, [(up_loc.at[1], 0), (down_loc.at[1], 2)], beside, *take(5))
    tokens = Tokens(hid, x0, *take(3))
    cotangents = Cotangents(cot, cots, *take(4))
    greet(dp_group() + chips_around())()
    a0.s0()
    tokens.start()
    cotangents.load(True)
    a0.s1()
    m0.s0()
    a0.s2()
    m0.s1()
    a0.s3()
    tokens.arrive()

    cos_here, sin_here = cosine[...], sine[...]
    low = lanes((TOK, 128)) < 64
    seg_keys = segr[...]

    def flat(column):
        wide = jnp.broadcast_to(column, (column.shape[0], 128))
        return jnp.transpose(wide)[0:8, :]

    def keeping(app):
        slot = app % 2
        return [
            pltpu.make_async_copy(held[name].at[slot], outs[name].at[app], ksem.at[slot, n])
            for n, name in enumerate(STATE)
        ]

    for app in range(4):
        slot = app % 2
        wa, wm = ((wa0, wm0), (wa1, wm1))[slot]
        mod = mods.at[slot]
        qkv, lse, att, ba, mid, pre, bb = (held[name].at[slot] for name in STATE[1:])
        if app == 0:
            v = x0[...].astype(F32)
        else:
            v = held["y"][1 - slot].astype(F32)
            if app == 2:
                v = v + x0[...].astype(F32)
        hat, _ = normalize(v)
        normed = (hat * (1.0 + mod[1:2, :]) + mod[0:1, :]).astype(BF)
        if app == 0:
            a0.s4()
            m0.s2()
            a0.s5()
            save(wa0, weights_out[0])
        if app == 1:
            a1.s5()
            save(wa1, weights_out[2])
        for t in range(4):
            got = nt(normed, attn_rows(wa, t, 0, 640))
            t0, t1, t2, t3, t4 = (got[:, 128 * i : 128 * (i + 1)] for i in range(5))
            s0, s1, s2, s3, s4 = (swap(u) for u in (t0, t1, t2, t3, t4))
            for head, (q, k, w) in enumerate(
                (
                    (jnp.where(low, t0, s3), jnp.where(low, s0, t3), jnp.where(low, t1, s4)),
                    (jnp.where(low, s1, s3), jnp.where(low, t2, t3), jnp.where(low, s2, s4)),
                )
            ):
                j = 2 * t + head
                sbuf[j, :, 0:128] = (turn(q, cos_here, sin_here).astype(BF).astype(F32) * 0.125).astype(BF)
                sbuf[j, :, 128:256] = turn(k, cos_here, sin_here).astype(BF)
                sbuf[j, :, 256:384] = w.astype(BF)
                deal(j, places[j][1], me, sbuf.at[j], qkv.at[me], place_of(ss.at[app]), place_of(rs.at[app]))
        if app == 0:
            m0.s3()
            a1.s0()
            m1.s0()
        if app == 1:
            m1.s3()
        for j, where in places:
            dealt(j, where, me, sbuf.at[j], qkv.at[j], place_of(ss.at[app]), place_of(rs.at[app]))
        if app:
            for cp in keeping(app - 1):
                cp.wait()

        keys = qkv[:, :, 128:256].reshape(SEQ, 128)
        values = qkv[:, :, 256:384].reshape(SEQ, 128)

        def softmax(q, seg_q, keys=keys, values=values):
            scores = jnp.where(seg_q == seg_keys, nt(q, keys), -1e30)
            largest = jnp.max(scores, axis=-1, keepdims=True)
            raised = jnp.exp(scores - largest)
            total = jnp.sum(raised, axis=-1, keepdims=True)
            mixed = nn(raised.astype(BF), values) * (1.0 / total)
            return mixed, largest + jnp.log(total)

        for a in range(4):
            if app == 0 and a == 0:
                a1.s1()
            if app == 0 and a == 2:
                a1.s2()
            q = qkv[2 * a : 2 * a + 2, :, 0:128].reshape(256, 128)
            q = jnp.where(lanes((256, 128)) < 64, q, 0).astype(BF)
            mixed, total = softmax(q, segc[256 * a : 256 * (a + 1), :])
            q2 = jnp.where(low, 0, qkv[2 * a + c, :, 0:128]).astype(BF)
            mixed2, total2 = softmax(q2, segc[pl.ds(256 * a + TOK * c, TOK), :])
            lse[a, :, 0:256] = flat(total)
            lse[a, :, 256:384] = flat(total2)
            for b in range(2):
                j = 2 * a + b
                part = mixed[TOK * b : TOK * (b + 1)]
                obuf[j] = jnp.where(low | (c != b), part, mixed2).astype(BF)
                deal(j, places[j][1], me, obuf.at[j], rbuf.at[me], place_of(ss2.at[app]), place_of(rs2.at[app]))
        if app == 0:
            a1.s3()
            m0.s4()
        if app == 1:
            m1.s4()
        for j, where in places:
            dealt(j, where, me, obuf.at[j], rbuf.at[j], place_of(ss2.at[app]), place_of(rs2.at[app]))

        if app == 0:
            cotangents.load(False)
        cotangents.move(app, True)
        branch_a = jnp.zeros((TOK, D), F32)
        for t in range(4):
            first, second = rbuf[2 * t], rbuf[2 * t + 1]
            own = jnp.where(low, first.astype(F32), swap(second.astype(F32))).astype(BF)
            extra = jnp.where(low, 0, rbuf[2 * t + c]).astype(BF)
            att[:, 128 * t : 128 * (t + 1)] = own
            att[:, 512 + 128 * t : 512 + 128 * (t + 1)] = extra
            branch_a = branch_a + nn(own, attn_rows(wa, t, 576, 704)) + nn(extra, attn_rows(wa, t, 640, 768))
        ba[...] = branch_a
        middle = v + mod[2:3, :] * branch_a
        mid[...] = middle
        hat_b, _ = normalize(middle)
        normed_b = (hat_b * (1.0 + mod[4:5, :]) + mod[3:4, :]).astype(BF)
        if app == 0:
            m0.s5()
            save(wm0, weights_out[1])
            m1.s1()
        if app == 1:
            m1.s5()
            save(wm1, weights_out[3])
        total_b = jnp.zeros((TOK, D), F32)
        for t in range(4):
            before = nn(normed_b, up_rows(wm.at[t]))
            pre[:, D * t : D * (t + 1)] = before
            total_b = total_b + nn(jax.nn.gelu(before, approximate=True).astype(BF), down_rows(wm.at[t]))
        bb[...] = total_b
        held["y"][slot] = (middle + mod[5:6, :] * total_b).astype(BF)
        for cp in keeping(app):
            cp.start()
        if app == 0:
            m1.s2()
            a1.s4()
    for b in range(4):
        cotangents.move(b, False)
    tokens.sent()
    for cp in keeping(3) + saved:
        cp.wait()


def forward(*operands):
    dma = pltpu.SemaphoreType.DMA
    outs = [jax.ShapeDtypeStruct((4,) + dims, dtype) for dims, dtype in state_shapes()]
    outs += [jax.ShapeDtypeStruct(dims, BF) for dims in ((TOK, D), (4, TOK, D))]
    outs += [jax.ShapeDtypeStruct((4,) + group, BF) for group in (ATTN, MLP, ATTN, MLP)]
    scratch = [pltpu.VMEM((2,) + dims, dtype) for dims, dtype in state_shapes()]
    scratch += [
        pltpu.VMEM((8, TOK, 384), BF),
        pltpu.VMEM((8, TOK, 128), BF),
        pltpu.VMEM((8, TOK, 128), BF),
    ]
    scratch += [pltpu.VMEM((4,) + group, BF) for group in (ATTN, ATTN, MLP, MLP)]
    scratch += [dma((4,)), dma((2, 8))] + [dma((4, 8))] * 4
    for _ in range(4):
        scratch += gather_scratch()
    scratch += [dma((4,)), dma((1,)), dma((1,))]
    scratch += [pltpu.VMEM((TOK, D), BF), dma((4,)), dma((4,)), dma((2,))]
    return pl.pallas_call(
        forward_kernel,
        out_shape=tuple(outs),
        in_specs=[ANY] * 2 + [VM] * 5 + [ANY] * 3,
        out_specs=tuple([ANY] * 8 + [VM] + [ANY] * 5),
        scratch_shapes=scratch,
        compiler_params=pltpu.CompilerParams(
            collective_id=1, has_side_effects=True, vmem_limit_bytes=62 * 2**20
        ),
        name="forward",
    )(*operands)


def across(dim, o):
    x, ylo, z, yhi, c = here()
    if dim == "x":
        to = (x + o) % 4
        return dev(to, ylo, z, yhi, c), to
    if dim == "z":
        to = (z + o) % 4
        return dev(x, ylo, to, yhi, c), to
    to = (2 * yhi + ylo + o) % 4
    return dev(x, to % 2, z, to // 2, c), to


def own_place(dim):
    x, ylo, z, yhi, c = here()
    return {"x": x, "z": z, "y": 2 * yhi + ylo}[dim]


def reduce_greeted():
    return [across(dim, o)[0] for dim in "xy" for o in (1, 2, 3)]


def left(order, steps):
    return [label for label in "Yxz" if label.lower() not in order[:steps]]


def block(order, steps, rows):
    sizes = {"Y": 2, "x": 4, "z": 4}
    lane_count = HALF if "y" in order[:steps] else D
    return tuple(sizes[label] for label in left(order, steps)) + (rows, lane_count)


def pick(labels, dim, to):
    index = [slice(None)] * len(labels)
    if dim == "y":
        index[labels.index("Y")] = to // 2
        return tuple(index), half(to % 2)
    index[labels.index(dim)] = to
    return tuple(index), slice(None)


def each_unit(dims, body):
    count = 1
    for size in dims:
        count *= size

    def step(i, carry):
        index, rest = [], i
        for size in reversed(dims):
            index.append(rest % size)
            rest = rest // size
        body(tuple(reversed(index)))
        return carry

    lax.fori_loop(0, count, step, 0)


class ReduceFirst:
    def __init__(self, grads, orders, own, arrived, ls, ss, rs):
        self.grads, self.orders, self.own, self.arrived = grads, orders, own, arrived
        self.ls, self.ss, self.rs = ls, ss, rs

    def source(self, p, to):
        index, cols = pick(["Y", "x", "z"], self.orders[p][0], to)
        return self.grads.at[index + (p, slice(None), cols)]

    def copies(self):
        found = []
        if self.ls is not None:
            for p, order in enumerate(self.orders):
                found.append(pltpu.make_async_copy(self.source(p, own_place(order[0])), self.own[p], self.ls.at[p]))
        for o in (2, 1, 3):
            for p, order in enumerate(self.orders):
                where, to = across(order[0], o)
                n = 3 * p + o - 1
                found.append(push(self.source(p, to), self.arrived[p].at[o - 1], self.ss.at[n], self.rs.at[n], where))
        return found

    def begin(self):
        for cp in self.copies():
            cp.start()

    def sum(self):
        for cp in self.copies():
            cp.wait()
        for p in range(len(self.orders)):
            own, arrived = self.own[p], self.arrived[p]
            mine = own if self.ls is not None else self.source(p, own_place(self.orders[p][0]))

            def body(index, own=own, arrived=arrived, mine=mine):
                total = mine[index].astype(F32)
                for n in range(3):
                    total = total + arrived[(n,) + index].astype(F32)
                own[index] = total.astype(BF)

            each_unit(own.shape[:-2], body)

    @staticmethod
    def shapes(orders, rows):
        return [block(order, 1, rows) for order in orders]

    @staticmethod
    def scratch(orders, rows):
        dma = pltpu.SemaphoreType.DMA
        arrived = [pltpu.VMEM((3,) + dims, BF) for dims in ReduceFirst.shapes(orders, rows)]
        return arrived + [dma((3,)), dma((9,)), dma((9,))]


class ReduceRest:
    def __init__(self, orders, own, refs):
        refs = list(refs)
        count = len(orders)
        self.orders, self.own = orders, own
        self.mid, self.tot, self.end = refs[:count], refs[count : 2 * count], refs[2 * count : 3 * count]
        self.ss2, self.rs2, self.ss3, self.rs3 = refs[3 * count :]

    @staticmethod
    def scratch(orders, rows):
        dma = pltpu.SemaphoreType.DMA
        shapes = [pltpu.VMEM((3,) + block(order, 2, rows), BF) for order in orders]
        shapes += [pltpu.VMEM(block(order, 2, rows), BF) for order in orders]
        shapes += [pltpu.VMEM((3,) + block(order, 3, rows), BF) for order in orders]
        return shapes + [dma((9,))] * 4

    @staticmethod
    def count(orders):
        return 3 * len(orders) + 4

    def copies(self, step):
        found = []
        sources, targets = (self.own, self.mid) if step == 1 else (self.tot, self.end)
        send, recv = (self.ss2, self.rs2) if step == 1 else (self.ss3, self.rs3)
        for o in (2, 1, 3):
            for p, order in enumerate(self.orders):
                where, to = across(order[step], o)
                index, cols = pick(left(order, step), order[step], to)
                n = 3 * p + o - 1
                found.append(
                    push(sources[p].at[index + (slice(None), cols)], targets[p].at[o - 1], send.at[n], recv.at[n], where)
                )
        return found

    def begin(self):
        for cp in self.copies(1):
            cp.start()

    def sum_second(self):
        for cp in self.copies(1):
            cp.wait()
        for p, order in enumerate(self.orders):
            own, mid, tot = self.own[p], self.mid[p], self.tot[p]
            labels = left(order, 1)
            index, cols = pick(labels, order[1], own_place(order[1]))
            free = [n for n, value in enumerate(index) if isinstance(value, slice)]
            for i in range(tot.shape[0]):
                spot = list(index)
                spot[free[0]] = i
                total = own[tuple(spot) + (slice(None), cols)].astype(F32)
                for n in range(3):
                    total = total + mid[n, i].astype(F32)
                tot[i] = total.astype(BF)
        for cp in self.copies(2):
            cp.start()

    def sum_third(self, fin):
        for cp in self.copies(2):
            cp.wait()
        for p, order in enumerate(self.orders):
            index, cols = pick(left(order, 2), order[2], own_place(order[2]))
            total = self.tot[p][index + (slice(None), cols)].astype(F32)
            for n in range(3):
                total = total + self.end[p][n].astype(F32)
            fin[p] = total.astype(BF)


MLP_SUM = ("xyz", "yxz")
ATTN_SUM = ("xyz", "yzx", "zxy")
MLP_ROWS, ATTN_ROWS = 48, 16


def gelu_parts(u):
    k = 0.7978845608028654
    square = u * u
    th = jnp.tanh(k * u * (1.0 + 0.044715 * square))
    half_up = 0.5 * (1.0 + th)
    slope = half_up + 0.5 * u * (1.0 - th * th) * (k * (1.0 + 0.134145 * square))
    return u * half_up, slope


def backward_kernel(layer, *refs):
    refs = list(refs)

    def take(count):
        got = refs[:count]
        del refs[:count]
        return got

    mods, segc, segr = take(3)
    more_dy, prior, *last_shares = take(4) if layer == 0 else [None, None]
    cosine_in, sine_in, x0_in, cots_in = take(4)
    outer = dict(zip(STATE, take(8)))
    wa_in, wm_in = take(2)
    before = take(1)[0] if layer == 0 else None
    din, dinb, dmod, grads, *shares = take(6)
    (spread_out,) = take(1)
    if layer == 0:
        fin_attn, fin_mlp = take(2)
    held = dict(zip(STATE, take(8)))
    cosine, sine, x0, cots, lsem = take(5)
    mod = mods.at[layer]
    own_na, own_nb, own_dba, own_dbb, own_act, own_dpre, own_dpj = take(7)
    got_na, got_nb, got_dba, got_dbb, got_at, got_act, got_dpre, got_dpj = take(8)
    sbuf, rbuf, sbig, rbig, dmid, dnb, k_own, k_sh, v_own, v_sh = take(10)
    wa, wm, mlp_grads, stage_attn = take(4)
    wsem, gsem, ss, rs, ss2, rs2, xs, xr = take(8)
    mlp_first = ReduceFirst(mlp_grads, MLP_SUM, shares, take(2), None, *take(3)[1:])
    rows_of = [slice(TOK * e, TOK * (e + 1)) for e in range(2)]
    x, ylo, z, yhi, c = here()
    places, me = row_places()
    partner = dev(x, ylo, z, yhi, 1 - c)
    scattered = Scatter(spread_out, *take(2))
    if layer == 1:
        (ys,) = take(1)
    if layer == 0:
        mlp_rest = ReduceRest(MLP_SUM, last_shares, take(ReduceRest.count(MLP_SUM)))
        attn_first = ReduceFirst(before, ATTN_SUM, take(3), take(3), *take(3))
        attn_rest = ReduceRest(ATTN_SUM, attn_first.own, take(ReduceRest.count(ATTN_SUM)))
    entered = greet(dp_group() + reduce_greeted())
    loads = {}

    def load(name, src, dst):
        cp = pltpu.make_async_copy(src, dst, lsem.at[len(loads)])
        cp.start()
        loads[name] = cp

    def loaded(*names):
        for name in names:
            loads[name].wait()

    def load_state(name):
        for e in range(2):
            load((name, e), outer[name].at[layer + 2 * e], held[name].at[e])

    def state(name):
        loaded((name, 0), (name, 1))

    for e in range(2):
        load(("cots", e), cots_in.at[layer + 2 * e], cots.at[e])
    load_state("mid")
    load_state("bb")
    if layer == 0:
        load("x0", x0_in, x0)
        load(("y", 1), outer["y"].at[1], held["y"].at[1])
    else:
        load("y", outer["y"], ys)
    load_state("att")

    def wm_fetch(t):
        return pltpu.make_async_copy(wm_in.at[t], wm.at[t % 2], wsem.at[1 + t])

    wm_fetch(0).start()
    load_state("pre")
    wm_fetch(1).start()
    wa_fetch = pltpu.make_async_copy(wa_in, wa, wsem.at[0])
    wa_fetch.start()
    for name in ("ba", "qkv", "lse"):
        load_state(name)
    load("cosine", cosine_in, cosine)
    load("sine", sine_in, sine)
    qkvs, lses, atts, bas, mids, pres, bbs = ([held[name].at[e] for e in range(2)] for name in STATE[1:])
    scale_a, gate_a = mod[1:2, :], mod[2:3, :]
    scale_b, gate_b = mod[4:5, :], mod[5:6, :]
    low = lanes((TOK, 128)) < 64
    exchanged = {}

    def hand(name, src, dst):
        n = len(exchanged)
        cp = push(src, dst, xs.at[n], xr.at[n], partner)
        cp.start()
        exchanged[name] = cp

    def have(*names):
        for name in names:
            exchanged[name].wait_send()
            exchanged[name].wait_recv()

    def gradient(e):
        dy = cots[e].astype(F32)
        return dy if more_dy is None else dy + more_dy[e]

    def entry(e):
        if layer == 1:
            return ys[2 * e].astype(F32)
        v = x0[...].astype(F32)
        return v + held["y"][1].astype(F32) if e else v

    loaded(("cots", 0), ("cots", 1))
    state("mid")
    state("bb")
    loaded(*(["x0", ("y", 1)] if layer == 0 else ["y"]))
    dgate_b = jnp.zeros((1, D), F32)
    for e in range(2):
        dy = gradient(e)
        dgate_b = dgate_b + jnp.sum(dy * bbs[e][...], axis=0, keepdims=True)
        own_dbb[rows_of[e], :] = (gate_b * dy).astype(BF)
        hat_b, _ = normalize(mids[e][...])
        own_nb[rows_of[e], :] = (hat_b * (1.0 + scale_b) + mod[3:4, :]).astype(BF)
        hat_a, _ = normalize(entry(e))
        own_na[rows_of[e], :] = (hat_a * (1.0 + scale_a) + mod[0:1, :]).astype(BF)
    entered()
    hand("dbb", own_dbb, got_dbb)
    hand("nb", own_nb, got_nb)
    hand("na", own_na, got_na)
    state("att")
    for e in range(2):
        hand(f"at{e}", atts[e], got_at.at[e])
    given = {s: ys.at[s] for s in range(4)} if layer == 1 else {1: prior.at[0], 3: prior.at[1]}
    for s, ref in given.items():
        scattered.send(s, ref, True)
    if layer == 0:
        mlp_rest.begin()
        attn_first.begin()
    state("pre")

    for t in range(4):
        wm_fetch(t).wait()
        d_act = nt(own_dbb[...], down_rows(wm.at[t % 2]))
        for e in range(2):
            act, slope = gelu_parts(pres[e][:, D * t : D * (t + 1)])
            own_act[t, rows_of[e], :] = act.astype(BF)
            own_dpre[t, rows_of[e], :] = (d_act[rows_of[e]] * slope).astype(BF)
        more = nt(own_dpre[t], up_rows(wm.at[t % 2]))
        dnb[...] = more if t == 0 else dnb[...] + more
        if t < 2:
            wm_fetch(t + 2).start()
    for h in range(2):
        hand(f"act{h}", own_act.at[2 * h + 1 - c], got_act.at[h])
        hand(f"dpre{h}", own_dpre.at[2 * h + 1 - c], got_dpre.at[h])

    state("ba")
    dgate_a = jnp.zeros((1, D), F32)
    dscale_b = jnp.zeros((1, D), F32)
    dshift_b = jnp.zeros((1, D), F32)
    for e in range(2):
        hat_b, inv_b = normalize(mids[e][...])
        g = dnb[rows_of[e], :]
        dscale_b = dscale_b + jnp.sum(g * hat_b, axis=0, keepdims=True)
        dshift_b = dshift_b + jnp.sum(g, axis=0, keepdims=True)
        d_middle = gradient(e) + norm_back(g * (1.0 + scale_b), hat_b, inv_b)
        dmid[rows_of[e], :] = d_middle
        dgate_a = dgate_a + jnp.sum(d_middle * bas[e][...], axis=0, keepdims=True)
        own_dba[rows_of[e], :] = (gate_a * d_middle).astype(BF)
    hand("dba", own_dba, got_dba)
    wa_fetch.wait()
    for t in range(4):
        first = nt(own_dba[...], attn_rows(wa, t, 576, 704))
        second = nt(own_dba[...], attn_rows(wa, t, 640, 768))
        for e in range(2):
            sbuf[2 * t, e] = jnp.where(low, first[rows_of[e]], second[rows_of[e]]).astype(BF)
            sbuf[2 * t + 1, e] = second[rows_of[e]].astype(BF)
        for b in range(2):
            j = 2 * t + b
            deal(j, places[j][1], me, sbuf.at[j], rbuf.at[me], place_of(ss), place_of(rs))

    if layer == 0:
        mlp_rest.sum_second()
        attn_first.sum()
        attn_rest.begin()
    have("dbb", "nb", "act0", "dpre0", "act1", "dpre1")

    for h in range(2):
        t = 2 * h + c
        total = tn(own_nb[...], own_dpre[t]) + tn(got_nb[...], got_dpre[h])
        mlp_grads[h, 0:2] = total.astype(BF).reshape(2, 4, 2, 48, D)
        total = tn(own_act[t], own_dbb[...]) + tn(got_act[h], got_dbb[...])
        mlp_grads[h, 2:4] = total.astype(BF).reshape(2, 4, 2, 48, D)
    mlp_first.begin()
    for j, where in places:
        dealt(j, where, me, sbuf.at[j], rbuf.at[j], place_of(ss), place_of(rs))

    state("qkv")
    state("lse")
    loaded("cosine", "sine")
    seg_keys = segc[...]
    wide = lanes((256, 128)) < 64
    for e in range(2):
        qkv, lse = qkvs[e], lses[e]
        for ref in (k_own, k_sh, v_own, v_sh):
            ref[...] = jnp.zeros_like(ref)

        def one(q, go, seg_q, total, k_sum, v_sum, qkv=qkv):
            keys = qkv[:, :, 128:256].reshape(SEQ, 128)
            values = qkv[:, :, 256:384].reshape(SEQ, 128)
            scores = jnp.where(seg_keys == seg_q, nt(keys, q), -1e30)
            p = jnp.exp(scores - total)
            d_p = nt(values, go)
            centre = jnp.sum(d_p * p, axis=0, keepdims=True)
            d_s = (p * (d_p - centre)).astype(BF)
            v_sum[...] += nn(p.astype(BF), go)
            k_sum[...] += nn(d_s, q)
            return tn(d_s, keys) * 0.125

        for a in range(4):
            q = qkv[2 * a : 2 * a + 2, :, 0:128].reshape(256, 128)
            go = rbuf[2 * a : 2 * a + 2, e].reshape(256, 128)
            dq = one(
                jnp.where(wide, q, 0).astype(BF),
                jnp.where(wide, go, 0).astype(BF),
                segr[0:1, 256 * a : 256 * (a + 1)],
                lse[a, 0:1, 0:256],
                k_own,
                v_own,
            )
            q2 = jnp.where(low, 0, qkv[2 * a + c, :, 0:128]).astype(BF)
            go2 = jnp.where(low, 0, rbuf[2 * a + c, e]).astype(BF)
            seg2 = jnp.where(
                c == 0,
                segr[0:1, 256 * a : 256 * a + 128],
                segr[0:1, 256 * a + 128 : 256 * a + 256],
            )
            dq2 = one(q2, go2, seg2, lse[a, 0:1, 256:384], k_sh, v_sh)
            for b in range(2):
                rows = slice(256 * a + TOK * b, 256 * a + TOK * (b + 1))
                whole = jnp.where(low, dq[TOK * b : TOK * (b + 1)], jnp.where(c == b, dq2, 0.0))
                sbig[2 * a + b, e, :, 0:128] = turn(whole, cosine[rows, :], -sine[rows, :]).astype(BF)
        for j, where in places:
            rows = slice(TOK * j, TOK * (j + 1))
            whole = jnp.where(low, k_own[rows, :], k_sh[rows, :])
            sbig[j, e, :, 128:256] = turn(whole, cosine[rows, :], -sine[rows, :]).astype(BF)
            sbig[j, e, :, 256:384] = jnp.where(low, v_own[rows, :], v_sh[rows, :]).astype(BF)
            deal(
                j, where, me, sbig.at[j, e], rbig.at[me, e],
                lambda i, e=e: ss2.at[e, i], lambda i, e=e: rs2.at[e, i],
            )
        if layer == 0 and e == 0:
            mlp_rest.sum_third(fin_mlp)
            attn_rest.sum_second()
    for e in range(2):
        for j, where in places:
            dealt(
                j, where, me, sbig.at[j, e], rbig.at[j, e],
                lambda i, e=e: ss2.at[e, i], lambda i, e=e: rs2.at[e, i],
            )
        for t in range(4):
            q0, k0, v0 = (rbig[2 * t, e, :, 128 * i : 128 * (i + 1)].astype(F32) for i in range(3))
            q1, k1, v1 = (rbig[2 * t + 1, e, :, 128 * i : 128 * (i + 1)].astype(F32) for i in range(3))
            tiles = (
                jnp.where(low, q0, swap(k0)),
                jnp.where(low, v0, swap(q1)),
                jnp.where(low, k1, swap(v1)),
                jnp.where(low, swap(q0 + q1), k0 + k1),
                jnp.where(low, swap(v0 + v1), 0.0),
            )
            for i, tile in enumerate(tiles):
                own_dpj[t, rows_of[e], 128 * i : 128 * (i + 1)] = tile.astype(BF)
    for h in range(2):
        hand(f"dpj{h}", own_dpj.at[2 * h + 1 - c], got_dpj.at[h])
    dna = jnp.zeros((2 * TOK, D), F32)
    for t in range(4):
        dna = dna + nn(own_dpj[t], attn_rows(wa, t, 0, 640))
    dscale_a = jnp.zeros((1, D), F32)
    dshift_a = jnp.zeros((1, D), F32)
    for e in range(2):
        hat_a, inv_a = normalize(entry(e))
        g = dna[rows_of[e]]
        dscale_a = dscale_a + jnp.sum(g * hat_a, axis=0, keepdims=True)
        dshift_a = dshift_a + jnp.sum(g, axis=0, keepdims=True)
        total = dmid[rows_of[e], :] + norm_back(g * (1.0 + scale_a), hat_a, inv_a)
        din[e] = total
        dinb[e] = total.astype(BF)
    for i, part in enumerate((dshift_a, dscale_a, dgate_a, dshift_b, dscale_b, dgate_b)):
        dmod[i : i + 1, :] = part
    dmod[6:8, :] = jnp.zeros((2, D), F32)

    have("na", "at0", "at1", "dba", "dpj0", "dpj1")
    for h in range(2):
        t = 2 * h + c
        copy = pltpu.make_async_copy(stage_attn, grads.at[h], gsem.at[0])
        if h:
            copy.wait()
        total = tn(own_dpj[t], own_na[...]) + tn(got_dpj[h], got_na[...])
        stage_attn[0:3] = total[0:576].astype(BF).reshape(3, 4, 3, 16, D)
        parts = []
        for first in (0, 512):
            cols = pl.ds(pl.multiple_of(first + 128 * t, 128), 128)
            total = jnp.zeros((128, D), F32)
            for e in range(2):
                total = total + tn(atts[e][:, cols], own_dba[rows_of[e], :])
                total = total + tn(got_at[e, :, cols], got_dba[rows_of[e], :])
            parts.append(total)
        total = jnp.concatenate([parts[0], parts[1][64:128]], axis=0)
        stage_attn[3] = total.astype(BF).reshape(4, 3, 16, D)
        copy.start()
    if layer == 0:
        attn_rest.sum_third(fin_attn)
    mlp_first.sum()
    for s, ref in given.items():
        scattered.send(s, ref, False)
        scattered.received(s)
    pltpu.make_async_copy(stage_attn, grads.at[1], gsem.at[0]).wait()


def backward(layer, *operands):
    dma = pltpu.SemaphoreType.DMA
    both = 2 * TOK

    def buf(*dims, dtype=BF):
        return pltpu.VMEM(dims, dtype)

    outs = [
        jax.ShapeDtypeStruct((2, TOK, D), F32),
        jax.ShapeDtypeStruct((2, TOK, D), BF),
        jax.ShapeDtypeStruct((8, D), F32),
        jax.ShapeDtypeStruct((2,) + ATTN, BF),
    ]
    outs += [jax.ShapeDtypeStruct(dims, BF) for dims in ReduceFirst.shapes(MLP_SUM, MLP_ROWS)]
    outs.append(jax.ShapeDtypeStruct((2, 2, TOK, D), BF))
    out_specs = [VM, VM, VM, ANY, VM, VM, ANY]
    if layer == 0:
        outs += [jax.ShapeDtypeStruct(dims, BF) for dims in ((3, 16, HALF), (2, 48, HALF))]
        out_specs += [VM, VM]
    scratch = [buf(2, *dims, dtype=dtype) for dims, dtype in state_shapes()]
    scratch += [buf(SEQ, 128, dtype=F32)] * 2 + [buf(TOK, D), buf(2, TOK, D), dma((24,))]
    scratch += [buf(both, D)] * 4 + [buf(4, both, D)] * 2 + [buf(4, both, 640)]
    scratch += [buf(both, D)] * 4 + [buf(2, TOK, 1024)] + [buf(2, both, D)] * 2 + [buf(2, both, 640)]
    scratch += [buf(8, 2, TOK, 128)] * 2 + [buf(8, 2, TOK, 384)] * 2
    scratch += [buf(both, D, dtype=F32)] * 2 + [buf(SEQ, 128, dtype=F32)] * 4
    scratch += [buf(4, *ATTN), buf(2, *MLP), buf(2, *MLP), buf(*ATTN)]
    scratch += [dma((5,)), dma((1,)), dma((8,)), dma((8,)), dma((2, 8)), dma((2, 8)), dma((12,)), dma((12,))]
    scratch += ReduceFirst.scratch(MLP_SUM, MLP_ROWS)
    scratch += [dma((4,)), dma((4,))]
    if layer == 1:
        scratch.append(buf(4, TOK, D))
    if layer == 0:
        scratch += ReduceRest.scratch(MLP_SUM, MLP_ROWS)
        scratch += [pltpu.VMEM(dims, BF) for dims in ReduceFirst.shapes(ATTN_SUM, ATTN_ROWS)]
        scratch += ReduceFirst.scratch(ATTN_SUM, ATTN_ROWS)
        scratch += ReduceRest.scratch(ATTN_SUM, ATTN_ROWS)
    vmem_in = 7 if layer == 0 else 3
    return pl.pallas_call(
        functools.partial(backward_kernel, layer),
        out_shape=tuple(outs),
        in_specs=[VM] * vmem_in + [ANY] * (len(operands) - vmem_in),
        out_specs=tuple(out_specs),
        scratch_shapes=scratch,
        compiler_params=pltpu.CompilerParams(
            collective_id=2 + layer, has_side_effects=True, vmem_limit_bytes=62 * 2**20
        ),
        name=f"backward_{layer}",
    )(*operands)


def finish_kernel(*refs):
    refs = list(refs)

    def take(count):
        got = refs[:count]
        del refs[:count]
        return got

    shares = take(2)
    fin_a1, fin_m1, dm0, dm1, feat, db0 = take(6)
    (attn_grads,) = take(1)
    out_a0, out_m0, out_a1, out_m1, g_out, rows_out = take(6)
    fin_a0, fin_m0, dm_in, dsum = take(4)
    mlp_rest = ReduceRest(MLP_SUM, shares, take(ReduceRest.count(MLP_SUM)))
    attn_first = ReduceFirst(attn_grads, ATTN_SUM, take(3), take(3), *take(3))
    attn_rest = ReduceRest(ATTN_SUM, attn_first.own, take(ReduceRest.count(ATTN_SUM)))
    ag_a0 = Spread(out_a0, ("xzy", "xyz", "xzy"), *take(2))
    ag_m0 = Spread(out_m0, ("zyx", "xzy"), *take(2))
    ag_a1 = Spread(out_a1, ("xyz", "xzy", "xyz"), *take(2))
    ag_m1 = Spread(out_m1, ("zyx", "yxz"), *take(2))
    scattered = Scatter(g_out, *take(2))
    ms, mr, ms2, mr2, fsem = take(5)
    x, ylo, z, yhi, c = here()
    dp = 2 * x + ylo
    places, me = row_places()
    row = 2 * dp + yhi
    others = []
    for o in range(1, 16):
        r = (row + o) % 16
        others.append(dev(r // 4, (r // 2) % 2, z, r % 2, c))
    far = []
    for o in range(1, 8):
        g = (dp + o) % 8
        far += [(g, z, 2 * b + c) for b in range(2)]
    greet(dp_group() + far)()

    def place_in(n, fin, out):
        return pltpu.make_async_copy(fin, out.at[x, z, :, :, half(ylo)], fsem.at[n])

    settled = [place_in(0, fin_m1, out_m1), place_in(1, fin_a1, out_a1)]
    for cp in settled:
        cp.start()
    mlp_rest.begin()
    attn_first.begin()
    for cp in settled:
        cp.wait()
    ag_m1.start(0)
    ag_a1.start(0)
    for j, where in places:

        @pl.when(me != j)
        def _(j=j, where=where):
            push(dm0, dm_in.at[me, 0], ms.at[0, j], mr.at[0, me], where).start()
            push(dm1, dm_in.at[me, 1], ms.at[1, j], mr.at[1, me], where).start()

    for e in range(2):
        scattered.send(2 * e, db0.at[e], True)
    mlp_rest.sum_second()
    ag_m1.finish()
    ag_m1.start(1)
    ag_a1.finish()
    ag_a1.start(1)

    for j, where in places:

        @pl.when(me != j)
        def _(j=j, where=where):
            for l, ref in enumerate((dm0, dm1)):
                cp = push(ref, dm_in.at[j, l], ms.at[l, j], mr.at[l, j], where)
                cp.wait_send()
                cp.wait_recv()

        @pl.when(me == j)
        def _(j=j):
            dm_in[j, 0] = dm0[...]
            dm_in[j, 1] = dm1[...]

    total = dm_in[0]
    for j in range(1, 8):
        total = total + dm_in[j]
    lane = lax.broadcasted_iota(jnp.int32, (2, 8, D), 1)
    wide = jnp.concatenate([feat[...]] * 6, axis=1)
    high = wide.astype(BF).astype(F32)
    total = jnp.where(lane == 6, high, jnp.where(lane == 7, wide - high, total))
    dsum[...] = total.astype(BF)
    mlp_rest.sum_third(fin_m0)
    done = place_in(0, fin_m0, out_m0)
    done.start()
    attn_first.sum()
    attn_rest.begin()
    done.wait()
    ag_m0.start(0)
    ag_m1.finish()
    ag_m1.start(2)
    ag_a1.finish()
    ag_a1.start(2)
    attn_rest.sum_second()
    ag_m0.finish()
    ag_m0.start(1)
    moved = [push(dsum, rows_out.at[row], ms2.at[o], mr2.at[o], where) for o, where in enumerate(others)]
    for cp in moved:
        cp.start()
    keep = pltpu.make_async_copy(dsum, rows_out.at[row], fsem.at[2])
    keep.start()
    attn_rest.sum_third(fin_a0)
    done = place_in(1, fin_a0, out_a0)
    done.start()
    done.wait()
    ag_a0.start(0)
    ag_m0.finish()
    ag_m0.start(2)
    ag_a0.finish()
    ag_a0.start(1)
    ag_a0.finish()
    ag_a0.start(2)
    for ag in (ag_m1, ag_a1, ag_m0, ag_a0):
        ag.finish()
    keep.wait()
    for cp in moved:
        cp.wait()
    for s in (0, 2):
        scattered.send(s, db0.at[s // 2], False)
        scattered.received(s)


def finish(*operands):
    dma = pltpu.SemaphoreType.DMA
    shapes = [ATTN, MLP, ATTN, MLP, (2, 2, TOK, D)]
    scratch = [
        pltpu.VMEM((3, 16, HALF), BF),
        pltpu.VMEM((2, 48, HALF), BF),
        pltpu.VMEM((8, 2, 8, D), F32),
        pltpu.VMEM((2, 8, D), BF),
    ]
    scratch += ReduceRest.scratch(MLP_SUM, MLP_ROWS)
    scratch += [pltpu.VMEM(dims, BF) for dims in ReduceFirst.shapes(ATTN_SUM, ATTN_ROWS)]
    scratch += ReduceFirst.scratch(ATTN_SUM, ATTN_ROWS)
    scratch += ReduceRest.scratch(ATTN_SUM, ATTN_ROWS)
    scratch += [dma((27,))] * 8 + [dma((4,)), dma((4,))]
    scratch += [dma((2, 8)), dma((2, 8)), dma((15,)), dma((15,)), dma((3,))]
    return pl.pallas_call(
        finish_kernel,
        out_shape=tuple(
            [jax.ShapeDtypeStruct(dims, BF) for dims in shapes] + [jax.ShapeDtypeStruct((16, 2, 8, D), BF)]
        ),
        in_specs=[VM] * 8 + [ANY],
        out_specs=(ANY,) * 6,
        scratch_shapes=scratch,
        compiler_params=pltpu.CompilerParams(
            collective_id=4, has_side_effects=True, vmem_limit_bytes=62 * 2**20
        ),
        name="finish",
    )(*operands)


def modulation_kernel(rows, grad_mod, grad_bias):
    features = rows[:, 0, 6, 0:128].astype(F32) + rows[:, 0, 7, 0:128].astype(F32)
    for l in range(2):
        for i in range(6):
            cols = slice(D * i, D * (i + 1))
            d = rows[:, l, i, :].astype(F32)
            grad_mod[l, :, cols] = lax.dot_general(
                features, d, (((0,), (0,)), ((), ())), precision=highest, preferred_element_type=F32
            )
            grad_bias[l : l + 1, cols] = jnp.sum(d, axis=0, keepdims=True)


def modulation_grads(rows):
    return pl.pallas_call(
        modulation_kernel,
        out_shape=(
            jax.ShapeDtypeStruct((2, 128, 6 * D), F32),
            jax.ShapeDtypeStruct((2, 6 * D), F32),
        ),
        in_specs=[VM],
        out_specs=(VM, VM),
        compiler_params=pltpu.CompilerParams(vmem_limit_bytes=30 * 2**20),
        name="modulation_grads",
    )(rows)


def rotary(count):
    frequency = np.exp(-np.log(10000.0) * np.arange(32) / 32)
    angles = np.arange(count)[:, None] * frequency[None, :]
    cos, sin = np.cos(angles), np.sin(angles)
    return (
        np.concatenate([cos] * 4, axis=1).astype(np.float32),
        np.concatenate([-sin, sin, -sin, sin], axis=1).astype(np.float32),
    )


def time_features(step_values, feature_count):
    half_count = feature_count // 2
    frequency = jnp.exp(-np.log(10000.0) * jnp.arange(half_count, dtype=F32) / half_count)
    angles = step_values.astype(F32)[:, None] * frequency[None, :]
    return jnp.concatenate([jnp.cos(angles), jnp.sin(angles)], axis=1)


def on_device(hidden_in, segments, timestep, w_qkv, w_out, w_up, w_down, w_mod, b_mod, cotangent):
    x, ylo, z, yhi, c = here()
    attn_loc = jnp.concatenate([jnp.swapaxes(w_qkv, 1, 2), w_out], axis=1).reshape((2,) + ATTN)
    up_loc = w_up.reshape(2, 2, 4, 2, 48, D)
    down_loc = w_down.reshape(2, 2, 4, 2, 48, D)

    mine = lax.dynamic_slice_in_dim(timestep, yhi, 1, 0)
    features = time_features(mine, w_mod.shape[1])
    modulation = jnp.einsum(
        "rf,lfm->lrm", features, w_mod.astype(F32), precision=highest
    ) + b_mod.astype(F32)[:, None, :]
    modulation = modulation.reshape(2, 6, D)
    seg = lax.dynamic_slice_in_dim(segments, yhi, 1, 0)
    segc, segr = seg.reshape(SEQ, 1), seg
    cosine, sine = (jnp.asarray(v) for v in rotary(SEQ))
    place = (2 * z + c) * TOK
    cos_here = lax.dynamic_slice_in_dim(cosine, place, TOK, 0)
    sin_here = lax.dynamic_slice_in_dim(sine, place, TOK, 0)

    *state, x0, cots, wa0, wm0, wa1, wm1 = forward(
        hidden_in.reshape(2, 2, TOK, D),
        cotangent.reshape(2, 2, TOK, D),
        modulation,
        segc,
        segr,
        cos_here,
        sin_here,
        attn_loc,
        up_loc,
        down_loc,
    )
    known = (cosine, sine, x0, cots, *state)
    din1, dinb1, dm1, ga1, *shares1, y_out = backward(1, modulation, segc, segr, *known, wa1, wm1)
    _, dinb0, dm0, ga0, *shares0, g_out1, fin_a1, fin_m1 = backward(
        0, modulation, segc, segr, din1, dinb1, *shares1, *known, wa0, wm0, ga1
    )
    out_a0, out_m0, out_a1, out_m1, g_out0, rows = finish(
        *shares0, fin_a1, fin_m1, dm0, dm1, features, dinb0, ga0
    )
    g_out = jnp.where(z % 2 == 1, g_out1, g_out0)
    grad_mod, grad_bias = modulation_grads(rows)

    attn = jnp.stack([out_a0, out_a1]).reshape(2, D, D)
    mlp = jnp.stack([out_m0, out_m1]).reshape(2, 2 * D, D)
    return (
        y_out.reshape(1, 2, 2 * TOK, D),
        g_out.reshape(1, 2, 2 * TOK, D).astype(F32),
        attn[:, 0:576].swapaxes(1, 2).astype(F32),
        attn[:, 576:768].astype(F32),
        mlp[:, 0:768].astype(F32),
        mlp[:, 768:1536].astype(F32),
        grad_mod,
        grad_bias,
    )


def solution(mesh):
    placed = (
        P("dp", "tensor", None),
        P("dp", None),
        P("dp"),
        P(None, None, "tensor"),
        P(None, "tensor", None),
        P(None, None, "tensor"),
        P(None, "tensor", None),
        P(),
        P(),
        P("section", "dp", "tensor", None),
    )
    return jax.shard_map(
        on_device,
        mesh=mesh,
        in_specs=placed,
        out_specs=(
            P("section", "dp", "tensor", None),
            P("section", "dp", "tensor", None),
            P(None, None, "tensor"),
            P(None, "tensor", None),
            P(None, None, "tensor"),
            P(None, "tensor", None),
            P(),
            P(),
        ),
        check_vma=False,
    )
```

time: 503 us -> 443 us (0.88)
  the two profiles are of different devices: /device:TPU:0 before, /device:TPU:16 now
where the time goes in v3:
time: 443 us; the launch traced here: 435 us
  Pallas kernels  412 us (93%)
  other arithmetic  11.6 us (3%)
  local copies, waits for them, and re-layouts  6.15 us (1%)
    pallas_call x1, Pallas kernels, forward(): pl.pallas_call(forward_kernel, out_shape=tuple(outs), in_specs=[ANY] * 2...  149 us
    pallas_call x2, Pallas kernels, backward(): pl.pallas_call(functools.partial(backward_kernel, layer), out_shape=tuple...  141 us
    pallas_call x1, Pallas kernels, finish(): pl.pallas_call(finish_kernel, out_shape=tuple([jax.ShapeDtypeStruct(dims,...  115 us

profile of v3, /device:TPU:16, one launch (start us, length us, event | category | flops | bytes accessed | tf_op | source)
XLA Modules:
  0.0 434.6 jit_solution(2115428953023256783)
XLA Ops:
  0.6 0.0 copy-start
  0.7 1.4 dynamic_slice.12
  2.8 0.1 fusion.7
  2.8 0.1 pad_maximum_fusion.3.refs_6_
  2.9 0.6 constant_dynamic-slice_fusion.2.refs_4_.refs_2_
  3.5 2.7 fusion.5
  6.2 0.7 reshape.99.refs_2_.refs_0_
  6.9 1.5 constant_dynamic-slice_fusion
  8.4 1.0 copy.21.refs_3_.refs_1_
  9.5 1.6 pad_maximum_fusion.1
  11.0 0.0 copy-done.12
  11.0 149.4 %forward.1 = (bf16[4,128,768]{2,1,0:T(8,128)(2,1)}, bf16[4,8,128,384]{3,2,1,0:T(8,128)(2,1)}, f32[4,4,8,384]{3,2,1,0:T(8,128)}, bf16[4,128,1024]{2,1,0:T(8,128)(...) custom-call(bf16[2,2,128,768]{3,2,1,0:T(8,128)(2,1)} %bitcast.37, ...), custom_call_target="tpu_custom_call" | custom-call | tf_op jit(solution)/shard_map/forward/pallas_call | solution.py:631
  160.4 65.7 %backward_1.1 = (f32[2,128,768]{2,1,0:T(8,128)}, bf16[2,128,768]{2,1,0:T(8,128)(2,1)}, f32[8,768]{1,0:T(8,128)}, bf16[2,4,4,3,16,768]{5,4,3,2,1,0:T(8,128)(2,1)}...) custom-call(f32[2,6,768]{2,1,0:T(8,128)} %reshape.99.refs_2_.refs_0_, ...), custom_call_target="tpu_custom_call" | custom-call | tf_op jit(solution)/shard_map/backward_1/pallas_call | solution.py:1182
  226.1 75.5 %backward_0.1 = (f32[2,128,768]{2,1,0:T(8,128)}, bf16[2,128,768]{2,1,0:T(8,128)(2,1)}, f32[8,768]{1,0:T(8,128)}, bf16[2,4,4,3,16,768]{5,4,3,2,1,0:T(8,128)(2,1)}...) custom-call(f32[2,6,768]{2,1,0:T(8,128)} %reshape.99.refs_2_.refs_0_, ...), custom_call_target="tpu_custom_call" | custom-call | tf_op jit(solution)/shard_map/backward_0/pallas_call | solution.py:1182
  301.7 115.5 %finish.1 = (bf16[4,4,3,16,768]{4,3,2,1,0:T(8,128)(2,1)}, bf16[4,4,2,48,768]{4,3,2,1,0:T(8,128)(2,1)}, bf16[4,4,3,16,768]{4,3,2,1,0:T(8,128)(2,1)}, bf16[4,4,2,4...) custom-call(bf16[2,4,48,768]{3,2,1,0:T(8,128)(2,1)} %get-tuple-element.66.refs_0_, ...), custom_call_target="tpu_custom_call" | custom-call | tf_op jit(solution)/shard_map/finish/pallas_call | solution.py:1335
  417.1 0.0 copy-done.8
  417.2 1.4 broadcast_select_fusion
  418.6 1.3 convert.2
  419.9 1.1 fusion.4
  421.0 2.0 convert_bitcast_fusion
  423.0 6.1 %modulation_grads.1 = (f32[2,128,4608]{2,1,0:T(8,128)}, f32[2,4608]{1,0:T(2,128)}) custom-call(bf16[16,2,8,768]{3,2,1,0:T(8,128)(2,1)S(1)} %copy-done.2), custom_call_target="tpu_custom_call" | custom-call | tf_op jit(solution)/shard_map/modulation_grads/pallas_call | solution.py:1363
  429.1 0.0 copy-start.1
  429.1 4.1 fusion.2
  433.2 0.9 copy.26
  (24 shorter events, 0.1 us)
Async XLA Ops:
  0.6 2.3 copy-start
  0.7 5.6 %copy-start.11 = (bf16[2,4608]{1,0:T(2,128)(2,1)S(1)}, bf16[2,4608]{1,0:T(2,128)(2,1)}, u32[]{:S(2)}) copy-start(bf16[2,4608]{1,0:T(2,128)(2,1)} %param.20) | copy-start | bytes 55300
  0.7 8.8 %copy-start.10 = (bf16[2,192,768]{2,1,0:T(8,128)(2,1)S(1)}, bf16[2,192,768]{2,1,0:T(8,128)(2,1)}, u32[]{:S(2)}) copy-start(bf16[2,192,768]{2,1,0:T(8,128)(2,1)} %param.16) | copy-start | bytes 1769476
  0.7 8.8 %copy-start.7 = (bf16[2,768,576]{1,2,0:T(8,128)(2,1)S(1)}, bf16[2,768,576]{1,2,0:T(8,128)(2,1)}, u32[]{:S(2)}) copy-start(bf16[2,768,576]{1,2,0:T(8,128)(2,1)} %param.15) | copy-start | bytes 5308420
  2.9 8.1 %copy-start.12 = (f32[1,128]{1,0:T(1,128)}, f32[1,128]{1,0:T(1,128)S(1)}, u32[]{:S(2)}) copy-start(f32[1,128]{1,0:T(1,128)S(1)} %pad_maximum_fusion.3.refs_6_) | copy-start | bytes 1540
  301.6 115.5 %copy-start.8 = (bf16[2,2,128,768]{3,2,1,0:T(8,128)(2,1)S(1)}, bf16[2,2,128,768]{3,2,1,0:T(8,128)(2,1)}, u32[]{:S(2)}) copy-start(bf16[2,2,128,768]{3,2,1,0:T(8,128)(2,1)} %get-tuple-element.65) | copy-start | bytes 2359300
  417.2 2.7 copy-start.3
  417.2 2.7 copy-start.4
  420.9 2.0 copy-start.2
  420.9 8.1 %copy-start.5 = (bf16[4,4,2,48,768]{4,3,2,1,0:T(8,128)(2,1)S(1)}, bf16[4,4,2,48,768]{4,3,2,1,0:T(8,128)(2,1)}, u32[]{:S(2)}) copy-start(bf16[4,4,2,48,768]{4,3,2,1,0:T(8,128)(2,1)} %get-tuple-element.77) | copy-start | bytes 7077892
  421.0 8.1 %copy-start.6 = (bf16[4,4,2,48,768]{4,3,2,1,0:T(8,128)(2,1)S(1)}, bf16[4,4,2,48,768]{4,3,2,1,0:T(8,128)(2,1)}, u32[]{:S(2)}) copy-start(bf16[4,4,2,48,768]{4,3,2,1,0:T(8,128)(2,1)} %get-tuple-element.78) | copy-start | bytes 7077892
  429.1 4.1 copy-start.9
  429.1 5.0 %copy-start.1 = (s32[2,1024]{1,0:T(2,128)S(1)}, s32[2,1024]{1,0:T(2,128)}, u32[]{:S(2)}) copy-start(s32[2,1024]{1,0:T(2,128)} %param.13) | copy-start | bytes 24580
